TPU v7x, 256 devices: a whole 4x4x8 slice. The times are simulated.
256 devices in a mesh: rows: 64 (over z, x, core), tm: 4 (over y).
Axes of the slice: x: 4, y: 4, z: 8, core: 2. Of those that a mesh axis runs over, the one named last changes fastest.
Arguments:
- features: bfloat16 [8, 128, 160, 384], P('tm', 'rows'), may hold values from -16 to 16
- cotangent: bfloat16 [8, 128, 160, 384], P('tm', 'rows'), may hold values from -6 to 6
- gamma: float32 [384], replicated, may hold values from 0.5 to 2
- kernel: bfloat16 [384, 27, 384], replicated, may hold values from -0.0625 to 0.0625
Outputs:
- input_grad: bfloat16 [8, 128, 160, 384], P('tm', 'rows')
- weight_grad: float32 [384, 27, 384], P('tm', None, 'rows')
All inputs are finite; a program needn't handle non-finite values.
Results may differ from a plain program's by a relative error of at most 0.0029.
Values may be sent and summed in bfloat16 or wider, within the bound.
No kernel may reach another device: no remote copies, remote signals or barrier semaphores. Data moves between devices by JAX's collectives and lax.ppermute only.
A program may use at most 192 MiB of HBM per device.

v0:
```python
import math

import jax
import jax.numpy as jnp
from jax import lax
from jax.sharding import PartitionSpec as P


def from_behind(value, axis, steps):
    count = lax.axis_size(axis)
    initial, last = (max(0, -steps), min(count, count - steps))
    return lax.ppermute(value, axis, [(source, source + steps) for source in range(initial, last)])


def extended_2(shard, sides, width):
    for axis, dim in sides:
        peers, length = (lax.axis_size(axis), shard.shape[dim])
        up = [(i, (i + 1) % peers) for i in range(peers - 1)]
        down = [(j, i) for i, j in up]
        last = lax.slice_in_dim(shard, length - width, length, axis=dim)
        initial = lax.slice_in_dim(shard, 0, width, axis=dim)
        before = lax.ppermute(last, axis, up)
        after = lax.ppermute(initial, axis, down)
        shard = jnp.concatenate([before, shard, after], axis=dim)
    return shard


def normalize(values, gamma):
    floats = values.astype(jnp.float32)
    inverse = lax.rsqrt(jnp.mean(floats * floats, axis=-1, keepdims=True) + 1e-06)
    normed = floats * inverse
    return (normed, normed * gamma, inverse)


def tap_list():
    return [
        ((time_tap * 3 + row_tap) * 3 + col_tap, time_tap, row_tap, col_tap)
        for time_tap in range(3)
        for row_tap in range(3)
        for col_tap in range(3)
    ]


def body(features, cotangent, gamma, kernel):
    frames, height, columns, width = features.shape
    normed, pre_act, inverse = normalize(features, gamma)
    active = jax.nn.silu(pre_act).astype(jnp.bfloat16)
    earlier = from_behind(active, "tm", 1)
    extended = extended_2(jnp.concatenate([earlier, active], 0), (("rows", 1),), 1)
    padded = jnp.pad(extended, ((0, 0), (0, 0), (1, 1), (0, 0)))
    cot_rows = cotangent.reshape(-1, width)
    blocks_count = lax.axis_size("tm")
    total = frames * height * columns * blocks_count * lax.axis_size("rows")
    tap_grads = []
    for pixel_tap_index, pixel_time_tap, pixel_row_tap, pixel_col_tap in tap_list():
        window = padded[
            pixel_time_tap : pixel_time_tap + frames,
            pixel_row_tap : pixel_row_tap + height,
            pixel_col_tap : pixel_col_tap + columns,
        ].reshape(-1, width)
        tap_grads.append(
            lax.dot_general(
                cot_rows, window, (((0,), (0,)), ((), ())), preferred_element_type=jnp.float32
            )
        )
    shard = lax.psum_scatter(jnp.stack(tap_grads, 2), "rows", scatter_dimension=0, tiled=True)
    shard = lax.psum_scatter(shard, "tm", scatter_dimension=1, tiled=True)
    weight_grad = jnp.transpose(shard, (1, 2, 0)) * (1.0 / math.sqrt(total))
    grads_ext = jnp.zeros((frames + 2, height + 2, columns + 2, width), jnp.float32)
    for tap_index, time_tap, row_tap, col_tap in tap_list():
        contrib = lax.dot_general(
            cot_rows,
            kernel[:, tap_index, :],
            (((1,), (1,)), ((), ())),
            preferred_element_type=jnp.float32,
        )
        contrib = contrib.reshape(frames, height, columns, width)
        grads_ext = grads_ext.at[
            time_tap : time_tap + frames, row_tap : row_tap + height, col_tap : col_tap + columns
        ].add(contrib)
    trimmed = grads_ext[:, :, 1 : columns + 1]
    handed = from_behind(trimmed[:2], "tm", -1)
    owned = trimmed[2:].at[frames - 2 :].add(handed)
    from_below = from_behind(owned[:, 0], "rows", -1)
    from_above = from_behind(owned[:, height + 1], "rows", 1)
    inner = owned[:, 1 : height + 1].at[:, height - 1].add(from_below).at[:, 0].add(from_above)
    sigma = jax.nn.sigmoid(pre_act)
    grad_pre = inner * sigma * (1.0 + pre_act * (1.0 - sigma))
    grad_norm = grad_pre * gamma
    input_grad = inverse * (
        grad_norm - normed * jnp.mean(grad_norm * normed, axis=-1, keepdims=True)
    )
    return (input_grad.astype(jnp.bfloat16), weight_grad)


def solution(mesh):
    placed = (P("tm", "rows", None, None), P("tm", "rows", None, None), P(), P())
    return jax.shard_map(
        body,
        mesh=mesh,
        in_specs=placed,
        out_specs=(P("tm", "rows", None, None), P("tm", None, "rows")),
        check_vma=False,
    )
```

profile of v0, /device:TPU:1, one launch (start us, length us, event | category | flops | bytes accessed | tf_op | source)
XLA Modules:
  0.0 517.2 jit_solution(18329076282578855303)
XLA Ops:
  26.6 3.5 scatter-add.104
  30.1 3.7 convolution_add_fusion.21
  33.8 5.4 %scatter-add.105 = f32[4,4,162,384]{3,2,1,0:T(8,128)} dynamic-update-slice(f32[4,4,162,384]{3,2,1,0:T(8,128)} %scatter-add.104, f32[2,2,160,384]{3,2,1,0:T(8,128)S(1)} %convolution_add_fusion.21, s32[]{:T(128)} %bitcast.15, s32[]{:T(128)} %bitcast.16, s32[]{:T(128)} %bitcast.17, s32[]{:T(128)} %constant.978.clone.1) | dynamic-update-slice | bytes 1966084 | tf_op jit(solution)/shard_map/scatter-add | solution.py:80
  57.0 3.5 scatter-add.114
  62.3 3.5 scatter-add.115
  70.4 3.5 scatter-add.119
  75.6 3.5 scatter-add.120
  83.7 3.5 scatter-add.124
  89.0 3.5 scatter-add.125
  97.0 3.5 scatter-add.129
  102.3 3.5 scatter-add.130
  110.3 3.5 scatter-add.134
  123.6 3.5 scatter-add.139
  128.9 3.5 scatter-add.140
  135.5 43.0 %collective-permute-done = f32[2,4,160,384]{3,2,1,0:T(8,128)S(1)} collective-permute-done((f32[2,4,160,384]{3,2,1,0:T(8,128)S(1)}, f32[2,4,160,384]{3,2,1,0:T(8,128)S(1)}, u32[]{:S(2)}, u32[]{:S(2)}) %collective-permute-start) | collective-permute-done | bytes 1966112 | tf_op jit(solution)/shard_map/ppermute | solution.py:12
  180.4 5.4 %collective-permute-start.1 = (f32[2,160,384]{2,1,0:T(8,128)S(1)}, f32[2,160,384]{2,1,0:T(8,128)S(1)}, u32[]{:S(2)}, u32[]{:S(2)}) collective-permute-start(f32[2,160,384]{2,1,0:T(8,128)S(1)} %get-tuple-element.395), channel_id=1, source_target_pairs={{4,0},{8,4},{12,8},{16,12},{20,16},{24,20},{28,24},{32,28},{36,32}... | collective-permute-start | bytes 1474568 | tf_op jit(solution)/shard_map/ppermute | solution.py:12
  189.4 4.2 collective-permute-done.1
  199.5 6.6 %collective-permute-done.3 = bf16[2,2,160,384]{3,2,0,1:T(8,128)(2,1)S(1)} collective-permute-done((bf16[2,2,160,384]{3,2,0,1:T(8,128)(2,1)S(1)}, bf16[2,2,160,384]{3,2,0,1:T(8,128)(2,1)S(1)}, u32[]{:S(2)}, u32[]{:S(2)}) %collective-permute-start.3) | collective-permute-done | bytes 491552 | tf_op jit(solution)/shard_map/ppermute | solution.py:12
  206.2 7.8 %collective-permute-start.4 = (bf16[4,1,160,384]{3,2,0,1:T(8,128)(2,1)S(1)}, bf16[4,1,160,384]{3,2,0,1:T(8,128)(2,1)S(1)}, u32[]{:S(2)}, u32[]{:S(2)}) collective-permute-start(bf16[4,1,160,384]{3,2,0,1:T(8,128)(2,1)S(1)} %get-tuple-element.404), channel_id=1, source_target_pairs={{0,4},{4,8},{8,12},{12,16},{16,20},{20,24},{24,28},{28,32},{32,36}... | collective-permute-start | bytes 1474568 | tf_op jit(solution)/shard_map/ppermute | solution.py:22
  216.0 3.8 collective-permute-done.4
  219.8 4.4 collective-permute-done.5
  263.9 19.0 %copy.103 = f32[384,384,27]{1,2,0:T(8,128)} copy(f32[384,384,27]{0,1,2:T(8,128)} %fusion.12) | data formatting | bytes 31850496 | tf_op jit(solution)/shard_map/stack | solution.py:66
  283.0 198.9 %reduce-scatter.5.cloned.1.call-done = f32[6,384,27]{1,2,0:T(8,128)} async-done(((f32[384,384,27]{1,2,0:T(8,128)}), f32[6,384,27]{1,2,0:T(8,128)}) %reduce-scatter.5.cloned.1.call-update) | async-done | bytes 248848 | tf_op jit(solution)/shard_map/reduce_scatter | solution.py:66
  485.5 23.0 %reduce-scatter.7.cloned.1.call-done = f32[96,162]{1,0:T(8,128)} async-done(((f32[384,162]{1,0:T(8,128)}), f32[96,162]{1,0:T(8,128)}) %reduce-scatter.7.cloned.1.call-update) | async-done | bytes 62224
  (99 shorter events, 135.4 us)
Async XLA Ops:
  7.2 1.0 copy-start
  7.2 474.8 %reduce-scatter.5.cloned.1.call-start = ((), (), s32[]{:S(2)}) async-start(), calls=%async_computation.2 | async-start | bytes 19169280 | tf_op jit(solution)/shard_map/reduce_scatter | solution.py:66
  127.1 61.9 %copy-start.1 = (bf16[2,2,160,384]{3,2,1,0:T(8,128)(2,1)S(1)}, bf16[2,2,160,384]{3,2,1,0:T(8,128)(2,1)}, u32[]{:S(2)}) copy-start(bf16[2,2,160,384]{3,2,1,0:T(8,128)(2,1)} %param.66) | copy-start | bytes 1474564
  134.2 60.7 %copy-start.2 = (f32[384]{0:T(512)S(1)}, f32[384]{0:T(512)}, u32[]{:S(2)}) copy-start(f32[384]{0:T(512)} %param.68) | copy-start | bytes 4612
  134.2 44.3 %collective-permute-start = (f32[2,4,160,384]{3,2,1,0:T(8,128)S(1)}, f32[2,4,160,384]{3,2,1,0:T(8,128)S(1)}, u32[]{:S(2)}, u32[]{:S(2)}) collective-permute-start(f32[2,4,160,384]{3,2,1,0:T(8,128)S(1)} %slice.1480), channel_id=1, source_target_pairs={{1,0},{2,1},{3,2},{5,4},{6,5},{7,6},{9,8},{10,9},{11,10},{13,12},{... | collective-permute-start | bytes 5898248 | tf_op jit(solution)/shard_map/ppermute | solution.py:12
  180.4 13.2 %collective-permute-start.1 = (f32[2,160,384]{2,1,0:T(8,128)S(1)}, f32[2,160,384]{2,1,0:T(8,128)S(1)}, u32[]{:S(2)}, u32[]{:S(2)}) collective-permute-start(f32[2,160,384]{2,1,0:T(8,128)S(1)} %get-tuple-element.395), channel_id=1, source_target_pairs={{4,0},{8,4},{12,8},{16,12},{20,16},{24,20},{28,24},{32,28},{36,32}... | collective-permute-start | bytes 1474568 | tf_op jit(solution)/shard_map/ppermute | solution.py:12
  185.8 8.9 %collective-permute-start.2 = (f32[2,160,384]{2,1,0:T(8,128)S(1)}, f32[2,160,384]{2,1,0:T(8,128)S(1)}, u32[]{:S(2)}, u32[]{:S(2)}) collective-permute-start(f32[2,160,384]{2,1,0:T(8,128)S(1)} %get-tuple-element.394), channel_id=1, source_target_pairs={{0,4},{4,8},{8,12},{12,16},{16,20},{20,24},{24,28},{28,32},{32,36}... | collective-permute-start | bytes 1474568 | tf_op jit(solution)/shard_map/ppermute | solution.py:12
  196.3 9.8 %collective-permute-start.3 = (bf16[2,2,160,384]{3,2,0,1:T(8,128)(2,1)S(1)}, bf16[2,2,160,384]{3,2,0,1:T(8,128)(2,1)S(1)}, u32[]{:S(2)}, u32[]{:S(2)}) collective-permute-start(bf16[2,2,160,384]{3,2,0,1:T(8,128)(2,1)S(1)} %get-tuple-element.406), channel_id=1, source_target_pairs={{0,1},{1,2},{2,3},{4,5},{5,6},{6,7},{8,9},{9,10},{10,11},{12,13},{... | collective-permute-start | bytes 1474568 | tf_op jit(solution)/shard_map/ppermute | solution.py:12
  206.2 13.6 %collective-permute-start.4 = (bf16[4,1,160,384]{3,2,0,1:T(8,128)(2,1)S(1)}, bf16[4,1,160,384]{3,2,0,1:T(8,128)(2,1)S(1)}, u32[]{:S(2)}, u32[]{:S(2)}) collective-permute-start(bf16[4,1,160,384]{3,2,0,1:T(8,128)(2,1)S(1)} %get-tuple-element.404), channel_id=1, source_target_pairs={{0,4},{4,8},{8,12},{12,16},{16,20},{20,24},{24,28},{28,32},{32,36}... | collective-permute-start | bytes 1474568 | tf_op jit(solution)/shard_map/ppermute | solution.py:22
  214.0 10.1 %collective-permute-start.5 = (bf16[4,1,160,384]{3,2,0,1:T(8,128)(2,1)S(1)}, bf16[4,1,160,384]{3,2,0,1:T(8,128)(2,1)S(1)}, u32[]{:S(2)}, u32[]{:S(2)}) collective-permute-start(bf16[4,1,160,384]{3,2,0,1:T(8,128)(2,1)S(1)} %get-tuple-element.405), channel_id=1, source_target_pairs={{4,0},{8,4},{12,8},{16,12},{20,16},{24,20},{28,24},{32,28},{36,32}... | collective-permute-start | bytes 1474568 | tf_op jit(solution)/shard_map/ppermute | solution.py:23
  283.0 225.6 %reduce-scatter.7.cloned.1.call-start = ((), (), s32[]{:S(2)}) async-start(), calls=%async_computation.3 | async-start | bytes 491520
Sparse Core Ops, SparseCore 0:
  283.1 198.8 reduce-scatter.4
  484.8 23.7 reduce-scatter.6
where the time goes:
time: 521 us; the launch traced here: 517 us
  waiting for transfers between devices  285 us (55%)
  local copies, waits for them, and re-layouts  96.7 us (19%)
  matrix products  92.2 us (18%)
  starting transfers between devices  22.9 us (4%)
  between operations  14.4 us (3%)
  other arithmetic  5.97 us (1%)
    reduce_scatter x1, waiting for transfers between devices, body(): lax.psum_scatter(jnp.stack(tap_grads, 2), 'rows', scatter_dimension=0, ti...  199 us
    scatter-add x19, local copies, waits for them, and re-layouts, body(): grads_ext = grads_ext.at[time_tap:time_tap + frames, row_tap:row_tap + he...  67.1 us
    dot_general x27, matrix products, body(): lax.dot_general(cot_rows, kernel[:, tap_index, :], (((1,), (1,)), ((), ()...  56.9 us
    ppermute x4, waiting for transfers between devices, from_behind(): lax.ppermute(value, axis, [(source, source + steps) for source in range(i...  54.9 us
    dot_general x27, matrix products, body(): lax.dot_general(cot_rows, window, (((0,), (0,)), ((), ())), preferred_ele...  35.2 us
    unnamed x3, waiting for transfers between devices  23.1 us
    another operation x1, local copies, waits for them, and re-layouts, body(): jnp.stack(tap_grads, 2)  19 us
    ppermute x4, starting transfers between devices, from_behind(): lax.ppermute(value, axis, [(source, source + steps) for source in range(i...  13.1 us
  transfers between devices with their start and end apart: 8, of which 8 were waited for; matrix products, arithmetic and copies ran while one was open for 0% of the time, Pallas kernels for 0%

commit v1 on v0

v1 whole, which is shorter than its diff:
```python
import functools
import math

import jax
import jax.numpy as jnp
import numpy as np
from jax import lax
from jax.experimental import pallas as pl
from jax.experimental.pallas import tpu as pltpu
from jax.sharding import PartitionSpec as P

F32, BF16 = jnp.float32, jnp.bfloat16
VMEM_LIMIT = 60 * 1024 * 1024
C, COLS, PART, LANES = 384, 160, 96, 128
ZS, XS, YS, SLOTS = 8, 4, 4, 14
NT = (((1,), (1,)), ((), ()))


def rows_perm(move):
    pairs = []
    for z in range(ZS):
        for x in range(XS):
            for c in range(2):
                z2, x2, c2 = move(z, x, c)
                pairs.append(((z * XS + x) * 2 + c, (z2 * XS + x2) * 2 + c2))
    return pairs


def z_shift(steps):
    return rows_perm(lambda z, x, c: ((z + steps) % ZS, x, c))


def x_shift(steps):
    return rows_perm(lambda z, x, c: (z, (x + steps) % XS, c))


def core_swap():
    return rows_perm(lambda z, x, c: (z, x, 1 - c))


def y_shift(steps):
    return [(i, (i + steps) % YS) for i in range(YS)]


def line(count, steps):
    return [(i, i + steps) for i in range(count) if 0 <= i + steps < count]


def activation_kernel(features_ref, gamma_ref, out_ref):
    floats = features_ref[...].astype(F32)
    inverse = lax.rsqrt(jnp.mean(floats * floats, axis=-1, keepdims=True) + 1e-6)
    pre_act = floats * inverse * gamma_ref[...]
    active = pre_act * jax.nn.sigmoid(pre_act)
    blank = jnp.zeros((active.shape[0], LANES - PART), F32)
    for part in range(YS):
        piece = active[:, part * PART : (part + 1) * PART]
        out_ref[part] = jnp.concatenate([piece, blank], axis=1).astype(BF16)


def activations(features, gamma):
    pixels = features.shape[0]
    return pl.pallas_call(
        activation_kernel,
        out_shape=jax.ShapeDtypeStruct((YS, pixels, LANES), BF16),
        compiler_params=pltpu.CompilerParams(vmem_limit_bytes=VMEM_LIMIT),
    )(features, gamma)


def weight_kernel(meta_ref, c3, c2, c1, c0, a3, a2, a1, a0, up, dn, order_ref, own, send, same, before, cot, acc):
    y, core = meta_ref[0], meta_ref[1]
    cots, acts = (c0, c1, c2, c3), (a0, a1, a2, a3)
    column = lax.broadcasted_iota(jnp.int32, (4 * COLS, LANES), 0) % COLS
    for k in range(4):
        place = 3 - k
        for f in range(2):
            value = jnp.concatenate(
                [up[k, f, 0], acts[k][f, 0], acts[k][f, 1], dn[k, f, 0]], axis=0
            ).astype(F32)
            left = jnp.where(column == 0, 0.0, pltpu.roll(value, 1, 0))
            right = jnp.where(column == COLS - 1, 0.0, pltpu.roll(value, 4 * COLS - 1, 0))
            spread = jnp.concatenate([left, value, right], axis=1).astype(BF16)
            same[place * 2 + f] = spread
            later = (k + 3) % 4
            first = lax.rem(y - later + 4, 4) == 0
            before[(3 - later) * 2 + f] = jnp.where(first, jnp.zeros_like(spread), spread)
        block = lax.dot_general(
            order_ref[...], cots[k][...], NT, preferred_element_type=F32
        )
        cot[:, place * 640 : (place + 1) * 640] = block.astype(BF16)

    def window(a, b, low, count):
        rows, lanes = slice(b * COLS, (b + 2) * COLS), slice(low, low + count)
        pieces = []
        for place in range(4):
            for f in range(2):
                if a == 2:
                    pieces.append(same[place * 2 + f, rows, lanes])
                elif a == 0:
                    pieces.append(before[place * 2 + f, rows, lanes])
                elif f == 0:
                    pieces.append(before[place * 2 + 1, rows, lanes])
                else:
                    pieces.append(same[place * 2, rows, lanes])
        return jnp.concatenate(pieces, axis=0)

    def put(tap, value):
        half, slot = divmod(tap, SLOTS)
        rows, lanes = slice(half * 24, half * 24 + 24), slice(slot * LANES, slot * LANES + LANES)
        for c in range(2):
            chunk = value[c * 192 : (c + 1) * 192].reshape(ZS, 24, LANES)

            @pl.when(core == c)
            def _():
                own[:, rows, lanes] = chunk

            @pl.when(core != c)
            def _():
                acc[:, rows, lanes] = chunk

    def product(windows):
        return jnp.dot(cot[...], windows, preferred_element_type=F32)

    for a in range(3):
        for b in range(3):
            both = product(window(a, b, 0, 256))
            put((a * 3 + b) * 3, both[:, :LANES])
            put((a * 3 + b) * 3 + 1, both[:, LANES:])
    last = [(a, b) for a in range(3) for b in range(3)]
    for at in range(0, 9, 2):
        group = last[at : at + 2]
        result = product(jnp.concatenate([window(a, b, 256, 128) for a, b in group], axis=1))
        for n, (a, b) in enumerate(group):
            put((a * 3 + b) * 3 + 2, result[:, n * LANES : (n + 1) * LANES])
    put(27, jnp.zeros((C, LANES), F32))
    send[...] = acc[...].astype(BF16)


def weight_partials(meta, cots, acts, up, dn, order):
    shape = (ZS, 48, SLOTS * LANES)
    return pl.pallas_call(
        weight_kernel,
        in_specs=[pl.BlockSpec(memory_space=pltpu.SMEM)] + [pl.BlockSpec(memory_space=pltpu.VMEM)] * 11,
        out_specs=[pl.BlockSpec(memory_space=pltpu.VMEM)] * 2,
        out_shape=[jax.ShapeDtypeStruct(shape, F32), jax.ShapeDtypeStruct(shape, BF16)],
        scratch_shapes=[
            pltpu.VMEM((8, 4 * COLS, C), BF16),
            pltpu.VMEM((8, 4 * COLS, C), BF16),
            pltpu.VMEM((C, 2560), BF16),
            pltpu.VMEM(shape, F32),
        ],
        compiler_params=pltpu.CompilerParams(vmem_limit_bytes=VMEM_LIMIT),
        cost_estimate=pl.CostEstimate(flops=14 * 2 * 384 * 2560 * 256, bytes_accessed=8_000_000, transcendentals=0),
    )(meta, *cots[::-1], *acts[::-1], up, dn, order)


def input_kernel(meta_ref, own, following, up, dn, taps_ref, features_ref, gamma_ref, out_ref, ext, side, total):
    a, e = pl.program_id(1), pl.program_id(0)

    @pl.when((a == 0) & (e == 0))
    def _():
        keep = meta_ref[0] != 3
        for f in range(2):
            ext[f, COLS : 3 * COLS] = own[f]
            ext[f + 2, COLS : 3 * COLS] = jnp.where(keep, following[f], jnp.zeros_like(following[f]))
        for f in range(4):
            good = keep if f >= 2 else True
            ext[f, :COLS] = jnp.where(good, up[f], jnp.zeros_like(up[f]))
            ext[f, 3 * COLS :] = jnp.where(good, dn[f], jnp.zeros_like(dn[f]))

    rows = []
    for f in range(2):
        pieces = [ext[f + 2 - a, (2 - b) * COLS : (4 - b) * COLS] for b in range(3)]
        rows.append(jnp.concatenate(pieces, axis=1))
    weights = jnp.concatenate([taps_ref[0, b, 0] for b in range(3)], axis=1)
    value = lax.dot_general(jnp.concatenate(rows, axis=0), weights, NT, preferred_element_type=F32)

    @pl.when(a == 0)
    def _():
        side[...] = value

    @pl.when(a != 0)
    def _():
        side[...] += value

    column = lax.broadcasted_iota(jnp.int32, (4 * COLS, C), 0) % COLS

    @pl.when((a == 2) & (e == 0))
    def _():
        total[...] = jnp.where(column == COLS - 1, 0.0, pltpu.roll(side[...], 4 * COLS - 1, 0))

    @pl.when((a == 2) & (e == 1))
    def _():
        total[...] += side[...]

    @pl.when((a == 2) & (e == 2))
    def _():
        grad_act = total[...] + jnp.where(column == 0, 0.0, pltpu.roll(side[...], 1, 0))
        gamma = gamma_ref[...]
        floats = features_ref[...].astype(F32)
        inverse = lax.rsqrt(jnp.mean(floats * floats, axis=-1, keepdims=True) + 1e-6)
        normed = floats * inverse
        pre_act = normed * gamma
        sigma = jax.nn.sigmoid(pre_act)
        grad_norm = grad_act * sigma * (1.0 + pre_act * (1.0 - sigma)) * gamma
        inner = jnp.mean(grad_norm * normed, axis=-1, keepdims=True)
        out_ref[...] = (inverse * (grad_norm - normed * inner)).astype(BF16)


def input_gradient(meta, own, following, up, dn, taps, features, gamma):
    pixels = features.shape[0]
    whole = lambda shape: pl.BlockSpec(shape, lambda e, a: (0,) * len(shape))
    return pl.pallas_call(
        input_kernel,
        grid=(3, 3),
        in_specs=[
            pl.BlockSpec(memory_space=pltpu.SMEM),
            whole((2, 2 * COLS, C)),
            whole((2, 2 * COLS, C)),
            whole((4, COLS, C)),
            whole((4, COLS, C)),
            pl.BlockSpec((1, 3, 1, C, C), lambda e, a: (a, 0, e, 0, 0)),
            whole((pixels, C)),
            whole((1, C)),
        ],
        out_specs=whole((pixels, C)),
        out_shape=jax.ShapeDtypeStruct((pixels, C), BF16),
        scratch_shapes=[
            pltpu.VMEM((4, 4 * COLS, C), BF16),
            pltpu.VMEM((pixels, C), F32),
            pltpu.VMEM((pixels, C), F32),
        ],
        compiler_params=pltpu.CompilerParams(vmem_limit_bytes=VMEM_LIMIT),
        cost_estimate=pl.CostEstimate(flops=27 * 2 * 640 * C * C, bytes_accessed=12_000_000, transcendentals=0),
    )(meta, own, following, up, dn, taps, features, gamma)


def output_order():
    order = np.zeros((C, C), np.float32)
    for c in range(2):
        for z in range(ZS):
            for x in range(XS):
                for j in range(6):
                    order[((c * ZS + z) * XS + x) * 6 + j, ((z * XS + x) * 2 + c) * 6 + j] = 1.0
    return jnp.asarray(order, BF16)


def body(features, cotangent, gamma, kernel):
    frames, height, columns, width = features.shape
    pixels = frames * height * columns
    y, r = lax.axis_index("tm"), lax.axis_index("rows")
    z, x, core = r // (2 * XS), (r // 2) % XS, r % 2
    meta = jnp.stack([y, core]).astype(jnp.int32)
    gamma = gamma.reshape(1, width)
    flat = features.reshape(pixels, width)

    cots = [cotangent] + [lax.ppermute(cotangent, "tm", y_shift(k)) for k in (1, 2, 3)]
    taps = jnp.transpose(kernel, (1, 0, 2)).reshape(3, 3, 3, width, width)
    active = activations(flat, gamma)
    acts = [lax.dynamic_index_in_dim(active, y, 0, keepdims=False)]
    for k in (1, 2, 3):
        piece = lax.dynamic_index_in_dim(active, (y + k) % YS, 0, keepdims=False)
        acts.append(lax.ppermute(piece, "tm", y_shift(k)))
    acts = [value.reshape(2, 2, columns, LANES) for value in acts]
    stacked = jnp.stack(acts)
    act_up = lax.ppermute(stacked[:, :, 1:], "rows", line(64, 1))
    act_dn = lax.ppermute(stacked[:, :, :1], "rows", line(64, -1))
    own, send = weight_partials(
        meta, [c.reshape(pixels, width) for c in cots], acts, act_up, act_dn, output_order()
    )
    other = lax.ppermute(send, "rows", core_swap())

    following = cots[3]
    ext = jnp.concatenate([cotangent, following], axis=0)
    cot_up = lax.ppermute(ext[:, 1], "rows", line(64, 1))
    cot_dn = lax.ppermute(ext[:, 0], "rows", line(64, -1))
    input_grad = input_gradient(
        meta,
        cotangent.reshape(2, 2 * columns, width),
        following.reshape(2, 2 * columns, width),
        cot_up,
        cot_dn,
        taps,
        flat,
        gamma,
    )

    def chunk(offset):
        at = (z + offset) % ZS
        return lax.dynamic_index_in_dim(own, at, 0, keepdims=False) + lax.dynamic_index_in_dim(
            other, at, 0, keepdims=False
        ).astype(F32)

    ahead = lax.ppermute(chunk(4).astype(BF16), "rows", z_shift(1))
    behind = lax.ppermute(chunk(-3).astype(BF16), "rows", z_shift(-1))
    for step in (3, 2, 1):
        ahead = lax.ppermute((ahead.astype(F32) + chunk(step)).astype(BF16), "rows", z_shift(1))
        if step > 1:
            behind = lax.ppermute(
                (behind.astype(F32) + chunk(1 - step)).astype(BF16), "rows", z_shift(-1)
            )
    total = chunk(0) + ahead.astype(F32) + behind.astype(F32)
    total = total.reshape(2, XS, 6, SLOTS * LANES)
    mine = lax.dynamic_index_in_dim(total, x, 1, keepdims=False)
    for k in (1, 2, 3):
        piece = lax.dynamic_index_in_dim(total, (x + k) % XS, 1, keepdims=False)
        mine = mine + lax.ppermute(piece, "rows", x_shift(k))
    mine = mine.reshape(2, 6, SLOTS, LANES)[..., :PART]
    mine = jnp.transpose(mine, (3, 0, 2, 1)).reshape(PART, 2 * SLOTS, 6)[:, :27]
    count = frames * height * columns * lax.axis_size("tm") * lax.axis_size("rows")
    weight_grad = mine * (1.0 / math.sqrt(count))
    return input_grad.reshape(features.shape), weight_grad


def solution(mesh):
    placed = (P("tm", "rows", None, None), P("tm", "rows", None, None), P(), P())
    return jax.shard_map(
        body,
        mesh=mesh,
        in_specs=placed,
        out_specs=(P("tm", "rows", None, None), P("tm", None, "rows")),
        check_vma=False,
    )
```

time: 521 us -> 141 us (0.27)
  the two profiles are of different devices: /device:TPU:1 before, /device:TPU:79 now
where the time goes in v1:
time: 141 us; the launch traced here: 140 us
  waiting for transfers between devices  50.3 us (36%)
  Pallas kernels  40.3 us (29%)
  starting transfers between devices  37 us (26%)
  other arithmetic  7.1 us (5%)
  local copies, waits for them, and re-layouts  4.6 us (3%)
    pallas_call x1, Pallas kernels, weight_partials(): pl.pallas_call(weight_kernel, in_specs=[pl.BlockSpec(memory_space=pltpu.S...  22.8 us
    ppermute x3, waiting for transfers between devices, body(): acts.append(lax.ppermute(piece, 'tm', y_shift(k)))  19.7 us
    pallas_call x1, Pallas kernels, input_gradient(): pl.pallas_call(input_kernel, grid=(3, 3), in_specs=[pl.BlockSpec(memory_s...  15.1 us
    ppermute x1, waiting for transfers between devices, body(): cot_dn = lax.ppermute(ext[:, 0], 'rows', line(64, -1))  8.11 us
    ppermute x3, starting transfers between devices, body(): lax.ppermute((ahead.astype(F32) + chunk(step)).astype(BF16), 'rows', z_sh...  7.3 us
    ppermute x1, starting transfers between devices, body(): cot_up = lax.ppermute(ext[:, 1], 'rows', line(64, 1))  6.81 us
    ppermute x1, waiting for transfers between devices, body(): act_dn = lax.ppermute(stacked[:, :, :1], 'rows', line(64, -1))  6.61 us
    ppermute x3, starting transfers between devices, body(): acts.append(lax.ppermute(piece, 'tm', y_shift(k)))  5 us
  transfers between devices with their start and end apart: 21, of which 11 were waited for; matrix products, arithmetic and copies ran while one was open for 5% of the time, Pallas kernels for 12%

profile of v1, /device:TPU:79, one launch (start us, length us, event | category | flops | bytes accessed | tf_op | source)
XLA Modules:
  0.0 140.2 jit_solution(8183549045474721500)
XLA Ops:
  0.6 2.1 %collective-permute-start.3 = (bf16[2,2,160,384]{3,2,1,0:T(8,128)(2,1)}, bf16[2,2,160,384]{3,2,1,0:T(8,128)(2,1)}, u32[]{:S(2)}, u32[]{:S(2)}) collective-permute-start(bf16[2,2,160,384]{3,2,1,0:T(8,128)(2,1)} %param.6), channel_id=1, source_target_pairs={{0,2},{1,3},{2,0},{3,1},{4,6},{5,7},{6,4},{7,5},{8,10},{9,11},{10,... | collective-permute-start | bytes 1474568 | tf_op jit(solution)/shard_map/ppermute | solution.py:256
  4.0 2.4 %shard_map.69 = bf16[4,640,128]{2,1,0:T(8,128)(2,1)} custom-call(bf16[640,384]{1,0:T(8,128)(2,1)} %bitcast.82, f32[1,384]{1,0:T(1,128)} %reshape.79.gamma_ref), custom_call_target="tpu_custom_call" | custom-call | tf_op jit(solution)/shard_map/pallas_call | solution.py:62
  7.6 1.5 %collective-permute-start.5 = (bf16[640,128]{1,0:T(8,128)(2,1)S(1)}, bf16[640,128]{1,0:T(8,128)(2,1)S(1)}, u32[]{:S(2)}, u32[]{:S(2)}) collective-permute-start(bf16[640,128]{1,0:T(8,128)(2,1)S(1)} %get-tuple-element.19), channel_id=1, source_target_pairs={{0,3},{1,0},{2,1},{3,2},{4,7},{5,4},{6,5},{7,6},{8,11},{9,8},{10,9... | collective-permute-start | bytes 491528 | tf_op jit(solution)/shard_map/ppermute | solution.py:262
  10.6 2.0 %collective-permute-start.7 = (bf16[640,128]{1,0:T(8,128)(2,1)S(1)}, bf16[640,128]{1,0:T(8,128)(2,1)S(1)}, u32[]{:S(2)}, u32[]{:S(2)}) collective-permute-start(bf16[640,128]{1,0:T(8,128)(2,1)S(1)} %get-tuple-element.17), channel_id=1, source_target_pairs={{0,1},{1,2},{2,3},{3,0},{4,5},{5,6},{6,7},{7,4},{8,9},{9,10},{10,1... | collective-permute-start | bytes 491528 | tf_op jit(solution)/shard_map/ppermute | solution.py:262
  12.7 7.5 %collective-permute-done.5 = bf16[640,128]{1,0:T(8,128)(2,1)S(1)} collective-permute-done((bf16[640,128]{1,0:T(8,128)(2,1)S(1)}, bf16[640,128]{1,0:T(8,128)(2,1)S(1)}, u32[]{:S(2)}, u32[]{:S(2)}) %collective-permute-start.5) | collective-permute-done | bytes 163872 | tf_op jit(solution)/shard_map/ppermute | solution.py:262
  21.6 10.7 %collective-permute-done.7 = bf16[640,128]{1,0:T(8,128)(2,1)S(1)} collective-permute-done((bf16[640,128]{1,0:T(8,128)(2,1)S(1)}, bf16[640,128]{1,0:T(8,128)(2,1)S(1)}, u32[]{:S(2)}, u32[]{:S(2)}) %collective-permute-start.7) | collective-permute-done | bytes 163872 | tf_op jit(solution)/shard_map/ppermute | solution.py:262
  33.1 4.8 %collective-permute-start.8 = (bf16[4,2,1,160,128]{4,3,2,1,0:T(8,128)(2,1)S(1)}, bf16[4,2,1,160,128]{4,3,2,1,0:T(8,128)(2,1)S(1)}, u32[]{:S(2)}, u32[]{:S(2)}) collective-permute-start(bf16[4,2,1,160,128]{4,3,2,1,0:T(8,128)(2,1)S(1)} %get-tuple-element.15), channel_id=1, source_target_pairs={{0,4},{4,8},{8,12},{12,16},{16,20},{20,24},{24,28},{28,32},{32,36}... | collective-permute-start | bytes 983048 | tf_op jit(solution)/shard_map/ppermute | solution.py:265
  38.0 1.9 %collective-permute-start.9 = (bf16[4,2,1,160,128]{4,3,2,1,0:T(8,128)(2,1)S(1)}, bf16[4,2,1,160,128]{4,3,2,1,0:T(8,128)(2,1)}, u32[]{:S(2)}, u32[]{:S(2)}) collective-permute-start(bf16[4,2,1,160,128]{4,3,2,1,0:T(8,128)(2,1)S(1)} %get-tuple-element.14), channel_id=1, source_target_pairs={{4,0},{8,4},{12,8},{16,12},{20,16},{24,20},{28,24},{32,28},{36,32}... | collective-permute-start | bytes 983048 | tf_op jit(solution)/shard_map/ppermute | solution.py:266
  42.0 6.6 %collective-permute-done.9.dn = bf16[4,2,1,160,128]{4,3,2,1,0:T(8,128)(2,1)} collective-permute-done((bf16[4,2,1,160,128]{4,3,2,1,0:T(8,128)(2,1)S(1)}, bf16[4,2,1,160,128]{4,3,2,1,0:T(8,128)(2,1)}, u32[]{:S(2)}, u32[]{:S(2)}) %collective-permute-start.9) | collective-permute-done | bytes 327712 | tf_op jit(solution)/shard_map/ppermute | solution.py:266
  48.6 22.8 %shard_map.70 = (f32[8,48,1792]{2,1,0:T(8,128)}, bf16[8,48,1792]{2,1,0:T(8,128)(2,1)}) custom-call(s32[2]{0:T(128)} %pad_add_fusion.meta_ref, bf16[640,384]{1,0:T(8,128)(2,1)} %bitcast.86, bf16[640,384]{1,0:T(8,128)(2,1)} %bitcast.11.c2, bf16[640,384]{1,0:T(8,128)(2,1)} %bitcast.12.c1, bf16[640,384]{1,0:T(8,128)(2,1)} %bitcast.84, ...), custom_call_target="tpu_custom_call" | custom-call | flops 7046430720 | bytes 8000000 | tf_op jit(solution)/shard_map/pallas_call | solution.py:140
  71.4 3.3 %collective-permute-done.10 = bf16[8,48,1792]{2,1,0:T(8,128)(2,1)S(1)} collective-permute-done((bf16[8,48,1792]{2,1,0:T(8,128)(2,1)}, bf16[8,48,1792]{2,1,0:T(8,128)(2,1)S(1)}, u32[]{:S(2)}, u32[]{:S(2)}) %collective-permute-start.10) | collective-permute-done | bytes 1376288 | tf_op jit(solution)/shard_map/ppermute | solution.py:270
  75.9 4.1 %collective-permute-start.11 = (bf16[48,1792]{1,0:T(8,128)(2,1)S(1)}, bf16[48,1792]{1,0:T(8,128)(2,1)S(1)}, u32[]{:S(2)}, u32[]{:S(2)}) collective-permute-start(bf16[48,1792]{1,0:T(8,128)(2,1)S(1)} %get-tuple-element.10), channel_id=1, source_target_pairs={{0,32},{4,36},{8,40},{12,44},{16,48},{20,52},{24,56},{28,60},{32,6... | collective-permute-start | bytes 516104 | tf_op jit(solution)/shard_map/ppermute | solution.py:293
  80.1 3.6 %collective-permute-done.11 = bf16[48,1792]{1,0:T(8,128)(2,1)S(1)} collective-permute-done((bf16[48,1792]{1,0:T(8,128)(2,1)S(1)}, bf16[48,1792]{1,0:T(8,128)(2,1)S(1)}, u32[]{:S(2)}, u32[]{:S(2)}) %collective-permute-start.11) | collective-permute-done | bytes 172064 | tf_op jit(solution)/shard_map/ppermute | solution.py:293
  84.8 2.3 %collective-permute-start.12 = (bf16[48,1792]{1,0:T(8,128)(2,1)S(1)}, bf16[48,1792]{1,0:T(8,128)(2,1)S(1)}, u32[]{:S(2)}, u32[]{:S(2)}) collective-permute-start(bf16[48,1792]{1,0:T(8,128)(2,1)S(1)} %fusion.4), channel_id=1, source_target_pairs={{0,32},{4,36},{8,40},{12,44},{16,48},{20,52},{24,56},{28,60},{32,6... | collective-permute-start | bytes 516104 | tf_op jit(solution)/shard_map/ppermute | solution.py:296
  87.0 2.7 %collective-permute-done.12 = bf16[48,1792]{1,0:T(8,128)(2,1)S(1)} collective-permute-done((bf16[48,1792]{1,0:T(8,128)(2,1)S(1)}, bf16[48,1792]{1,0:T(8,128)(2,1)S(1)}, u32[]{:S(2)}, u32[]{:S(2)}) %collective-permute-start.12) | collective-permute-done | bytes 172064 | tf_op jit(solution)/shard_map/ppermute | solution.py:296
  91.0 2.3 %collective-permute-start.13 = (bf16[48,1792]{1,0:T(8,128)(2,1)S(1)}, bf16[48,1792]{1,0:T(8,128)(2,1)S(1)}, u32[]{:S(2)}, u32[]{:S(2)}) collective-permute-start(bf16[48,1792]{1,0:T(8,128)(2,1)S(1)} %get-tuple-element.8), channel_id=1, source_target_pairs={{0,32},{4,36},{8,40},{12,44},{16,48},{20,52},{24,56},{28,60},{32,6... | collective-permute-start | bytes 516104 | tf_op jit(solution)/shard_map/ppermute | solution.py:296
  93.3 2.3 %collective-permute-done.13 = bf16[48,1792]{1,0:T(8,128)(2,1)S(1)} collective-permute-done((bf16[48,1792]{1,0:T(8,128)(2,1)S(1)}, bf16[48,1792]{1,0:T(8,128)(2,1)S(1)}, u32[]{:S(2)}, u32[]{:S(2)}) %collective-permute-start.13) | collective-permute-done | bytes 172064 | tf_op jit(solution)/shard_map/ppermute | solution.py:296
  95.6 3.4 %collective-permute-done.16 = bf16[48,1792]{1,0:T(8,128)(2,1)S(1)} collective-permute-done((bf16[48,1792]{1,0:T(8,128)(2,1)S(1)}, bf16[48,1792]{1,0:T(8,128)(2,1)S(1)}, u32[]{:S(2)}, u32[]{:S(2)}) %collective-permute-start.16) | collective-permute-done | bytes 172064 | tf_op jit(solution)/shard_map/ppermute | solution.py:298
  100.3 2.7 %collective-permute-start.14 = (bf16[48,1792]{1,0:T(8,128)(2,1)S(1)}, bf16[48,1792]{1,0:T(8,128)(2,1)S(1)}, u32[]{:S(2)}, u32[]{:S(2)}) collective-permute-start(bf16[48,1792]{1,0:T(8,128)(2,1)S(1)} %get-tuple-element.6), channel_id=1, source_target_pairs={{0,32},{4,36},{8,40},{12,44},{16,48},{20,52},{24,56},{28,60},{32,6... | collective-permute-start | bytes 516104 | tf_op jit(solution)/shard_map/ppermute | solution.py:296
  103.1 6.8 %collective-permute-start.1 = (bf16[4,160,384]{2,1,0:T(8,128)(2,1)S(1)}, bf16[4,160,384]{2,1,0:T(8,128)(2,1)}, u32[]{:S(2)}, u32[]{:S(2)}) collective-permute-start(bf16[4,160,384]{2,1,0:T(8,128)(2,1)S(1)} %get-tuple-element.13), channel_id=1, source_target_pairs={{0,4},{4,8},{8,12},{12,16},{16,20},{20,24},{24,28},{28,32},{32,36}... | collective-permute-start | bytes 1474568 | tf_op jit(solution)/shard_map/ppermute | solution.py:274
  109.9 1.9 %collective-permute-start.2 = (bf16[4,160,384]{2,1,0:T(8,128)(2,1)S(1)}, bf16[4,160,384]{2,1,0:T(8,128)(2,1)}, u32[]{:S(2)}, u32[]{:S(2)}) collective-permute-start(bf16[4,160,384]{2,1,0:T(8,128)(2,1)S(1)} %get-tuple-element.12), channel_id=1, source_target_pairs={{4,0},{8,4},{12,8},{16,12},{20,16},{24,20},{28,24},{32,28},{36,32}... | collective-permute-start | bytes 1474568 | tf_op jit(solution)/shard_map/ppermute | solution.py:275
  113.4 2.7 %collective-permute-start.18 = (f32[2,6,1792]{2,0,1:T(2,128)S(1)}, f32[2,6,1792]{2,0,1:T(2,128)S(1)}, u32[]{:S(2)}, u32[]{:S(2)}) collective-permute-start(f32[2,6,1792]{2,0,1:T(2,128)S(1)} %bitcast.96), channel_id=1, source_target_pairs={{0,8},{4,12},{8,16},{12,20},{16,24},{20,28},{24,0},{28,4},{32,40},... | collective-permute-start | bytes 258056 | tf_op jit(solution)/shard_map/ppermute | solution.py:306
  116.1 8.1 %collective-permute-done.2.dn = bf16[4,160,384]{2,1,0:T(8,128)(2,1)} collective-permute-done((bf16[4,160,384]{2,1,0:T(8,128)(2,1)S(1)}, bf16[4,160,384]{2,1,0:T(8,128)(2,1)}, u32[]{:S(2)}, u32[]{:S(2)}) %collective-permute-start.2) | collective-permute-done | bytes 491552 | tf_op jit(solution)/shard_map/ppermute | solution.py:275
  124.2 15.1 %shard_map.68 = bf16[640,384]{1,0:T(8,128)(2,1)} custom-call(s32[2]{0:T(128)} %pad_add_fusion.meta_ref, bf16[2,320,384]{2,1,0:T(8,128)(2,1)} %bitcast.85, bf16[2,320,384]{2,1,0:T(8,128)(2,1)} %bitcast.87, bf16[4,160,384]{2,1,0:T(8,128)(2,1)} %collective-permute-done.1.up, bf16[4,160,384]{2,1,0:T(8,128)(2,1)} %collective-permute-done.2.dn, ...), custom_call_target="tpu_custom_call" | custom-call | flops 5096079360 | bytes 12000000 | tf_op jit(solution)/shard_map/pallas_call | solution.py:212
  (57 shorter events, 15.5 us)
Async XLA Ops:
  0.6 11.9 %copy-start.1 = (bf16[2,2,160,384]{3,2,1,0:T(8,128)(2,1)S(1)}, bf16[2,2,160,384]{3,2,1,0:T(8,128)(2,1)}, u32[]{:S(2)}) copy-start(bf16[2,2,160,384]{3,2,1,0:T(8,128)(2,1)} %param.6) | copy-start | bytes 1474564
  0.6 40.8 %collective-permute-start.3 = (bf16[2,2,160,384]{3,2,1,0:T(8,128)(2,1)}, bf16[2,2,160,384]{3,2,1,0:T(8,128)(2,1)}, u32[]{:S(2)}, u32[]{:S(2)}) collective-permute-start(bf16[2,2,160,384]{3,2,1,0:T(8,128)(2,1)} %param.6), channel_id=1, source_target_pairs={{0,2},{1,3},{2,0},{3,1},{4,6},{5,7},{6,4},{7,5},{8,10},{9,11},{10,... | collective-permute-start | bytes 1474568 | tf_op jit(solution)/shard_map/ppermute | solution.py:256
  2.7 38.7 %collective-permute-start.4 = (bf16[2,2,160,384]{3,2,1,0:T(8,128)(2,1)}, bf16[2,2,160,384]{3,2,1,0:T(8,128)(2,1)}, u32[]{:S(2)}, u32[]{:S(2)}) collective-permute-start(bf16[2,2,160,384]{3,2,1,0:T(8,128)(2,1)} %param.6), channel_id=1, source_target_pairs={{0,1},{1,2},{2,3},{3,0},{4,5},{5,6},{6,7},{7,4},{8,9},{9,10},{10,1... | collective-permute-start | bytes 1474568 | tf_op jit(solution)/shard_map/ppermute | solution.py:256
  7.6 41.1 %copy-start = (bf16[1,640,128]{2,1,0:T(8,128)(2,1)}, bf16[1,640,128]{2,1,0:T(8,128)(2,1)S(1)}, u32[]{:S(2)}) copy-start(bf16[1,640,128]{2,1,0:T(8,128)(2,1)S(1)} %get-tuple-element.16) | copy-start | bytes 491524
  7.6 12.6 %collective-permute-start.5 = (bf16[640,128]{1,0:T(8,128)(2,1)S(1)}, bf16[640,128]{1,0:T(8,128)(2,1)S(1)}, u32[]{:S(2)}, u32[]{:S(2)}) collective-permute-start(bf16[640,128]{1,0:T(8,128)(2,1)S(1)} %get-tuple-element.19), channel_id=1, source_target_pairs={{0,3},{1,0},{2,1},{3,2},{4,7},{5,4},{6,5},{7,6},{8,11},{9,8},{10,9... | collective-permute-start | bytes 491528 | tf_op jit(solution)/shard_map/ppermute | solution.py:262
  9.1 12.5 %collective-permute-start.6 = (bf16[640,128]{1,0:T(8,128)(2,1)S(1)}, bf16[640,128]{1,0:T(8,128)(2,1)S(1)}, u32[]{:S(2)}, u32[]{:S(2)}) collective-permute-start(bf16[640,128]{1,0:T(8,128)(2,1)S(1)} %get-tuple-element.18), channel_id=1, source_target_pairs={{0,2},{1,3},{2,0},{3,1},{4,6},{5,7},{6,4},{7,5},{8,10},{9,11},{10,... | collective-permute-start | bytes 491528 | tf_op jit(solution)/shard_map/ppermute | solution.py:262
  10.6 21.7 %collective-permute-start.7 = (bf16[640,128]{1,0:T(8,128)(2,1)S(1)}, bf16[640,128]{1,0:T(8,128)(2,1)S(1)}, u32[]{:S(2)}, u32[]{:S(2)}) collective-permute-start(bf16[640,128]{1,0:T(8,128)(2,1)S(1)} %get-tuple-element.17), channel_id=1, source_target_pairs={{0,1},{1,2},{2,3},{3,0},{4,5},{5,6},{6,7},{7,4},{8,9},{9,10},{10,1... | collective-permute-start | bytes 491528 | tf_op jit(solution)/shard_map/ppermute | solution.py:262
  20.2 28.4 %copy-start.2 = (bf16[640,128]{1,0:T(8,128)(2,1)}, bf16[640,128]{1,0:T(8,128)(2,1)S(1)}, u32[]{:S(2)}) copy-start(bf16[640,128]{1,0:T(8,128)(2,1)S(1)} %collective-permute-done.5) | copy-start | bytes 491524
  20.2 20.4 %collective-permute-start = (bf16[2,2,160,384]{3,2,0,1:T(8,128)(2,1)S(1)}, bf16[2,2,160,384]{3,2,0,1:T(8,128)(2,1)S(1)}, u32[]{:S(2)}, u32[]{:S(2)}) collective-permute-start(bf16[2,2,160,384]{3,2,0,1:T(8,128)(2,1)S(1)} %get-tuple-element.21), channel_id=1, source_target_pairs={{0,3},{1,0},{2,1},{3,2},{4,7},{5,4},{6,5},{7,6},{8,11},{9,8},{10,9... | collective-permute-start | bytes 1474568 | tf_op jit(solution)/shard_map/ppermute | solution.py:256
  33.1 8.9 %collective-permute-start.8 = (bf16[4,2,1,160,128]{4,3,2,1,0:T(8,128)(2,1)S(1)}, bf16[4,2,1,160,128]{4,3,2,1,0:T(8,128)(2,1)S(1)}, u32[]{:S(2)}, u32[]{:S(2)}) collective-permute-start(bf16[4,2,1,160,128]{4,3,2,1,0:T(8,128)(2,1)S(1)} %get-tuple-element.15), channel_id=1, source_target_pairs={{0,4},{4,8},{8,12},{12,16},{16,20},{20,24},{24,28},{28,32},{32,36}... | collective-permute-start | bytes 983048 | tf_op jit(solution)/shard_map/ppermute | solution.py:265
  38.0 10.6 %collective-permute-start.9 = (bf16[4,2,1,160,128]{4,3,2,1,0:T(8,128)(2,1)S(1)}, bf16[4,2,1,160,128]{4,3,2,1,0:T(8,128)(2,1)}, u32[]{:S(2)}, u32[]{:S(2)}) collective-permute-start(bf16[4,2,1,160,128]{4,3,2,1,0:T(8,128)(2,1)S(1)} %get-tuple-element.14), channel_id=1, source_target_pairs={{4,0},{8,4},{12,8},{16,12},{20,16},{24,20},{28,24},{32,28},{36,32}... | collective-permute-start | bytes 983048 | tf_op jit(solution)/shard_map/ppermute | solution.py:266
  71.4 3.3 %collective-permute-start.10 = (bf16[8,48,1792]{2,1,0:T(8,128)(2,1)}, bf16[8,48,1792]{2,1,0:T(8,128)(2,1)S(1)}, u32[]{:S(2)}, u32[]{:S(2)}) collective-permute-start(bf16[8,48,1792]{2,1,0:T(8,128)(2,1)} %get-tuple-element.5), channel_id=1, source_target_pairs={{0,4},{4,0},{8,12},{12,8},{16,20},{20,16},{24,28},{28,24},{32,36},... | collective-permute-start | bytes 4128776 | tf_op jit(solution)/shard_map/ppermute | solution.py:270
  75.9 7.8 %collective-permute-start.11 = (bf16[48,1792]{1,0:T(8,128)(2,1)S(1)}, bf16[48,1792]{1,0:T(8,128)(2,1)S(1)}, u32[]{:S(2)}, u32[]{:S(2)}) collective-permute-start(bf16[48,1792]{1,0:T(8,128)(2,1)S(1)} %get-tuple-element.10), channel_id=1, source_target_pairs={{0,32},{4,36},{8,40},{12,44},{16,48},{20,52},{24,56},{28,60},{32,6... | collective-permute-start | bytes 516104 | tf_op jit(solution)/shard_map/ppermute | solution.py:293
  80.1 7.0 %collective-permute-start.15 = (bf16[48,1792]{1,0:T(8,128)(2,1)S(1)}, bf16[48,1792]{1,0:T(8,128)(2,1)S(1)}, u32[]{:S(2)}, u32[]{:S(2)}) collective-permute-start(bf16[48,1792]{1,0:T(8,128)(2,1)S(1)} %get-tuple-element.11), channel_id=1, source_target_pairs={{0,224},{4,228},{8,232},{12,236},{16,240},{20,244},{24,248},{28,25... | collective-permute-start | bytes 516104 | tf_op jit(solution)/shard_map/ppermute | solution.py:294
  84.8 5.0 %collective-permute-start.12 = (bf16[48,1792]{1,0:T(8,128)(2,1)S(1)}, bf16[48,1792]{1,0:T(8,128)(2,1)S(1)}, u32[]{:S(2)}, u32[]{:S(2)}) collective-permute-start(bf16[48,1792]{1,0:T(8,128)(2,1)S(1)} %fusion.4), channel_id=1, source_target_pairs={{0,32},{4,36},{8,40},{12,44},{16,48},{20,52},{24,56},{28,60},{32,6... | collective-permute-start | bytes 516104 | tf_op jit(solution)/shard_map/ppermute | solution.py:296
  91.0 4.6 %collective-permute-start.13 = (bf16[48,1792]{1,0:T(8,128)(2,1)S(1)}, bf16[48,1792]{1,0:T(8,128)(2,1)S(1)}, u32[]{:S(2)}, u32[]{:S(2)}) collective-permute-start(bf16[48,1792]{1,0:T(8,128)(2,1)S(1)} %get-tuple-element.8), channel_id=1, source_target_pairs={{0,32},{4,36},{8,40},{12,44},{16,48},{20,52},{24,56},{28,60},{32,6... | collective-permute-start | bytes 516104 | tf_op jit(solution)/shard_map/ppermute | solution.py:296
  93.2 5.7 %collective-permute-start.16 = (bf16[48,1792]{1,0:T(8,128)(2,1)S(1)}, bf16[48,1792]{1,0:T(8,128)(2,1)S(1)}, u32[]{:S(2)}, u32[]{:S(2)}) collective-permute-start(bf16[48,1792]{1,0:T(8,128)(2,1)S(1)} %get-tuple-element.9), channel_id=1, source_target_pairs={{0,224},{4,228},{8,232},{12,236},{16,240},{20,244},{24,248},{28,25... | collective-permute-start | bytes 516104 | tf_op jit(solution)/shard_map/ppermute | solution.py:298
  100.2 11.7 %collective-permute-start.17 = (bf16[48,1792]{1,0:T(8,128)(2,1)S(1)}, bf16[48,1792]{1,0:T(8,128)(2,1)S(1)}, u32[]{:S(2)}, u32[]{:S(2)}) collective-permute-start(bf16[48,1792]{1,0:T(8,128)(2,1)S(1)} %get-tuple-element.7), channel_id=1, source_target_pairs={{0,224},{4,228},{8,232},{12,236},{16,240},{20,244},{24,248},{28,25... | collective-permute-start | bytes 516104 | tf_op jit(solution)/shard_map/ppermute | solution.py:298
  100.3 11.6 %collective-permute-start.14 = (bf16[48,1792]{1,0:T(8,128)(2,1)S(1)}, bf16[48,1792]{1,0:T(8,128)(2,1)S(1)}, u32[]{:S(2)}, u32[]{:S(2)}) collective-permute-start(bf16[48,1792]{1,0:T(8,128)(2,1)S(1)} %get-tuple-element.6), channel_id=1, source_target_pairs={{0,32},{4,36},{8,40},{12,44},{16,48},{20,52},{24,56},{28,60},{32,6... | collective-permute-start | bytes 516104 | tf_op jit(solution)/shard_map/ppermute | solution.py:296
  103.1 13.0 %collective-permute-start.1 = (bf16[4,160,384]{2,1,0:T(8,128)(2,1)S(1)}, bf16[4,160,384]{2,1,0:T(8,128)(2,1)}, u32[]{:S(2)}, u32[]{:S(2)}) collective-permute-start(bf16[4,160,384]{2,1,0:T(8,128)(2,1)S(1)} %get-tuple-element.13), channel_id=1, source_target_pairs={{0,4},{4,8},{8,12},{12,16},{16,20},{20,24},{24,28},{28,32},{32,36}... | collective-permute-start | bytes 1474568 | tf_op jit(solution)/shard_map/ppermute | solution.py:274
  109.9 14.3 %collective-permute-start.2 = (bf16[4,160,384]{2,1,0:T(8,128)(2,1)S(1)}, bf16[4,160,384]{2,1,0:T(8,128)(2,1)}, u32[]{:S(2)}, u32[]{:S(2)}) collective-permute-start(bf16[4,160,384]{2,1,0:T(8,128)(2,1)S(1)} %get-tuple-element.12), channel_id=1, source_target_pairs={{4,0},{8,4},{12,8},{16,12},{20,16},{24,20},{28,24},{32,28},{36,32}... | collective-permute-start | bytes 1474568 | tf_op jit(solution)/shard_map/ppermute | solution.py:275
  113.1 26.2 %collective-permute-start.20 = (f32[2,6,1792]{2,0,1:T(2,128)S(1)}, f32[2,6,1792]{2,0,1:T(2,128)S(1)}, u32[]{:S(2)}, u32[]{:S(2)}) collective-permute-start(f32[2,6,1792]{2,0,1:T(2,128)S(1)} %bitcast.94), channel_id=1, source_target_pairs={{0,24},{4,28},{8,0},{12,4},{16,8},{20,12},{24,16},{28,20},{32,56},... | collective-permute-start | bytes 258056 | tf_op jit(solution)/shard_map/ppermute | solution.py:306
  113.3 26.1 %collective-permute-start.19 = (f32[2,6,1792]{2,0,1:T(2,128)S(1)}, f32[2,6,1792]{2,0,1:T(2,128)S(1)}, u32[]{:S(2)}, u32[]{:S(2)}) collective-permute-start(f32[2,6,1792]{2,0,1:T(2,128)S(1)} %bitcast.95), channel_id=1, source_target_pairs={{0,16},{4,20},{8,24},{12,28},{16,0},{20,4},{24,8},{28,12},{32,48},... | collective-permute-start | bytes 258056 | tf_op jit(solution)/shard_map/ppermute | solution.py:306
  113.4 26.0 %collective-permute-start.18 = (f32[2,6,1792]{2,0,1:T(2,128)S(1)}, f32[2,6,1792]{2,0,1:T(2,128)S(1)}, u32[]{:S(2)}, u32[]{:S(2)}) collective-permute-start(f32[2,6,1792]{2,0,1:T(2,128)S(1)} %bitcast.96), channel_id=1, source_target_pairs={{0,8},{4,12},{8,16},{12,20},{16,24},{20,28},{24,0},{28,4},{32,40},... | collective-permute-start | bytes 258056 | tf_op jit(solution)/shard_map/ppermute | solution.py:306
  (3 other events, 18.0 us)

commit v2 on v1

v2 whole, which is shorter than its diff:
```python
import math

import jax
import jax.numpy as jnp
from jax import lax
from jax.experimental import pallas as pl
from jax.experimental.pallas import tpu as pltpu
from jax.sharding import PartitionSpec as P

F32, BF16 = jnp.float32, jnp.bfloat16
VMEM_LIMIT = 60 * 1024 * 1024
C, COLS, PART, LANES = 384, 160, 96, 128
ZS, XS, YS = 8, 4, 4
NT = (((1,), (1,)), ((), ()))


def rows_perm(move):
    pairs = []
    for z in range(ZS):
        for x in range(XS):
            for c in range(2):
                z2, x2, c2 = move(z, x, c)
                pairs.append(((z * XS + x) * 2 + c, (z2 * XS + x2) * 2 + c2))
    return pairs


def z_shift(steps):
    return rows_perm(lambda z, x, c: ((z + steps) % ZS, x, c))


def x_shift(steps):
    return rows_perm(lambda z, x, c: (z, (x + steps) % XS, c))


def core_swap():
    return rows_perm(lambda z, x, c: (z, x, 1 - c))


def y_shift(steps):
    return [(i, (i + steps) % YS) for i in range(YS)]


def line(count, steps):
    return [(i, i + steps) for i in range(count) if 0 <= i + steps < count]


def activation_kernel(y_ref, features_ref, gamma_ref, *out_refs):
    floats = features_ref[...].astype(F32)
    inverse = lax.rsqrt(jnp.mean(floats * floats, axis=-1, keepdims=True) + 1e-6)
    pre_act = floats * inverse * gamma_ref[...][None, :]
    active = pre_act * jax.nn.sigmoid(pre_act)
    blank = jnp.zeros((active.shape[0], LANES - PART), F32)
    for part in range(YS):
        piece = active[:, part * PART : (part + 1) * PART]
        piece = jnp.concatenate([piece, blank], axis=1).astype(BF16)
        place = lax.rem(part - y_ref[0] + YS, YS)
        for k in range(YS):

            @pl.when(place == k)
            def _():
                out_refs[k][...] = piece


def activations(y, features, gamma):
    pixels = features.shape[0]
    return pl.pallas_call(
        activation_kernel,
        in_specs=[pl.BlockSpec(memory_space=pltpu.SMEM)] + [pl.BlockSpec(memory_space=pltpu.VMEM)] * 2,
        out_shape=[jax.ShapeDtypeStruct((pixels, LANES), BF16)] * YS,
        compiler_params=pltpu.CompilerParams(vmem_limit_bytes=VMEM_LIMIT),
    )(y, features, gamma)


def weight_kernel(y_ref, c3, c2a, c2b, c1, c0, a0, a1, a2, a3, up, dn, order_ref, own, send, spread, cot):
    y = y_ref[0]
    acts = (a0, a1, a2, a3)
    column = lax.broadcasted_iota(jnp.int32, (4 * COLS, LANES), 0) % COLS
    for k in range(4):
        for f in range(2):
            value = jnp.concatenate(
                [up[k, f, 0], acts[k][f, 0], acts[k][f, 1], dn[k, f, 0]], axis=0
            )
            floats = value.astype(F32)
            left = jnp.where(column == 0, 0.0, pltpu.roll(floats, 1, 0)).astype(BF16)
            right = jnp.where(column == COLS - 1, 0.0, pltpu.roll(floats, 4 * COLS - 1, 0)).astype(BF16)
            places = [(4 - k) * 2 + f] + ([f] if k == 0 else [])
            for place in places:
                rows = slice(place * 320, place * 320 + 320)
                for b in range(3):
                    for e, part in enumerate((left, value, right)):
                        at = (b * 3 + e) * LANES
                        spread[rows, at : at + LANES] = part[b * COLS : (b + 2) * COLS]
    order = order_ref[...]
    for k, pieces in enumerate(((c0,), (c1,), (c2a, c2b), (c3,))):
        first = lax.rem(y - k + 4, 4) == 0
        at = (3 - k) * 640
        for piece in pieces:
            size = piece.shape[0]
            block = lax.dot_general(order, piece[...], NT, preferred_element_type=F32).astype(BF16)
            blank = jnp.zeros_like(block)
            cot[2, :, at : at + size] = block
            cot[0, :, at : at + size] = jnp.where(first, blank, block)
            at += size
        at = (3 - k) * 640
        frame = lax.broadcasted_iota(jnp.int32, (C, 640), 1)
        block = cot[2, :, at : at + 640]
        cot[1, :, at : at + 640] = jnp.where(first & (frame < 320), jnp.zeros_like(block), block)
    pieces = []
    for a in range(3):
        value = jnp.dot(
            cot[a], spread[a * 320 : a * 320 + 2560, :], preferred_element_type=F32
        )
        pieces += [value[:, s * LANES : s * LANES + PART] for s in range(9)]
    packed = jnp.concatenate(pieces, axis=1)
    own[...] = packed[: C // 2]
    send[...] = packed[C // 2 :].astype(BF16)


def weight_partials(y, cots, acts, up, dn, order):
    shape = (C // 2, 27 * PART)
    return pl.pallas_call(
        weight_kernel,
        in_specs=[pl.BlockSpec(memory_space=pltpu.SMEM)] + [pl.BlockSpec(memory_space=pltpu.VMEM)] * 12,
        out_specs=[pl.BlockSpec(memory_space=pltpu.VMEM)] * 2,
        out_shape=[jax.ShapeDtypeStruct(shape, F32), jax.ShapeDtypeStruct(shape, BF16)],
        scratch_shapes=[
            pltpu.VMEM((10 * 320, 9 * LANES), BF16),
            pltpu.VMEM((3, C, 2560), BF16),
        ],
        compiler_params=pltpu.CompilerParams(vmem_limit_bytes=VMEM_LIMIT),
        cost_estimate=pl.CostEstimate(flops=14 * 2 * 384 * 2560 * 256, bytes_accessed=8_000_000, transcendentals=0),
    )(y, *cots, *acts, up, dn, order)


def input_kernel(y_ref, own, following, up, dn, taps_ref, features_ref, gamma_ref, out_ref, ext, side):
    a = pl.program_id(0)

    @pl.when(a == 0)
    def _():
        keep = y_ref[0] != 3
        for f in range(2):
            ext[f, COLS : 3 * COLS] = own[f]
            ext[f + 2, COLS : 3 * COLS] = jnp.where(keep, following[f], jnp.zeros_like(following[f]))
        for f in range(4):
            good = keep if f >= 2 else True
            ext[f, :COLS] = jnp.where(good, up[f], jnp.zeros_like(up[f]))
            ext[f, 3 * COLS :] = jnp.where(good, dn[f], jnp.zeros_like(dn[f]))

    rows = []
    for f in range(2):
        pieces = [ext[f + 2 - a, (2 - b) * COLS : (4 - b) * COLS] for b in range(3)]
        rows.append(jnp.concatenate(pieces, axis=1))
    weights = jnp.concatenate(
        [jnp.concatenate([taps_ref[0, b, e] for b in range(3)], axis=1) for e in range(3)], axis=0
    )
    value = lax.dot_general(jnp.concatenate(rows, axis=0), weights, NT, preferred_element_type=F32)

    @pl.when(a == 0)
    def _():
        side[...] = value

    @pl.when(a == 1)
    def _():
        side[...] += value

    @pl.when(a == 2)
    def _():
        column = lax.broadcasted_iota(jnp.int32, (4 * COLS, C), 0) % COLS
        side[...] += value
        grad_act = side[:, C : 2 * C]
        grad_act += jnp.where(column == COLS - 1, 0.0, pltpu.roll(side[:, :C], 4 * COLS - 1, 0))
        grad_act += jnp.where(column == 0, 0.0, pltpu.roll(side[:, 2 * C :], 1, 0))
        gamma = gamma_ref[...][None, :]
        floats = features_ref[...].astype(F32)
        inverse = lax.rsqrt(jnp.mean(floats * floats, axis=-1, keepdims=True) + 1e-6)
        normed = floats * inverse
        pre_act = normed * gamma
        sigma = jax.nn.sigmoid(pre_act)
        grad_norm = grad_act * sigma * (1.0 + pre_act * (1.0 - sigma)) * gamma
        inner = jnp.mean(grad_norm * normed, axis=-1, keepdims=True)
        out_ref[...] = (inverse * (grad_norm - normed * inner)).astype(BF16)


def input_gradient(y, own, following, up, dn, taps, features, gamma):
    pixels = features.shape[0]
    whole = lambda shape: pl.BlockSpec(shape, lambda a: (0,) * len(shape))
    return pl.pallas_call(
        input_kernel,
        grid=(3,),
        in_specs=[
            pl.BlockSpec(memory_space=pltpu.SMEM),
            whole((2, 2 * COLS, C)),
            whole((2, 2 * COLS, C)),
            whole((4, COLS, C)),
            whole((4, COLS, C)),
            pl.BlockSpec((1, 3, 3, C, C), lambda a: (a, 0, 0, 0, 0)),
            whole((pixels, C)),
            whole((C,)),
        ],
        out_specs=whole((pixels, C)),
        out_shape=jax.ShapeDtypeStruct((pixels, C), BF16),
        scratch_shapes=[
            pltpu.VMEM((4, 4 * COLS, C), BF16),
            pltpu.VMEM((pixels, 3 * C), F32),
        ],
        compiler_params=pltpu.CompilerParams(vmem_limit_bytes=VMEM_LIMIT),
        cost_estimate=pl.CostEstimate(flops=27 * 2 * 640 * C * C, bytes_accessed=12_000_000, transcendentals=0),
    )(y, own, following, up, dn, taps, features, gamma)


def output_order(z, x, core):
    row = jnp.arange(C)
    c2, x2, z2, j = row // 192, row // 48 % XS, row // 6 % ZS, row % 6
    bits = z2 // 4 ^ z2 // 2 % 2 * 2 ^ z2 % 2 * 6
    channel = (z ^ bits) * 48 + (x + x2) % XS * 12 + (core + c2) % 2 * 6 + j
    return (channel[:, None] == jnp.arange(C)[None, :]).astype(BF16)


def body(features, cotangent, gamma, kernel):
    frames, height, columns, width = features.shape
    pixels = frames * height * columns
    y, r = lax.axis_index("tm"), lax.axis_index("rows")
    z, x, core = r // (2 * XS), (r // 2) % XS, r % 2
    block = y.reshape(1).astype(jnp.int32)
    order = output_order(z, x, core)
    flat = features.reshape(pixels, width)
    taps = jnp.transpose(kernel, (1, 0, 2)).reshape(3, 3, 3, width, width)

    following = lax.ppermute(cotangent, "tm", y_shift(3))
    previous = lax.ppermute(cotangent, "tm", y_shift(1))
    active = activations(block, flat, gamma)
    acts = [active[0]] + [lax.ppermute(active[k], "tm", y_shift(k)) for k in (1, 2, 3)]
    acts = [value.reshape(2, 2, columns, LANES) for value in acts]
    far = [
        lax.ppermute(previous[0], "tm", y_shift(1)).reshape(pixels // 2, width),
        lax.ppermute(following[1], "tm", y_shift(3)).reshape(pixels // 2, width),
    ]
    stacked = jnp.stack(acts)
    act_up = lax.ppermute(stacked[:, :, 1:], "rows", line(64, 1))
    act_dn = lax.ppermute(stacked[:, :, :1], "rows", line(64, -1))
    cots = [following.reshape(pixels, width), *far, previous.reshape(pixels, width), cotangent.reshape(pixels, width)]
    own, send = weight_partials(block, cots, acts, act_up, act_dn, order)
    other = lax.ppermute(send, "rows", core_swap())

    def part(k):
        rows = slice(48 * k, 48 * k + 48)
        return own[rows] + other[rows].astype(F32)

    kept = part(0)
    parts = [part(k).astype(BF16) for k in (2, 1, 3)]
    block, *parts = lax.optimization_barrier((block, *parts))
    received = [lax.ppermute(value, "rows", x_shift(k)) for value, k in zip(parts, (2, 1, 3))]

    ext = jnp.concatenate([cotangent, following], axis=0)
    cot_up = lax.ppermute(ext[:, 1], "rows", line(64, 1))
    cot_dn = lax.ppermute(ext[:, 0], "rows", line(64, -1))
    input_grad = input_gradient(
        block,
        cotangent.reshape(2, 2 * columns, width),
        following.reshape(2, 2 * columns, width),
        cot_up,
        cot_dn,
        taps,
        flat,
        gamma,
    )

    input_grad, *received = lax.optimization_barrier((input_grad, *received))
    total = kept
    for value in received:
        total = total + value.astype(F32)
    for bits, wire in ((1, BF16), (2, F32), (6, F32)):
        half = total.shape[0] // 2
        pairs = rows_perm(lambda z, x, c: (z ^ bits, x, c))
        total = total[:half] + lax.ppermute(total[half:].astype(wire), "rows", pairs).astype(F32)
    mine = total.reshape(6, 27, PART)
    count = pixels * lax.axis_size("tm") * lax.axis_size("rows")
    weight_grad = jnp.transpose(mine, (2, 1, 0)) * (1.0 / math.sqrt(count))
    return input_grad.reshape(features.shape), weight_grad


def solution(mesh):
    placed = (P("tm", "rows", None, None), P("tm", "rows", None, None), P(), P())
    return jax.shard_map(
        body,
        mesh=mesh,
        in_specs=placed,
        out_specs=(P("tm", "rows", None, None), P("tm", None, "rows")),
        check_vma=False,
    )
```

time: 141 us -> 112 us (0.79)
  the two profiles are of different devices: /device:TPU:79 before, /device:TPU:56 now
where the time goes in v2:
time: 112 us
  waiting for transfers between devices  37.1 us (33%)
  starting transfers between devices  36.3 us (32%)
  Pallas kernels  29 us (26%)
  local copies, waits for them, and re-layouts  5.5 us (5%)
  other arithmetic  3.41 us (3%)
    pallas_call x1, Pallas kernels, weight_partials(): pl.pallas_call(weight_kernel, in_specs=[pl.BlockSpec(memory_space=pltpu.S...  14.4 us
    ppermute x3, waiting for transfers between devices, body(): lax.ppermute(total[half:].astype(wire), 'rows', pairs).astype(F32)  13.3 us
    pallas_call x1, Pallas kernels, input_gradient(): pl.pallas_call(input_kernel, grid=(3,), in_specs=[pl.BlockSpec(memory_spa...  11.9 us
    ppermute x3, starting transfers between devices, body(): lax.ppermute(total[half:].astype(wire), 'rows', pairs).astype(F32)  9.99 us
    ppermute x3, waiting for transfers between devices, body(): lax.ppermute(active[k], 'tm', y_shift(k))  8.7 us
    ppermute x1, waiting for transfers between devices, body(): cot_up = lax.ppermute(ext[:, 1], 'rows', line(64, 1))  7.39 us
    ppermute x1, starting transfers between devices, body(): lax.ppermute(previous[0], 'tm', y_shift(1)).reshape(pixels // 2, width)  5.42 us
    ppermute x3, starting transfers between devices, body(): lax.ppermute(value, 'rows', x_shift(k))  4.98 us
  transfers between devices with their start and end apart: 18, of which 8 were waited for; matrix products, arithmetic and copies ran while one was open for 4% of the time, Pallas kernels for 13%

profile of v2, /device:TPU:56, one launch (start us, length us, event | category | flops | bytes accessed | tf_op | source)
XLA Modules:
  0.0 112.1 jit_solution(4617365468442678230)
XLA Ops:
  0.9 2.6 %shard_map.59 = (bf16[640,128]{1,0:T(8,128)(2,1)}, bf16[640,128]{1,0:T(8,128)(2,1)}, bf16[640,128]{1,0:T(8,128)(2,1)}, bf16[640,128]{1,0:T(8,128)(2,1)}) custom-call(s32[1]{0:T(128)} %bitcast.y_ref, bf16[640,384]{1,0:T(8,128)(2,1)} %bitcast.32, f32[384]{0:T(512)} %gamma_ref.3), custom_call_target="tpu_custom_call" | custom-call | tf_op jit(solution)/shard_map/pallas_call | solution.py:66
  3.6 1.6 %collective-permute-start.4 = (bf16[640,128]{1,0:T(8,128)(2,1)}, bf16[640,128]{1,0:T(8,128)(2,1)S(1)}, u32[]{:S(2)}, u32[]{:S(2)}) collective-permute-start(bf16[640,128]{1,0:T(8,128)(2,1)} %get-tuple-element.17), channel_id=1, source_target_pairs={{0,1},{1,2},{2,3},{3,0},{4,5},{5,6},{6,7},{7,4},{8,9},{9,10},{10,1... | collective-permute-start | bytes 491528 | tf_op jit(solution)/shard_map/ppermute | solution.py:232
  5.2 2.3 %collective-permute-start.5 = (bf16[640,128]{1,0:T(8,128)(2,1)}, bf16[640,128]{1,0:T(8,128)(2,1)S(1)}, u32[]{:S(2)}, u32[]{:S(2)}) collective-permute-start(bf16[640,128]{1,0:T(8,128)(2,1)} %get-tuple-element.18), channel_id=1, source_target_pairs={{0,2},{1,3},{2,0},{3,1},{4,6},{5,7},{6,4},{7,5},{8,10},{9,11},{10,... | collective-permute-start | bytes 491528 | tf_op jit(solution)/shard_map/ppermute | solution.py:232
  8.7 1.1 %collective-permute-start = (bf16[2,2,160,384]{3,2,0,1:T(8,128)(2,1)S(1)}, bf16[2,2,160,384]{3,2,0,1:T(8,128)(2,1)S(1)}, u32[]{:S(2)}, u32[]{:S(2)}) collective-permute-start(bf16[2,2,160,384]{3,2,0,1:T(8,128)(2,1)S(1)} %get-tuple-element.38), channel_id=1, source_target_pairs={{0,3},{1,0},{2,1},{3,2},{4,7},{5,4},{6,5},{7,6},{8,11},{9,8},{10,9... | collective-permute-start | bytes 1474568 | tf_op jit(solution)/shard_map/ppermute | solution.py:229
  9.8 8.7 %collective-permute-done.4 = bf16[640,128]{1,0:T(8,128)(2,1)S(1)} collective-permute-done((bf16[640,128]{1,0:T(8,128)(2,1)}, bf16[640,128]{1,0:T(8,128)(2,1)S(1)}, u32[]{:S(2)}, u32[]{:S(2)}) %collective-permute-start.4) | collective-permute-done | bytes 163872 | tf_op jit(solution)/shard_map/ppermute | solution.py:232
  18.6 1.2 %pad_maximum_fusion = bf16[4,2,2,160,128]{4,3,2,1,0:T(8,128)(2,1)S(1)} fusion(bf16[1,2,2,160,128]{4,3,2,1,0:T(8,128)(2,1)S(1)} %bitcast.42, bf16[1,2,2,160,128]{4,3,2,1,0:T(8,128)(2,1)S(1)} %bitcast.40, bf16[1,2,2,160,128]{4,3,2,1,0:T(8,128)(2,1)S(1)} %bitcast.38, bf16[1,2,2,160,128]{4,3,2,1,0:T(8,128)(2,1)} %bitcast.36), kind=kLoop, calls=%fused_computation | loop fusion | flops 983040 | bytes 1310720 | tf_op jit(solution)/shard_map/stack | solution.py:238
  19.8 1.9 %collective-permute-start.8 = (bf16[4,2,1,160,128]{4,3,2,1,0:T(8,128)(2,1)S(1)}, bf16[4,2,1,160,128]{4,3,2,1,0:T(8,128)(2,1)S(1)}, u32[]{:S(2)}, u32[]{:S(2)}) collective-permute-start(bf16[4,2,1,160,128]{4,3,2,1,0:T(8,128)(2,1)S(1)} %get-tuple-element.35), channel_id=1, source_target_pairs={{4,0},{8,4},{12,8},{16,12},{20,16},{24,20},{28,24},{32,28},{36,32}... | collective-permute-start | bytes 983048 | tf_op jit(solution)/shard_map/ppermute | solution.py:240
  21.7 2.4 %collective-permute-start.7 = (bf16[4,2,1,160,128]{4,3,2,1,0:T(8,128)(2,1)S(1)}, bf16[4,2,1,160,128]{4,3,2,1,0:T(8,128)(2,1)S(1)}, u32[]{:S(2)}, u32[]{:S(2)}) collective-permute-start(bf16[4,2,1,160,128]{4,3,2,1,0:T(8,128)(2,1)S(1)} %get-tuple-element.36), channel_id=1, source_target_pairs={{0,4},{4,8},{8,12},{12,16},{16,20},{20,24},{24,28},{28,32},{32,36}... | collective-permute-start | bytes 983048 | tf_op jit(solution)/shard_map/ppermute | solution.py:239
  24.2 5.4 %collective-permute-start.2 = (bf16[2,160,384]{2,1,0:T(8,128)(2,1)S(1)}, bf16[2,160,384]{2,1,0:T(8,128)(2,1)S(1)}, u32[]{:S(2)}, u32[]{:S(2)}) collective-permute-start(bf16[2,160,384]{2,1,0:T(8,128)(2,1)S(1)} %slice_bitcast_fusion.3), channel_id=1, source_target_pairs={{0,1},{1,2},{2,3},{3,0},{4,5},{5,6},{6,7},{7,4},{8,9},{9,10},{10,1... | collective-permute-start | bytes 737288 | tf_op jit(solution)/shard_map/ppermute | solution.py:235
  32.2 3.5 %collective-permute-done.2 = bf16[2,160,384]{2,1,0:T(8,128)(2,1)S(1)} collective-permute-done((bf16[2,160,384]{2,1,0:T(8,128)(2,1)S(1)}, bf16[2,160,384]{2,1,0:T(8,128)(2,1)S(1)}, u32[]{:S(2)}, u32[]{:S(2)}) %collective-permute-start.2) | collective-permute-done | bytes 245792 | tf_op jit(solution)/shard_map/ppermute | solution.py:235
  35.7 3.7 %collective-permute-done.3 = bf16[2,160,384]{2,1,0:T(8,128)(2,1)S(1)} collective-permute-done((bf16[2,160,384]{2,1,0:T(8,128)(2,1)S(1)}, bf16[2,160,384]{2,1,0:T(8,128)(2,1)S(1)}, u32[]{:S(2)}, u32[]{:S(2)}) %collective-permute-start.3) | collective-permute-done | bytes 245792 | tf_op jit(solution)/shard_map/ppermute | solution.py:236
  40.1 14.4 %shard_map.60 = (f32[192,2592]{1,0:T(8,128)}, bf16[192,2592]{1,0:T(8,128)(2,1)}) custom-call(s32[1]{0:T(128)} %bitcast.y_ref, bf16[640,384]{1,0:T(8,128)(2,1)} %bitcast.34, bf16[320,384]{1,0:T(8,128)(2,1)} %bitcast.47, bf16[320,384]{1,0:T(8,128)(2,1)} %bitcast.48, bf16[640,384]{1,0:T(8,128)(2,1)} %bitcast.44, bf16[640,384]{1,0:T(8,128)(2,1)} %bitcast.30, ...), custom_call_target="tpu_custom_call" | custom-call | flops 7046430720 | bytes 8000000 | tf_op jit(solution)/shard_map/pallas_call | solution.py:121
  54.7 3.9 %collective-permute-start.11 = (bf16[4,160,384]{2,1,0:T(8,128)(2,1)S(1)}, bf16[4,160,384]{2,1,0:T(8,128)(2,1)S(1)}, u32[]{:S(2)}, u32[]{:S(2)}) collective-permute-start(bf16[4,160,384]{2,1,0:T(8,128)(2,1)S(1)} %get-tuple-element.33), channel_id=1, source_target_pairs={{4,0},{8,4},{12,8},{16,12},{20,16},{24,20},{28,24},{32,28},{36,32}... | collective-permute-start | bytes 1474568 | tf_op jit(solution)/shard_map/ppermute | solution.py:256
  58.6 1.9 %collective-permute-start.10 = (bf16[4,160,384]{2,1,0:T(8,128)(2,1)S(1)}, bf16[4,160,384]{2,1,0:T(8,128)(2,1)S(1)}, u32[]{:S(2)}, u32[]{:S(2)}) collective-permute-start(bf16[4,160,384]{2,1,0:T(8,128)(2,1)S(1)} %get-tuple-element.34), channel_id=1, source_target_pairs={{0,4},{4,8},{8,12},{12,16},{16,20},{20,24},{24,28},{28,32},{32,36}... | collective-permute-start | bytes 1474568 | tf_op jit(solution)/shard_map/ppermute | solution.py:255
  61.7 1.7 %collective-permute-start.12 = (bf16[48,2592]{1,0:T(8,128)(2,1)S(1)}, bf16[48,2592]{1,0:T(8,128)(2,1)S(1)}, u32[]{:S(2)}, u32[]{:S(2)}) collective-permute-start(bf16[48,2592]{1,0:T(8,128)(2,1)S(1)} %get-tuple-element.23), channel_id=1, source_target_pairs={{0,16},{4,20},{8,24},{12,28},{16,0},{20,4},{24,8},{28,12},{32,48},... | collective-permute-start | bytes 746504 | tf_op jit(solution)/shard_map/ppermute | solution.py:252
  64.1 2.6 %collective-permute-start.14 = (bf16[48,2592]{1,0:T(8,128)(2,1)S(1)}, bf16[48,2592]{1,0:T(8,128)(2,1)S(1)}, u32[]{:S(2)}, u32[]{:S(2)}) collective-permute-start(bf16[48,2592]{1,0:T(8,128)(2,1)S(1)} %get-tuple-element.25), channel_id=1, source_target_pairs={{0,24},{4,28},{8,0},{12,4},{16,8},{20,12},{24,16},{28,20},{32,56},... | collective-permute-start | bytes 746504 | tf_op jit(solution)/shard_map/ppermute | solution.py:252
  66.7 7.4 %collective-permute-done.10.up = bf16[4,160,384]{2,1,0:T(8,128)(2,1)S(1)} collective-permute-done((bf16[4,160,384]{2,1,0:T(8,128)(2,1)S(1)}, bf16[4,160,384]{2,1,0:T(8,128)(2,1)S(1)}, u32[]{:S(2)}, u32[]{:S(2)}) %collective-permute-start.10) | collective-permute-done | bytes 491552 | tf_op jit(solution)/shard_map/ppermute | solution.py:255
  74.9 11.9 %shard_map.61 = bf16[640,384]{1,0:T(8,128)(2,1)} custom-call(s32[1]{0:T(128)} %bitcast.y_ref, bf16[2,320,384]{2,1,0:T(8,128)(2,1)} %bitcast.31, bf16[2,320,384]{2,1,0:T(8,128)(2,1)} %bitcast.35, bf16[4,160,384]{2,1,0:T(8,128)(2,1)} %copy-done.7, bf16[4,160,384]{2,1,0:T(8,128)(2,1)} %copy-done.6, bf16[3,3,3,384,384]{4,3,2,1,0:T(8,128)(2,1)} %bitcast.46, ...), custom_call_target="tpu_custom_call" | custom-call | flops 5096079360 | bytes 12000000 | tf_op jit(solution)/shard_map/pallas_call | solution.py:187
  86.8 1.1 convert_add_fusion
  88.1 6.3 %collective-permute-done.15 = bf16[24,2592]{1,0:T(8,128)(2,1)S(1)} collective-permute-done((bf16[24,2592]{1,0:T(8,128)(2,1)S(1)}, bf16[24,2592]{1,0:T(8,128)(2,1)S(1)}, u32[]{:S(2)}, u32[]{:S(2)}) %collective-permute-start.15) | collective-permute-done | bytes 124448 | tf_op jit(solution)/shard_map/ppermute | solution.py:275
  94.4 3.4 %collective-permute-start.16 = (f32[12,2592]{1,0:T(8,128)S(1)}, f32[12,2592]{1,0:T(8,128)S(1)}, u32[]{:S(2)}, u32[]{:S(2)}) collective-permute-start(f32[12,2592]{1,0:T(8,128)S(1)} %slice.94), channel_id=1, source_target_pairs={{0,64},{4,68},{8,72},{12,76},{16,80},{20,84},{24,88},{28,92},{32,9... | collective-permute-start | bytes 373256 | tf_op jit(solution)/shard_map/ppermute | solution.py:275
  97.8 3.8 %collective-permute-done.16 = f32[12,2592]{1,0:T(8,128)S(1)} collective-permute-done((f32[12,2592]{1,0:T(8,128)S(1)}, f32[12,2592]{1,0:T(8,128)S(1)}, u32[]{:S(2)}, u32[]{:S(2)}) %collective-permute-start.16) | collective-permute-done | bytes 124448 | tf_op jit(solution)/shard_map/ppermute | solution.py:275
  101.6 6.5 %collective-permute-start.17 = (f32[6,2592]{1,0:T(8,128)S(1)}, f32[6,2592]{1,0:T(8,128)S(1)}, u32[]{:S(2)}, u32[]{:S(2)}) collective-permute-start(f32[6,2592]{1,0:T(8,128)S(1)} %slice.96), channel_id=1, source_target_pairs={{0,192},{4,196},{8,200},{12,204},{16,208},{20,212},{24,216},{28,22... | collective-permute-start | bytes 186632 | tf_op jit(solution)/shard_map/ppermute | solution.py:275
  108.2 3.2 %collective-permute-done.17 = f32[6,2592]{1,0:T(8,128)S(1)} collective-permute-done((f32[6,2592]{1,0:T(8,128)S(1)}, f32[6,2592]{1,0:T(8,128)S(1)}, u32[]{:S(2)}, u32[]{:S(2)}) %collective-permute-start.17) | collective-permute-done | bytes 62240 | tf_op jit(solution)/shard_map/ppermute | solution.py:275
  (58 shorter events, 8.6 us)
Async XLA Ops:
  0.6 23.5 %collective-permute-start.1 = (bf16[2,2,160,384]{3,2,1,0:T(8,128)(2,1)}, bf16[2,2,160,384]{3,2,1,0:T(8,128)(2,1)S(1)}, u32[]{:S(2)}, u32[]{:S(2)}) collective-permute-start(bf16[2,2,160,384]{3,2,1,0:T(8,128)(2,1)} %param.5), channel_id=1, source_target_pairs={{0,1},{1,2},{2,3},{3,0},{4,5},{5,6},{6,7},{7,4},{8,9},{9,10},{10,1... | collective-permute-start | bytes 1474568 | tf_op jit(solution)/shard_map/ppermute | solution.py:230
  3.6 15.0 %collective-permute-start.4 = (bf16[640,128]{1,0:T(8,128)(2,1)}, bf16[640,128]{1,0:T(8,128)(2,1)S(1)}, u32[]{:S(2)}, u32[]{:S(2)}) collective-permute-start(bf16[640,128]{1,0:T(8,128)(2,1)} %get-tuple-element.17), channel_id=1, source_target_pairs={{0,1},{1,2},{2,3},{3,0},{4,5},{5,6},{6,7},{7,4},{8,9},{9,10},{10,1... | collective-permute-start | bytes 491528 | tf_op jit(solution)/shard_map/ppermute | solution.py:232
  5.2 13.4 %collective-permute-start.5 = (bf16[640,128]{1,0:T(8,128)(2,1)}, bf16[640,128]{1,0:T(8,128)(2,1)S(1)}, u32[]{:S(2)}, u32[]{:S(2)}) collective-permute-start(bf16[640,128]{1,0:T(8,128)(2,1)} %get-tuple-element.18), channel_id=1, source_target_pairs={{0,2},{1,3},{2,0},{3,1},{4,6},{5,7},{6,4},{7,5},{8,10},{9,11},{10,... | collective-permute-start | bytes 491528 | tf_op jit(solution)/shard_map/ppermute | solution.py:232
  7.4 11.1 %collective-permute-start.6 = (bf16[640,128]{1,0:T(8,128)(2,1)}, bf16[640,128]{1,0:T(8,128)(2,1)S(1)}, u32[]{:S(2)}, u32[]{:S(2)}) collective-permute-start(bf16[640,128]{1,0:T(8,128)(2,1)} %get-tuple-element.19), channel_id=1, source_target_pairs={{0,3},{1,0},{2,1},{3,2},{4,7},{5,4},{6,5},{7,6},{8,11},{9,8},{10,9... | collective-permute-start | bytes 491528 | tf_op jit(solution)/shard_map/ppermute | solution.py:232
  8.7 20.9 %collective-permute-start = (bf16[2,2,160,384]{3,2,0,1:T(8,128)(2,1)S(1)}, bf16[2,2,160,384]{3,2,0,1:T(8,128)(2,1)S(1)}, u32[]{:S(2)}, u32[]{:S(2)}) collective-permute-start(bf16[2,2,160,384]{3,2,0,1:T(8,128)(2,1)S(1)} %get-tuple-element.38), channel_id=1, source_target_pairs={{0,3},{1,0},{2,1},{3,2},{4,7},{5,4},{6,5},{7,6},{8,11},{9,8},{10,9... | collective-permute-start | bytes 1474568 | tf_op jit(solution)/shard_map/ppermute | solution.py:229
  18.5 13.1 %copy-start.2 = (bf16[640,128]{1,0:T(8,128)(2,1)}, bf16[640,128]{1,0:T(8,128)(2,1)S(1)}, u32[]{:S(2)}) copy-start(bf16[640,128]{1,0:T(8,128)(2,1)S(1)} %collective-permute-done.4) | copy-start | bytes 491524
  18.5 13.1 %copy-start.3 = (bf16[640,128]{1,0:T(8,128)(2,1)}, bf16[640,128]{1,0:T(8,128)(2,1)S(1)}, u32[]{:S(2)}) copy-start(bf16[640,128]{1,0:T(8,128)(2,1)S(1)} %collective-permute-done.5) | copy-start | bytes 491524
  18.5 13.1 %copy-start.4 = (bf16[640,128]{1,0:T(8,128)(2,1)}, bf16[640,128]{1,0:T(8,128)(2,1)S(1)}, u32[]{:S(2)}) copy-start(bf16[640,128]{1,0:T(8,128)(2,1)S(1)} %collective-permute-done.6) | copy-start | bytes 491524
  19.8 11.9 %collective-permute-start.8 = (bf16[4,2,1,160,128]{4,3,2,1,0:T(8,128)(2,1)S(1)}, bf16[4,2,1,160,128]{4,3,2,1,0:T(8,128)(2,1)S(1)}, u32[]{:S(2)}, u32[]{:S(2)}) collective-permute-start(bf16[4,2,1,160,128]{4,3,2,1,0:T(8,128)(2,1)S(1)} %get-tuple-element.35), channel_id=1, source_target_pairs={{4,0},{8,4},{12,8},{16,12},{20,16},{24,20},{28,24},{32,28},{36,32}... | collective-permute-start | bytes 983048 | tf_op jit(solution)/shard_map/ppermute | solution.py:240
  21.7 10.5 %collective-permute-start.7 = (bf16[4,2,1,160,128]{4,3,2,1,0:T(8,128)(2,1)S(1)}, bf16[4,2,1,160,128]{4,3,2,1,0:T(8,128)(2,1)S(1)}, u32[]{:S(2)}, u32[]{:S(2)}) collective-permute-start(bf16[4,2,1,160,128]{4,3,2,1,0:T(8,128)(2,1)S(1)} %get-tuple-element.36), channel_id=1, source_target_pairs={{0,4},{4,8},{8,12},{12,16},{16,20},{20,24},{24,28},{28,32},{32,36}... | collective-permute-start | bytes 983048 | tf_op jit(solution)/shard_map/ppermute | solution.py:239
  24.1 15.3 %copy-start.5 = (bf16[2,2,160,384]{3,2,1,0:T(8,128)(2,1)}, bf16[2,2,160,384]{3,2,1,0:T(8,128)(2,1)S(1)}, u32[]{:S(2)}) copy-start(bf16[2,2,160,384]{3,2,1,0:T(8,128)(2,1)S(1)} %collective-permute-done.1) | copy-start | bytes 1474564
  24.2 11.5 %collective-permute-start.2 = (bf16[2,160,384]{2,1,0:T(8,128)(2,1)S(1)}, bf16[2,160,384]{2,1,0:T(8,128)(2,1)S(1)}, u32[]{:S(2)}, u32[]{:S(2)}) collective-permute-start(bf16[2,160,384]{2,1,0:T(8,128)(2,1)S(1)} %slice_bitcast_fusion.3), channel_id=1, source_target_pairs={{0,1},{1,2},{2,3},{3,0},{4,5},{5,6},{6,7},{7,4},{8,9},{9,10},{10,1... | collective-permute-start | bytes 737288 | tf_op jit(solution)/shard_map/ppermute | solution.py:235
  29.6 9.8 %collective-permute-start.3 = (bf16[2,160,384]{2,1,0:T(8,128)(2,1)S(1)}, bf16[2,160,384]{2,1,0:T(8,128)(2,1)S(1)}, u32[]{:S(2)}, u32[]{:S(2)}) collective-permute-start(bf16[2,160,384]{2,1,0:T(8,128)(2,1)S(1)} %slice_bitcast_fusion.2), channel_id=1, source_target_pairs={{0,3},{1,0},{2,1},{3,2},{4,7},{5,4},{6,5},{7,6},{8,11},{9,8},{10,9... | collective-permute-start | bytes 737288 | tf_op jit(solution)/shard_map/ppermute | solution.py:236
  31.7 7.8 %copy-start.8 = (bf16[4,2,1,160,128]{4,3,2,1,0:T(8,128)(2,1)}, bf16[4,2,1,160,128]{4,3,2,1,0:T(8,128)(2,1)S(1)}, u32[]{:S(2)}) copy-start(bf16[4,2,1,160,128]{4,3,2,1,0:T(8,128)(2,1)S(1)} %collective-permute-done.8.dn) | copy-start | bytes 983044
  54.5 6.1 %collective-permute-start.9 = (bf16[192,2592]{1,0:T(8,128)(2,1)}, bf16[192,2592]{1,0:T(8,128)(2,1)S(1)}, u32[]{:S(2)}, u32[]{:S(2)}) collective-permute-start(bf16[192,2592]{1,0:T(8,128)(2,1)} %get-tuple-element.21), channel_id=1, source_target_pairs={{0,4},{4,0},{8,12},{12,8},{16,20},{20,16},{24,28},{28,24},{32,36},... | collective-permute-start | bytes 2985992 | tf_op jit(solution)/shard_map/ppermute | solution.py:243
  54.7 12.0 %collective-permute-start.11 = (bf16[4,160,384]{2,1,0:T(8,128)(2,1)S(1)}, bf16[4,160,384]{2,1,0:T(8,128)(2,1)S(1)}, u32[]{:S(2)}, u32[]{:S(2)}) collective-permute-start(bf16[4,160,384]{2,1,0:T(8,128)(2,1)S(1)} %get-tuple-element.33), channel_id=1, source_target_pairs={{4,0},{8,4},{12,8},{16,12},{20,16},{24,20},{28,24},{32,28},{36,32}... | collective-permute-start | bytes 1474568 | tf_op jit(solution)/shard_map/ppermute | solution.py:256
  58.6 15.5 %collective-permute-start.10 = (bf16[4,160,384]{2,1,0:T(8,128)(2,1)S(1)}, bf16[4,160,384]{2,1,0:T(8,128)(2,1)S(1)}, u32[]{:S(2)}, u32[]{:S(2)}) collective-permute-start(bf16[4,160,384]{2,1,0:T(8,128)(2,1)S(1)} %get-tuple-element.34), channel_id=1, source_target_pairs={{0,4},{4,8},{8,12},{12,16},{16,20},{20,24},{24,28},{28,32},{32,36}... | collective-permute-start | bytes 1474568 | tf_op jit(solution)/shard_map/ppermute | solution.py:255
  61.7 25.1 %collective-permute-start.12 = (bf16[48,2592]{1,0:T(8,128)(2,1)S(1)}, bf16[48,2592]{1,0:T(8,128)(2,1)S(1)}, u32[]{:S(2)}, u32[]{:S(2)}) collective-permute-start(bf16[48,2592]{1,0:T(8,128)(2,1)S(1)} %get-tuple-element.23), channel_id=1, source_target_pairs={{0,16},{4,20},{8,24},{12,28},{16,0},{20,4},{24,8},{28,12},{32,48},... | collective-permute-start | bytes 746504 | tf_op jit(solution)/shard_map/ppermute | solution.py:252
  63.5 23.3 %collective-permute-start.13 = (bf16[48,2592]{1,0:T(8,128)(2,1)S(1)}, bf16[48,2592]{1,0:T(8,128)(2,1)S(1)}, u32[]{:S(2)}, u32[]{:S(2)}) collective-permute-start(bf16[48,2592]{1,0:T(8,128)(2,1)S(1)} %get-tuple-element.24), channel_id=1, source_target_pairs={{0,8},{4,12},{8,16},{12,20},{16,24},{20,28},{24,0},{28,4},{32,40},... | collective-permute-start | bytes 746504 | tf_op jit(solution)/shard_map/ppermute | solution.py:252
  64.1 22.8 %collective-permute-start.14 = (bf16[48,2592]{1,0:T(8,128)(2,1)S(1)}, bf16[48,2592]{1,0:T(8,128)(2,1)S(1)}, u32[]{:S(2)}, u32[]{:S(2)}) collective-permute-start(bf16[48,2592]{1,0:T(8,128)(2,1)S(1)} %get-tuple-element.25), channel_id=1, source_target_pairs={{0,24},{4,28},{8,0},{12,4},{16,8},{20,12},{24,16},{28,20},{32,56},... | collective-permute-start | bytes 746504 | tf_op jit(solution)/shard_map/ppermute | solution.py:252
  66.7 8.2 %copy-start.6 = (bf16[4,160,384]{2,1,0:T(8,128)(2,1)}, bf16[4,160,384]{2,1,0:T(8,128)(2,1)S(1)}, u32[]{:S(2)}) copy-start(bf16[4,160,384]{2,1,0:T(8,128)(2,1)S(1)} %collective-permute-done.11.dn) | copy-start | bytes 1474564
  88.0 6.4 %collective-permute-start.15 = (bf16[24,2592]{1,0:T(8,128)(2,1)S(1)}, bf16[24,2592]{1,0:T(8,128)(2,1)S(1)}, u32[]{:S(2)}, u32[]{:S(2)}) collective-permute-start(bf16[24,2592]{1,0:T(8,128)(2,1)S(1)} %slice.115), channel_id=1, source_target_pairs={{0,32},{4,36},{8,40},{12,44},{16,48},{20,52},{24,56},{28,60},{32,0... | collective-permute-start | bytes 373256 | tf_op jit(solution)/shard_map/ppermute | solution.py:275
  94.4 7.2 %collective-permute-start.16 = (f32[12,2592]{1,0:T(8,128)S(1)}, f32[12,2592]{1,0:T(8,128)S(1)}, u32[]{:S(2)}, u32[]{:S(2)}) collective-permute-start(f32[12,2592]{1,0:T(8,128)S(1)} %slice.94), channel_id=1, source_target_pairs={{0,64},{4,68},{8,72},{12,76},{16,80},{20,84},{24,88},{28,92},{32,9... | collective-permute-start | bytes 373256 | tf_op jit(solution)/shard_map/ppermute | solution.py:275
  101.6 9.7 %collective-permute-start.17 = (f32[6,2592]{1,0:T(8,128)S(1)}, f32[6,2592]{1,0:T(8,128)S(1)}, u32[]{:S(2)}, u32[]{:S(2)}) collective-permute-start(f32[6,2592]{1,0:T(8,128)S(1)} %slice.96), channel_id=1, source_target_pairs={{0,192},{4,196},{8,200},{12,204},{16,208},{20,212},{24,216},{28,22... | collective-permute-start | bytes 186632 | tf_op jit(solution)/shard_map/ppermute | solution.py:275
  (6 other events, 20.4 us)

commit v3 on v2

--- a/solution.py
+++ b/solution.py
@@ -8,7 +8,7 @@
 from jax.sharding import PartitionSpec as P
 
 F32, BF16 = jnp.float32, jnp.bfloat16
-VMEM_LIMIT = 60 * 1024 * 1024
+VMEM_LIMIT, VMEM_SMALL = 40 * 1024 * 1024, 26 * 1024 * 1024
 C, COLS, PART, LANES = 384, 160, 96, 128
 ZS, XS, YS = 8, 4, 4
 NT = (((1,), (1,)), ((), ()))
@@ -24,10 +24,6 @@
     return pairs
 
 
-def z_shift(steps):
-    return rows_perm(lambda z, x, c: ((z + steps) % ZS, x, c))
-
-
 def x_shift(steps):
     return rows_perm(lambda z, x, c: (z, (x + steps) % XS, c))
 
@@ -49,10 +45,10 @@
     inverse = lax.rsqrt(jnp.mean(floats * floats, axis=-1, keepdims=True) + 1e-6)
     pre_act = floats * inverse * gamma_ref[...][None, :]
     active = pre_act * jax.nn.sigmoid(pre_act)
-    blank = jnp.zeros((active.shape[0], LANES - PART), F32)
     for part in range(YS):
-        piece = active[:, part * PART : (part + 1) * PART]
-        piece = jnp.concatenate([piece, blank], axis=1).astype(BF16)
+        lanes = slice(part * PART, (part + 1) * PART)
+        lines = [active[q * COLS : (q + 1) * COLS, lanes] for q in range(4)]
+        piece = jnp.concatenate(lines, axis=1).astype(BF16)
         place = lax.rem(part - y_ref[0] + YS, YS)
         for k in range(YS):
 
@@ -62,25 +58,48 @@
 
 
 def activations(y, features, gamma):
-    pixels = features.shape[0]
     return pl.pallas_call(
         activation_kernel,
         in_specs=[pl.BlockSpec(memory_space=pltpu.SMEM)] + [pl.BlockSpec(memory_space=pltpu.VMEM)] * 2,
-        out_shape=[jax.ShapeDtypeStruct((pixels, LANES), BF16)] * YS,
+        out_shape=[jax.ShapeDtypeStruct((COLS, C), BF16)] * YS,
         compiler_params=pltpu.CompilerParams(vmem_limit_bytes=VMEM_LIMIT),
     )(y, features, gamma)
 
 
-def weight_kernel(y_ref, c3, c2a, c2b, c1, c0, a0, a1, a2, a3, up, dn, order_ref, own, send, spread, cot):
-    y = y_ref[0]
+def halo_kernel(a0, a1, a2, a3, up, dn):
+    acts = (a0, a1, a2, a3)
+    for out, h in ((up, 1), (dn, 0)):
+        for f in range(2):
+            at = (f * 2 + h) * PART
+            lines = [act[:, at : at + PART] for act in acts]
+            out[f] = jnp.concatenate(lines, axis=1)
+
+
+def halo_rows(acts):
+    return pl.pallas_call(
+        halo_kernel,
+        in_specs=[pl.BlockSpec(memory_space=pltpu.VMEM)] * 4,
+        out_specs=[pl.BlockSpec(memory_space=pltpu.VMEM)] * 2,
+        out_shape=[jax.ShapeDtypeStruct((2, COLS, C), BF16)] * 2,
+        compiler_params=pltpu.CompilerParams(vmem_limit_bytes=VMEM_SMALL),
+    )(*acts)
+
+
+def spread_kernel(a0, a1, a2, a3, up, dn, spread):
     acts = (a0, a1, a2, a3)
     column = lax.broadcasted_iota(jnp.int32, (4 * COLS, LANES), 0) % COLS
+    blank = jnp.zeros((4 * COLS, LANES - PART), F32)
     for k in range(4):
         for f in range(2):
-            value = jnp.concatenate(
-                [up[k, f, 0], acts[k][f, 0], acts[k][f, 1], dn[k, f, 0]], axis=0
-            )
-            floats = value.astype(F32)
+            lines = [
+                up[f, :, k * PART : (k + 1) * PART],
+                acts[k][:, f * 2 * PART : (f * 2 + 1) * PART],
+                acts[k][:, (f * 2 + 1) * PART : (f * 2 + 2) * PART],
+                dn[f, :, k * PART : (k + 1) * PART],
+            ]
+            floats = jnp.concatenate(lines, axis=0).astype(F32)
+            floats = jnp.concatenate([floats, blank], axis=1)
+            value = floats.astype(BF16)
             left = jnp.where(column == 0, 0.0, pltpu.roll(floats, 1, 0)).astype(BF16)
             right = jnp.where(column == COLS - 1, 0.0, pltpu.roll(floats, 4 * COLS - 1, 0)).astype(BF16)
             places = [(4 - k) * 2 + f] + ([f] if k == 0 else [])
@@ -90,21 +109,35 @@
                     for e, part in enumerate((left, value, right)):
                         at = (b * 3 + e) * LANES
                         spread[rows, at : at + LANES] = part[b * COLS : (b + 2) * COLS]
+
+
+def spread_windows(acts, up, dn):
+    return pl.pallas_call(
+        spread_kernel,
+        in_specs=[pl.BlockSpec(memory_space=pltpu.VMEM)] * 6,
+        out_specs=pl.BlockSpec(memory_space=pltpu.VMEM),
+        out_shape=jax.ShapeDtypeStruct((10 * 320, 9 * LANES), BF16),
+        compiler_params=pltpu.CompilerParams(vmem_limit_bytes=VMEM_SMALL),
+    )(*acts, up, dn)
+
+
+def weight_kernel(y_ref, c3, c2a, c2b, c1, c0, spread, order_ref, own, send, cot):
+    y = y_ref[0]
     order = order_ref[...]
+    rows = order.shape[0]
     for k, pieces in enumerate(((c0,), (c1,), (c2a, c2b), (c3,))):
         first = lax.rem(y - k + 4, 4) == 0
+        blocks = [
+            lax.dot_general(order, piece[...], NT, preferred_element_type=F32).astype(BF16)
+            for piece in pieces
+        ]
+        block = blocks[0] if len(blocks) == 1 else jnp.concatenate(blocks, axis=1)
+        blank = jnp.zeros_like(block)
+        frame = lax.broadcasted_iota(jnp.int32, block.shape, 1)
         at = (3 - k) * 640
-        for piece in pieces:
-            size = piece.shape[0]
-            block = lax.dot_general(order, piece[...], NT, preferred_element_type=F32).astype(BF16)
-            blank = jnp.zeros_like(block)
-            cot[2, :, at : at + size] = block
-            cot[0, :, at : at + size] = jnp.where(first, blank, block)
-            at += size
-        at = (3 - k) * 640
-        frame = lax.broadcasted_iota(jnp.int32, (C, 640), 1)
-        block = cot[2, :, at : at + 640]
-        cot[1, :, at : at + 640] = jnp.where(first & (frame < 320), jnp.zeros_like(block), block)
+        cot[2, :, at : at + 640] = block
+        cot[1, :, at : at + 640] = jnp.where(first & (frame < 320), blank, block)
+        cot[0, :, at : at + 640] = jnp.where(first, blank, block)
     pieces = []
     for a in range(3):
         value = jnp.dot(
@@ -112,24 +145,22 @@
         )
         pieces += [value[:, s * LANES : s * LANES + PART] for s in range(9)]
     packed = jnp.concatenate(pieces, axis=1)
-    own[...] = packed[: C // 2]
-    send[...] = packed[C // 2 :].astype(BF16)
-
-
-def weight_partials(y, cots, acts, up, dn, order):
-    shape = (C // 2, 27 * PART)
+    own[...] = packed[: rows // 2]
+    send[...] = packed[rows // 2 :]
+
+
+def weight_partials(y, cots, spread, order):
+    rows = order.shape[0]
+    shape = (rows // 2, 27 * PART)
     return pl.pallas_call(
         weight_kernel,
-        in_specs=[pl.BlockSpec(memory_space=pltpu.SMEM)] + [pl.BlockSpec(memory_space=pltpu.VMEM)] * 12,
+        in_specs=[pl.BlockSpec(memory_space=pltpu.SMEM)] + [pl.BlockSpec(memory_space=pltpu.VMEM)] * 7,
         out_specs=[pl.BlockSpec(memory_space=pltpu.VMEM)] * 2,
-        out_shape=[jax.ShapeDtypeStruct(shape, F32), jax.ShapeDtypeStruct(shape, BF16)],
-        scratch_shapes=[
-            pltpu.VMEM((10 * 320, 9 * LANES), BF16),
-            pltpu.VMEM((3, C, 2560), BF16),
-        ],
-        compiler_params=pltpu.CompilerParams(vmem_limit_bytes=VMEM_LIMIT),
-        cost_estimate=pl.CostEstimate(flops=14 * 2 * 384 * 2560 * 256, bytes_accessed=8_000_000, transcendentals=0),
-    )(y, *cots, *acts, up, dn, order)
+        out_shape=[jax.ShapeDtypeStruct(shape, F32)] * 2,
+        scratch_shapes=[pltpu.VMEM((3, rows, 2560), BF16)],
+        compiler_params=pltpu.CompilerParams(vmem_limit_bytes=VMEM_SMALL),
+        cost_estimate=pl.CostEstimate(flops=28 * rows * 2560 * 256 * 2, bytes_accessed=8_000_000, transcendentals=0),
+    )(y, *cots, spread, order)
 
 
 def input_kernel(y_ref, own, following, up, dn, taps_ref, features_ref, gamma_ref, out_ref, ext, side):
@@ -140,11 +171,11 @@
         keep = y_ref[0] != 3
         for f in range(2):
             ext[f, COLS : 3 * COLS] = own[f]
+            ext[f, :COLS] = up[f]
+            ext[f, 3 * COLS :] = dn[f]
             ext[f + 2, COLS : 3 * COLS] = jnp.where(keep, following[f], jnp.zeros_like(following[f]))
-        for f in range(4):
-            good = keep if f >= 2 else True
-            ext[f, :COLS] = jnp.where(good, up[f], jnp.zeros_like(up[f]))
-            ext[f, 3 * COLS :] = jnp.where(good, dn[f], jnp.zeros_like(dn[f]))
+            ext[f + 2, :COLS] = jnp.where(keep, up[f + 2], jnp.zeros_like(up[f + 2]))
+            ext[f + 2, 3 * COLS :] = jnp.where(keep, dn[f + 2], jnp.zeros_like(dn[f + 2]))
 
     rows = []
     for f in range(2):
@@ -208,9 +239,10 @@
     )(y, own, following, up, dn, taps, features, gamma)
 
 
-def output_order(z, x, core):
-    row = jnp.arange(C)
-    c2, x2, z2, j = row // 192, row // 48 % XS, row // 6 % ZS, row % 6
+def output_order(z, x, core, parts):
+    row = jnp.arange(len(parts) * 96)
+    c2, at, z2, j = row // (48 * len(parts)), row // 48 % len(parts), row // 6 % ZS, row % 6
+    x2 = jnp.where(at == 0, parts[0], parts[1])
     bits = z2 // 4 ^ z2 // 2 % 2 * 2 ^ z2 % 2 * 6
     channel = (z ^ bits) * 48 + (x + x2) % XS * 12 + (core + c2) % 2 * 6 + j
     return (channel[:, None] == jnp.arange(C)[None, :]).astype(BF16)
@@ -222,38 +254,43 @@
     y, r = lax.axis_index("tm"), lax.axis_index("rows")
     z, x, core = r // (2 * XS), (r // 2) % XS, r % 2
     block = y.reshape(1).astype(jnp.int32)
-    order = output_order(z, x, core)
+    groups = ((2, 1), (3, 0))
+    orders = [output_order(z, x, core, parts) for parts in groups]
     flat = features.reshape(pixels, width)
     taps = jnp.transpose(kernel, (1, 0, 2)).reshape(3, 3, 3, width, width)
 
-    following = lax.ppermute(cotangent, "tm", y_shift(3))
-    previous = lax.ppermute(cotangent, "tm", y_shift(1))
     active = activations(block, flat, gamma)
     acts = [active[0]] + [lax.ppermute(active[k], "tm", y_shift(k)) for k in (1, 2, 3)]
-    acts = [value.reshape(2, 2, columns, LANES) for value in acts]
+    local, *acts = lax.optimization_barrier((cotangent, *acts))
+    following = lax.ppermute(local, "tm", y_shift(3))
+    previous = lax.ppermute(local, "tm", y_shift(1))
+    rows_up, rows_dn = halo_rows(acts)
+    rows_up = lax.ppermute(rows_up, "rows", line(64, 1))
+    rows_dn = lax.ppermute(rows_dn, "rows", line(64, -1))
     far = [
         lax.ppermute(previous[0], "tm", y_shift(1)).reshape(pixels // 2, width),
         lax.ppermute(following[1], "tm", y_shift(3)).reshape(pixels // 2, width),
     ]
-    stacked = jnp.stack(acts)
-    act_up = lax.ppermute(stacked[:, :, 1:], "rows", line(64, 1))
-    act_dn = lax.ppermute(stacked[:, :, :1], "rows", line(64, -1))
-    cots = [following.reshape(pixels, width), *far, previous.reshape(pixels, width), cotangent.reshape(pixels, width)]
-    own, send = weight_partials(block, cots, acts, act_up, act_dn, order)
-    other = lax.ppermute(send, "rows", core_swap())
-
-    def part(k):
-        rows = slice(48 * k, 48 * k + 48)
-        return own[rows] + other[rows].astype(F32)
-
-    kept = part(0)
-    parts = [part(k).astype(BF16) for k in (2, 1, 3)]
-    block, *parts = lax.optimization_barrier((block, *parts))
-    received = [lax.ppermute(value, "rows", x_shift(k)) for value, k in zip(parts, (2, 1, 3))]
-
     ext = jnp.concatenate([cotangent, following], axis=0)
     cot_up = lax.ppermute(ext[:, 1], "rows", line(64, 1))
     cot_dn = lax.ppermute(ext[:, 0], "rows", line(64, -1))
+    far, rows_up, rows_dn = lax.optimization_barrier((far, rows_up, rows_dn))
+    spread = spread_windows(acts, rows_up, rows_dn)
+    orders[1], cot_up, cot_dn = lax.optimization_barrier((orders[1], cot_up, cot_dn))
+    cots = [following.reshape(pixels, width), *far, previous.reshape(pixels, width), cotangent.reshape(pixels, width)]
+
+    own, send = weight_partials(block, cots, spread, orders[0])
+    other = lax.ppermute(send, "rows", core_swap())
+    orders[1], own = lax.optimization_barrier((orders[1], own))
+    own_2, send_2 = weight_partials(block, cots, spread, orders[1])
+    other_2 = lax.ppermute(send_2, "rows", core_swap())
+
+    early = [(own[48 * n : 48 * n + 48] + other[48 * n : 48 * n + 48]).astype(BF16) for n in range(2)]
+    late = (own_2[:48] + other_2[:48]).astype(BF16)
+    block, *early = lax.optimization_barrier((block, *early))
+    received = [lax.ppermute(value, "rows", x_shift(k)) for value, k in zip(early, groups[0])]
+    block, late = lax.optimization_barrier((block, late))
+    received.append(lax.ppermute(late, "rows", x_shift(3)))
     input_grad = input_gradient(
         block,
         cotangent.reshape(2, 2 * columns, width),
@@ -264,15 +301,14 @@
         flat,
         gamma,
     )
-
     input_grad, *received = lax.optimization_barrier((input_grad, *received))
-    total = kept
+    total = own_2[48:] + other_2[48:]
     for value in received:
         total = total + value.astype(F32)
-    for bits, wire in ((1, BF16), (2, F32), (6, F32)):
+    for bits in (1, 2, 6):
         half = total.shape[0] // 2
         pairs = rows_perm(lambda z, x, c: (z ^ bits, x, c))
-        total = total[:half] + lax.ppermute(total[half:].astype(wire), "rows", pairs).astype(F32)
+        total = total[:half] + lax.ppermute(total[half:].astype(BF16), "rows", pairs).astype(F32)
     mine = total.reshape(6, 27, PART)
     count = pixels * lax.axis_size("tm") * lax.axis_size("rows")
     weight_grad = jnp.transpose(mine, (2, 1, 0)) * (1.0 / math.sqrt(count))

time: 112 us -> 91.7 us (0.82)
  the two profiles are of different devices: /device:TPU:56 before, /device:TPU:6 now
where the time goes in v3:
time: 91.7 us; the launch traced here: 91.3 us
  starting transfers between devices  37.4 us (41%)
  waiting for transfers between devices  24.9 us (27%)
  Pallas kernels  22.5 us (25%)
  local copies, waits for them, and re-layouts  4.96 us (5%)
  between operations  0.92 us (1%)
    ppermute x3, waiting for transfers between devices, body(): lax.ppermute(total[half:].astype(BF16), 'rows', pairs).astype(F32)  13.6 us
    pallas_call x2, Pallas kernels, weight_partials(): pl.pallas_call(weight_kernel, in_specs=[pl.BlockSpec(memory_space=pltpu.S...  10.1 us
    pallas_call x1, Pallas kernels, input_gradient(): pl.pallas_call(input_kernel, grid=(3,), in_specs=[pl.BlockSpec(memory_spa...  9.58 us
    ppermute x3, starting transfers between devices, body(): lax.ppermute(total[half:].astype(BF16), 'rows', pairs).astype(F32)  8.81 us
    ppermute x3, starting transfers between devices, body(): lax.ppermute(active[k], 'tm', y_shift(k))  5.9 us
    ppermute x3, waiting for transfers between devices, body(): lax.ppermute(active[k], 'tm', y_shift(k))  4.28 us
    ppermute x1, starting transfers between devices, body(): cot_dn = lax.ppermute(ext[:, 0], 'rows', line(64, -1))  3.82 us
    ppermute x1, starting transfers between devices, body(): rows_dn = lax.ppermute(rows_dn, 'rows', line(64, -1))  3.64 us
  transfers between devices with their start and end apart: 19, of which 9 were waited for; matrix products, arithmetic and copies ran while one was open for 3% of the time, Pallas kernels for 24%

profile of v3, /device:TPU:6, one launch (start us, length us, event | category | flops | bytes accessed | tf_op | source)
XLA Modules:
  0.0 91.3 jit_solution(14599610172882176632)
XLA Ops:
  3.1 1.7 %collective-permute-start = (bf16[160,384]{1,0:T(8,128)(2,1)S(1)}, bf16[160,384]{1,0:T(8,128)(2,1)S(1)}, u32[]{:S(2)}, u32[]{:S(2)}) collective-permute-start(bf16[160,384]{1,0:T(8,128)(2,1)S(1)} %get-tuple-element.36), channel_id=1, source_target_pairs={{0,1},{1,2},{2,3},{3,0},{4,5},{5,6},{6,7},{7,4},{8,9},{9,10},{10,1... | collective-permute-start | bytes 368648 | tf_op jit(solution)/shard_map/ppermute | solution.py:263
  4.8 2.9 %collective-permute-start.1 = (bf16[160,384]{1,0:T(8,128)(2,1)S(1)}, bf16[160,384]{1,0:T(8,128)(2,1)S(1)}, u32[]{:S(2)}, u32[]{:S(2)}) collective-permute-start(bf16[160,384]{1,0:T(8,128)(2,1)S(1)} %get-tuple-element.37), channel_id=1, source_target_pairs={{0,2},{1,3},{2,0},{3,1},{4,6},{5,7},{6,4},{7,5},{8,10},{9,11},{10,... | collective-permute-start | bytes 368648 | tf_op jit(solution)/shard_map/ppermute | solution.py:263
  7.7 1.3 %collective-permute-start.2 = (bf16[160,384]{1,0:T(8,128)(2,1)S(1)}, bf16[160,384]{1,0:T(8,128)(2,1)S(1)}, u32[]{:S(2)}, u32[]{:S(2)}) collective-permute-start(bf16[160,384]{1,0:T(8,128)(2,1)S(1)} %get-tuple-element.38), channel_id=1, source_target_pairs={{0,3},{1,0},{2,1},{3,2},{4,7},{5,4},{6,5},{7,6},{8,11},{9,8},{10,9... | collective-permute-start | bytes 368648 | tf_op jit(solution)/shard_map/ppermute | solution.py:263
  9.6 3.8 %collective-permute-done.1.a2 = bf16[160,384]{1,0:T(8,128)(2,1)S(1)} collective-permute-done((bf16[160,384]{1,0:T(8,128)(2,1)S(1)}, bf16[160,384]{1,0:T(8,128)(2,1)S(1)}, u32[]{:S(2)}, u32[]{:S(2)}) %collective-permute-start.1) | collective-permute-done | bytes 122912 | tf_op jit(solution)/shard_map/ppermute | solution.py:263
  13.4 1.2 %collective-permute-start.6 = (bf16[2,2,160,384]{3,2,1,0:T(8,128)(2,1)}, bf16[2,2,160,384]{3,2,1,0:T(8,128)(2,1)S(1)}, u32[]{:S(2)}, u32[]{:S(2)}) collective-permute-start(bf16[2,2,160,384]{3,2,1,0:T(8,128)(2,1)} %param.5), channel_id=1, source_target_pairs={{0,1},{1,2},{2,3},{3,0},{4,5},{5,6},{6,7},{7,4},{8,9},{9,10},{10,1... | collective-permute-start | bytes 1474568 | tf_op jit(solution)/shard_map/ppermute | solution.py:266
  15.8 2.1 %collective-permute-start.3 = (bf16[2,2,160,384]{3,2,0,1:T(8,128)(2,1)S(1)}, bf16[2,2,160,384]{3,2,0,1:T(8,128)(2,1)S(1)}, u32[]{:S(2)}, u32[]{:S(2)}) collective-permute-start(bf16[2,2,160,384]{3,2,0,1:T(8,128)(2,1)S(1)} %copy.8), channel_id=1, source_target_pairs={{0,3},{1,0},{2,1},{3,2},{4,7},{5,4},{6,5},{7,6},{8,11},{9,8},{10,9... | collective-permute-start | bytes 1474568 | tf_op jit(solution)/shard_map/ppermute | solution.py:265
  19.3 1.9 %collective-permute-start.9 = (bf16[2,160,384]{2,1,0:T(8,128)(2,1)S(1)}, bf16[2,160,384]{2,1,0:T(8,128)(2,1)S(1)}, u32[]{:S(2)}, u32[]{:S(2)}) collective-permute-start(bf16[2,160,384]{2,1,0:T(8,128)(2,1)S(1)} %get-tuple-element.45), channel_id=1, source_target_pairs={{0,4},{4,8},{8,12},{12,16},{16,20},{20,24},{24,28},{28,32},{32,36}... | collective-permute-start | bytes 737288 | tf_op jit(solution)/shard_map/ppermute | solution.py:268
  21.2 3.6 %collective-permute-start.10 = (bf16[2,160,384]{2,1,0:T(8,128)(2,1)S(1)}, bf16[2,160,384]{2,1,0:T(8,128)(2,1)S(1)}, u32[]{:S(2)}, u32[]{:S(2)}) collective-permute-start(bf16[2,160,384]{2,1,0:T(8,128)(2,1)S(1)} %get-tuple-element.46), channel_id=1, source_target_pairs={{4,0},{8,4},{12,8},{16,12},{20,16},{24,20},{28,24},{32,28},{36,32}... | collective-permute-start | bytes 737288 | tf_op jit(solution)/shard_map/ppermute | solution.py:269
  24.8 2.0 %collective-permute-done.6 = bf16[2,2,160,384]{3,2,1,0:T(8,128)(2,1)S(1)} collective-permute-done((bf16[2,2,160,384]{3,2,1,0:T(8,128)(2,1)}, bf16[2,2,160,384]{3,2,1,0:T(8,128)(2,1)S(1)}, u32[]{:S(2)}, u32[]{:S(2)}) %collective-permute-start.6) | collective-permute-done | bytes 491552 | tf_op jit(solution)/shard_map/ppermute | solution.py:266
  27.6 3.4 %collective-permute-start.8 = (bf16[2,160,384]{2,1,0:T(8,128)(2,1)S(1)}, bf16[2,160,384]{2,1,0:T(8,128)(2,1)S(1)}, u32[]{:S(2)}, u32[]{:S(2)}) collective-permute-start(bf16[2,160,384]{2,1,0:T(8,128)(2,1)S(1)} %slice_bitcast_fusion.2), channel_id=1, source_target_pairs={{0,3},{1,0},{2,1},{3,2},{4,7},{5,4},{6,5},{7,6},{8,11},{9,8},{10,9... | collective-permute-start | bytes 737288 | tf_op jit(solution)/shard_map/ppermute | solution.py:272
  31.2 1.9 %collective-permute-start.4 = (bf16[4,160,384]{2,1,0:T(8,128)(2,1)S(1)}, bf16[4,160,384]{2,1,0:T(8,128)(2,1)S(1)}, u32[]{:S(2)}, u32[]{:S(2)}) collective-permute-start(bf16[4,160,384]{2,1,0:T(8,128)(2,1)S(1)} %get-tuple-element.71), channel_id=1, source_target_pairs={{0,4},{4,8},{8,12},{12,16},{16,20},{20,24},{24,28},{28,32},{32,36}... | collective-permute-start | bytes 1474568 | tf_op jit(solution)/shard_map/ppermute | solution.py:275
  33.2 3.8 %collective-permute-start.5 = (bf16[4,160,384]{2,1,0:T(8,128)(2,1)S(1)}, bf16[4,160,384]{2,1,0:T(8,128)(2,1)S(1)}, u32[]{:S(2)}, u32[]{:S(2)}) collective-permute-start(bf16[4,160,384]{2,1,0:T(8,128)(2,1)S(1)} %get-tuple-element.70), channel_id=1, source_target_pairs={{4,0},{8,4},{12,8},{16,12},{20,16},{24,20},{28,24},{32,28},{36,32}... | collective-permute-start | bytes 1474568 | tf_op jit(solution)/shard_map/ppermute | solution.py:276
  37.0 1.7 %shard_map.61.spread = bf16[3200,1152]{1,0:T(8,128)(2,1)S(1)} custom-call(bf16[160,384]{1,0:T(8,128)(2,1)S(1)} %get-tuple-element.41.a0, bf16[160,384]{1,0:T(8,128)(2,1)S(1)} %collective-permute-done.a1, bf16[160,384]{1,0:T(8,128)(2,1)S(1)} %collective-permute-done.1.a2, bf16[160,384]{1,0:T(8,128)(2,1)S(1)} %collective-permute-done.2.a3, ...), custom_call_target="tpu_custom_call" | custom-call | tf_op jit(solution)/shard_map/pallas_call | solution.py:115
  38.8 5.1 %shard_map.62 = (f32[96,2592]{1,0:T(8,128)S(1)}, f32[96,2592]{1,0:T(8,128)S(1)}) custom-call(s32[1]{0:T(128)} %bitcast.y_ref, bf16[640,384]{1,0:T(8,128)(2,1)S(1)} %bitcast.27, bf16[320,384]{1,0:T(8,128)(2,1)S(1)} %bitcast.35, bf16[320,384]{1,0:T(8,128)(2,1)S(1)} %bitcast.37, bf16[640,384]{1,0:T(8,128)(2,1)S(1)} %bitcast.30, bf16[640,384]{1,0:T(8,128)(2,1)S(1)} %bitcast.22, ...), custom_call_target="tpu_custom_call" | custom-call | flops 7046430720 | bytes 8000000 | tf_op jit(solution)/shard_map/pallas_call | solution.py:155
  44.3 5.1 %shard_map.63 = (f32[96,2592]{1,0:T(8,128)S(1)}, f32[96,2592]{1,0:T(8,128)S(1)}) custom-call(s32[1]{0:T(128)} %bitcast.y_ref, bf16[640,384]{1,0:T(8,128)(2,1)S(1)} %bitcast.28, bf16[320,384]{1,0:T(8,128)(2,1)S(1)} %bitcast.36, bf16[320,384]{1,0:T(8,128)(2,1)S(1)} %bitcast.38, bf16[640,384]{1,0:T(8,128)(2,1)S(1)} %bitcast.31, bf16[640,384]{1,0:T(8,128)(2,1)S(1)} %bitcast.23, ...), custom_call_target="tpu_custom_call" | custom-call | flops 7046430720 | bytes 8000000 | tf_op jit(solution)/shard_map/pallas_call | solution.py:155
  49.4 3.2 %collective-permute-start.12 = (f32[96,2592]{1,0:T(8,128)S(1)}, f32[96,2592]{1,0:T(8,128)S(1)}, u32[]{:S(2)}, u32[]{:S(2)}) collective-permute-start(f32[96,2592]{1,0:T(8,128)S(1)} %get-tuple-element.57), channel_id=1, source_target_pairs={{0,4},{4,0},{8,12},{12,8},{16,20},{20,16},{24,28},{28,24},{32,36},... | collective-permute-start | bytes 2985992 | tf_op jit(solution)/shard_map/ppermute | solution.py:286
  53.5 1.3 %collective-permute-done.12 = f32[96,2592]{1,0:T(8,128)S(1)} collective-permute-done((f32[96,2592]{1,0:T(8,128)S(1)}, f32[96,2592]{1,0:T(8,128)S(1)}, u32[]{:S(2)}, u32[]{:S(2)}) %collective-permute-start.12) | collective-permute-done | bytes 995360 | tf_op jit(solution)/shard_map/ppermute | solution.py:286
  55.2 9.6 %shard_map.64 = bf16[640,384]{1,0:T(8,128)(2,1)} custom-call(s32[1]{0:T(128)} %bitcast.y_ref, bf16[2,320,384]{2,1,0:T(8,128)(2,1)S(1)} %bitcast.24, bf16[2,320,384]{2,1,0:T(8,128)(2,1)S(1)} %bitcast.29, bf16[4,160,384]{2,1,0:T(8,128)(2,1)S(1)} %collective-permute-done.4.up, bf16[4,160,384]{2,1,0:T(8,128)(2,1)S(1)} %collective-permute-done.5.dn, ...), custom_call_target="tpu_custom_call" | custom-call | flops 5096079360 | bytes 12000000 | tf_op jit(solution)/shard_map/pallas_call | solution.py:218
  64.8 3.1 %collective-permute-done.15 = bf16[48,2592]{1,0:T(8,128)(2,1)S(1)} collective-permute-done((bf16[48,2592]{1,0:T(8,128)(2,1)S(1)}, bf16[48,2592]{1,0:T(8,128)(2,1)S(1)}, u32[]{:S(2)}, u32[]{:S(2)}) %collective-permute-start.15) | collective-permute-done | bytes 248864 | tf_op jit(solution)/shard_map/ppermute | solution.py:293
  68.1 2.0 %collective-permute-start.16 = (bf16[24,2592]{1,0:T(8,128)(2,1)S(1)}, bf16[24,2592]{1,0:T(8,128)(2,1)S(1)}, u32[]{:S(2)}, u32[]{:S(2)}) collective-permute-start(bf16[24,2592]{1,0:T(8,128)(2,1)S(1)} %slice.121), channel_id=1, source_target_pairs={{0,32},{4,36},{8,40},{12,44},{16,48},{20,52},{24,56},{28,60},{32,0... | collective-permute-start | bytes 373256 | tf_op jit(solution)/shard_map/ppermute | solution.py:311
  70.1 3.7 %collective-permute-done.16 = bf16[24,2592]{1,0:T(8,128)(2,1)S(1)} collective-permute-done((bf16[24,2592]{1,0:T(8,128)(2,1)S(1)}, bf16[24,2592]{1,0:T(8,128)(2,1)S(1)}, u32[]{:S(2)}, u32[]{:S(2)}) %collective-permute-start.16) | collective-permute-done | bytes 124448 | tf_op jit(solution)/shard_map/ppermute | solution.py:311
  73.8 6.4 %collective-permute-start.17 = (bf16[12,2592]{1,0:T(8,128)(2,1)S(1)}, bf16[12,2592]{1,0:T(8,128)(2,1)S(1)}, u32[]{:S(2)}, u32[]{:S(2)}) collective-permute-start(bf16[12,2592]{1,0:T(8,128)(2,1)S(1)} %slice.122), channel_id=1, source_target_pairs={{0,64},{4,68},{8,72},{12,76},{16,80},{20,84},{24,88},{28,92},{32,9... | collective-permute-start | bytes 186632 | tf_op jit(solution)/shard_map/ppermute | solution.py:311
  80.2 4.1 %collective-permute-done.17 = bf16[12,2592]{1,0:T(8,128)(2,1)S(1)} collective-permute-done((bf16[12,2592]{1,0:T(8,128)(2,1)S(1)}, bf16[12,2592]{1,0:T(8,128)(2,1)S(1)}, u32[]{:S(2)}, u32[]{:S(2)}) %collective-permute-start.17) | collective-permute-done | bytes 62240 | tf_op jit(solution)/shard_map/ppermute | solution.py:311
  84.7 5.8 %collective-permute-done.18 = bf16[6,2592]{1,0:T(8,128)(2,1)S(1)} collective-permute-done((bf16[6,2592]{1,0:T(8,128)(2,1)S(1)}, bf16[6,2592]{1,0:T(8,128)(2,1)S(1)}, u32[]{:S(2)}, u32[]{:S(2)}) %collective-permute-start.18) | collective-permute-done | bytes 31136 | tf_op jit(solution)/shard_map/ppermute | solution.py:311
  (56 shorter events, 9.7 us)
Async XLA Ops:
  3.1 6.4 %collective-permute-start = (bf16[160,384]{1,0:T(8,128)(2,1)S(1)}, bf16[160,384]{1,0:T(8,128)(2,1)S(1)}, u32[]{:S(2)}, u32[]{:S(2)}) collective-permute-start(bf16[160,384]{1,0:T(8,128)(2,1)S(1)} %get-tuple-element.36), channel_id=1, source_target_pairs={{0,1},{1,2},{2,3},{3,0},{4,5},{5,6},{6,7},{7,4},{8,9},{9,10},{10,1... | collective-permute-start | bytes 368648 | tf_op jit(solution)/shard_map/ppermute | solution.py:263
  4.8 8.6 %collective-permute-start.1 = (bf16[160,384]{1,0:T(8,128)(2,1)S(1)}, bf16[160,384]{1,0:T(8,128)(2,1)S(1)}, u32[]{:S(2)}, u32[]{:S(2)}) collective-permute-start(bf16[160,384]{1,0:T(8,128)(2,1)S(1)} %get-tuple-element.37), channel_id=1, source_target_pairs={{0,2},{1,3},{2,0},{3,1},{4,6},{5,7},{6,4},{7,5},{8,10},{9,11},{10,... | collective-permute-start | bytes 368648 | tf_op jit(solution)/shard_map/ppermute | solution.py:263
  7.7 5.7 %collective-permute-start.2 = (bf16[160,384]{1,0:T(8,128)(2,1)S(1)}, bf16[160,384]{1,0:T(8,128)(2,1)S(1)}, u32[]{:S(2)}, u32[]{:S(2)}) collective-permute-start(bf16[160,384]{1,0:T(8,128)(2,1)S(1)} %get-tuple-element.38), channel_id=1, source_target_pairs={{0,3},{1,0},{2,1},{3,2},{4,7},{5,4},{6,5},{7,6},{8,11},{9,8},{10,9... | collective-permute-start | bytes 368648 | tf_op jit(solution)/shard_map/ppermute | solution.py:263
  9.0 29.7 %copy-start = (bf16[2,2,160,384]{3,2,1,0:T(8,128)(2,1)S(1)}, bf16[2,2,160,384]{3,2,1,0:T(8,128)(2,1)}, u32[]{:S(2)}) copy-start(bf16[2,2,160,384]{3,2,1,0:T(8,128)(2,1)} %param.5) | copy-start | bytes 1474564
  13.4 13.5 %collective-permute-start.6 = (bf16[2,2,160,384]{3,2,1,0:T(8,128)(2,1)}, bf16[2,2,160,384]{3,2,1,0:T(8,128)(2,1)S(1)}, u32[]{:S(2)}, u32[]{:S(2)}) collective-permute-start(bf16[2,2,160,384]{3,2,1,0:T(8,128)(2,1)} %param.5), channel_id=1, source_target_pairs={{0,1},{1,2},{2,3},{3,0},{4,5},{5,6},{6,7},{7,4},{8,9},{9,10},{10,1... | collective-permute-start | bytes 1474568 | tf_op jit(solution)/shard_map/ppermute | solution.py:266
  15.8 11.8 %collective-permute-start.3 = (bf16[2,2,160,384]{3,2,0,1:T(8,128)(2,1)S(1)}, bf16[2,2,160,384]{3,2,0,1:T(8,128)(2,1)S(1)}, u32[]{:S(2)}, u32[]{:S(2)}) collective-permute-start(bf16[2,2,160,384]{3,2,0,1:T(8,128)(2,1)S(1)} %copy.8), channel_id=1, source_target_pairs={{0,3},{1,0},{2,1},{3,2},{4,7},{5,4},{6,5},{7,6},{8,11},{9,8},{10,9... | collective-permute-start | bytes 1474568 | tf_op jit(solution)/shard_map/ppermute | solution.py:265
  19.3 13.9 %collective-permute-start.9 = (bf16[2,160,384]{2,1,0:T(8,128)(2,1)S(1)}, bf16[2,160,384]{2,1,0:T(8,128)(2,1)S(1)}, u32[]{:S(2)}, u32[]{:S(2)}) collective-permute-start(bf16[2,160,384]{2,1,0:T(8,128)(2,1)S(1)} %get-tuple-element.45), channel_id=1, source_target_pairs={{0,4},{4,8},{8,12},{12,16},{16,20},{20,24},{24,28},{28,32},{32,36}... | collective-permute-start | bytes 737288 | tf_op jit(solution)/shard_map/ppermute | solution.py:268
  21.2 15.8 %collective-permute-start.10 = (bf16[2,160,384]{2,1,0:T(8,128)(2,1)S(1)}, bf16[2,160,384]{2,1,0:T(8,128)(2,1)S(1)}, u32[]{:S(2)}, u32[]{:S(2)}) collective-permute-start(bf16[2,160,384]{2,1,0:T(8,128)(2,1)S(1)} %get-tuple-element.46), channel_id=1, source_target_pairs={{4,0},{8,4},{12,8},{16,12},{20,16},{24,20},{28,24},{32,28},{36,32}... | collective-permute-start | bytes 737288 | tf_op jit(solution)/shard_map/ppermute | solution.py:269
  26.9 10.1 %collective-permute-start.7 = (bf16[2,160,384]{2,1,0:T(8,128)(2,1)S(1)}, bf16[2,160,384]{2,1,0:T(8,128)(2,1)S(1)}, u32[]{:S(2)}, u32[]{:S(2)}) collective-permute-start(bf16[2,160,384]{2,1,0:T(8,128)(2,1)S(1)} %slice_bitcast_fusion.3), channel_id=1, source_target_pairs={{0,1},{1,2},{2,3},{3,0},{4,5},{5,6},{6,7},{7,4},{8,9},{9,10},{10,1... | collective-permute-start | bytes 737288 | tf_op jit(solution)/shard_map/ppermute | solution.py:271
  27.6 9.4 %collective-permute-start.8 = (bf16[2,160,384]{2,1,0:T(8,128)(2,1)S(1)}, bf16[2,160,384]{2,1,0:T(8,128)(2,1)S(1)}, u32[]{:S(2)}, u32[]{:S(2)}) collective-permute-start(bf16[2,160,384]{2,1,0:T(8,128)(2,1)S(1)} %slice_bitcast_fusion.2), channel_id=1, source_target_pairs={{0,3},{1,0},{2,1},{3,2},{4,7},{5,4},{6,5},{7,6},{8,11},{9,8},{10,9... | collective-permute-start | bytes 737288 | tf_op jit(solution)/shard_map/ppermute | solution.py:272
  31.2 13.1 %collective-permute-start.4 = (bf16[4,160,384]{2,1,0:T(8,128)(2,1)S(1)}, bf16[4,160,384]{2,1,0:T(8,128)(2,1)S(1)}, u32[]{:S(2)}, u32[]{:S(2)}) collective-permute-start(bf16[4,160,384]{2,1,0:T(8,128)(2,1)S(1)} %get-tuple-element.71), channel_id=1, source_target_pairs={{0,4},{4,8},{8,12},{12,16},{16,20},{20,24},{24,28},{28,32},{32,36}... | collective-permute-start | bytes 1474568 | tf_op jit(solution)/shard_map/ppermute | solution.py:275
  33.2 11.1 %collective-permute-start.5 = (bf16[4,160,384]{2,1,0:T(8,128)(2,1)S(1)}, bf16[4,160,384]{2,1,0:T(8,128)(2,1)S(1)}, u32[]{:S(2)}, u32[]{:S(2)}) collective-permute-start(bf16[4,160,384]{2,1,0:T(8,128)(2,1)S(1)} %get-tuple-element.70), channel_id=1, source_target_pairs={{4,0},{8,4},{12,8},{16,12},{20,16},{24,20},{28,24},{32,28},{36,32}... | collective-permute-start | bytes 1474568 | tf_op jit(solution)/shard_map/ppermute | solution.py:276
  38.8 16.4 %slice-start = ((s8[7962624]{0:T(1024)(128)(4,1)}), s8[4194304]{0:T(1024)(128)(4,1)S(1)}, s32[]{:S(2)}) async-start(s8[7962624]{0:T(1024)(128)(4,1)} %bitcast.32), calls=%async_computation | async-start | bytes 8388608
  43.8 8.7 %collective-permute-start.11 = (f32[96,2592]{1,0:T(8,128)S(1)}, f32[96,2592]{1,0:T(8,128)S(1)}, u32[]{:S(2)}, u32[]{:S(2)}) collective-permute-start(f32[96,2592]{1,0:T(8,128)S(1)} %get-tuple-element.53), channel_id=1, source_target_pairs={{0,4},{4,0},{8,12},{12,8},{16,20},{20,16},{24,28},{28,24},{32,36},... | collective-permute-start | bytes 2985992 | tf_op jit(solution)/shard_map/ppermute | solution.py:283
  44.3 10.9 %copy-start.2 = (bf16[2,2,160,384]{3,2,1,0:T(8,128)(2,1)S(1)}, bf16[2,2,160,384]{3,2,1,0:T(8,128)(2,1)}, u32[]{:S(2)}) copy-start(bf16[2,2,160,384]{3,2,1,0:T(8,128)(2,1)} %param.4) | copy-start | bytes 1474564
  44.3 10.9 %copy-start.4 = (f32[384]{0:T(512)S(1)}, f32[384]{0:T(512)}, u32[]{:S(2)}) copy-start(f32[384]{0:T(512)} %gamma_ref.3) | copy-start | bytes 4612
  44.3 10.9 %slice-start.1 = ((s8[7962624]{0:T(1024)(128)(4,1)}), s8[3768320]{0:T(1024)(128)(4,1)S(1)}, s32[]{:S(2)}) async-start(s8[7962624]{0:T(1024)(128)(4,1)} %bitcast.32), calls=%async_computation.1 | async-start | bytes 7536640
  49.4 5.4 %collective-permute-start.12 = (f32[96,2592]{1,0:T(8,128)S(1)}, f32[96,2592]{1,0:T(8,128)S(1)}, u32[]{:S(2)}, u32[]{:S(2)}) collective-permute-start(f32[96,2592]{1,0:T(8,128)S(1)} %get-tuple-element.57), channel_id=1, source_target_pairs={{0,4},{4,0},{8,12},{12,8},{16,20},{20,16},{24,28},{28,24},{32,36},... | collective-permute-start | bytes 2985992 | tf_op jit(solution)/shard_map/ppermute | solution.py:286
  52.6 12.2 %collective-permute-start.13 = (bf16[48,2592]{1,0:T(8,128)(2,1)S(1)}, bf16[48,2592]{1,0:T(8,128)(2,1)S(1)}, u32[]{:S(2)}, u32[]{:S(2)}) collective-permute-start(bf16[48,2592]{1,0:T(8,128)(2,1)S(1)} %get-tuple-element.61), channel_id=1, source_target_pairs={{0,16},{4,20},{8,24},{12,28},{16,0},{20,4},{24,8},{28,12},{32,48},... | collective-permute-start | bytes 746504 | tf_op jit(solution)/shard_map/ppermute | solution.py:291
  52.7 12.1 %collective-permute-start.14 = (bf16[48,2592]{1,0:T(8,128)(2,1)S(1)}, bf16[48,2592]{1,0:T(8,128)(2,1)S(1)}, u32[]{:S(2)}, u32[]{:S(2)}) collective-permute-start(bf16[48,2592]{1,0:T(8,128)(2,1)S(1)} %get-tuple-element.62), channel_id=1, source_target_pairs={{0,8},{4,12},{8,16},{12,20},{16,24},{20,28},{24,0},{28,4},{32,40},... | collective-permute-start | bytes 746504 | tf_op jit(solution)/shard_map/ppermute | solution.py:291
  54.9 13.1 %collective-permute-start.15 = (bf16[48,2592]{1,0:T(8,128)(2,1)S(1)}, bf16[48,2592]{1,0:T(8,128)(2,1)S(1)}, u32[]{:S(2)}, u32[]{:S(2)}) collective-permute-start(bf16[48,2592]{1,0:T(8,128)(2,1)S(1)} %fusion.3), channel_id=1, source_target_pairs={{0,24},{4,28},{8,0},{12,4},{16,8},{20,12},{24,16},{28,20},{32,56},... | collective-permute-start | bytes 746504 | tf_op jit(solution)/shard_map/ppermute | solution.py:293
  68.1 5.7 %collective-permute-start.16 = (bf16[24,2592]{1,0:T(8,128)(2,1)S(1)}, bf16[24,2592]{1,0:T(8,128)(2,1)S(1)}, u32[]{:S(2)}, u32[]{:S(2)}) collective-permute-start(bf16[24,2592]{1,0:T(8,128)(2,1)S(1)} %slice.121), channel_id=1, source_target_pairs={{0,32},{4,36},{8,40},{12,44},{16,48},{20,52},{24,56},{28,60},{32,0... | collective-permute-start | bytes 373256 | tf_op jit(solution)/shard_map/ppermute | solution.py:311
  73.8 10.5 %collective-permute-start.17 = (bf16[12,2592]{1,0:T(8,128)(2,1)S(1)}, bf16[12,2592]{1,0:T(8,128)(2,1)S(1)}, u32[]{:S(2)}, u32[]{:S(2)}) collective-permute-start(bf16[12,2592]{1,0:T(8,128)(2,1)S(1)} %slice.122), channel_id=1, source_target_pairs={{0,64},{4,68},{8,72},{12,76},{16,80},{20,84},{24,88},{28,92},{32,9... | collective-permute-start | bytes 186632 | tf_op jit(solution)/shard_map/ppermute | solution.py:311
  84.3 6.2 %collective-permute-start.18 = (bf16[6,2592]{1,0:T(8,128)(2,1)S(1)}, bf16[6,2592]{1,0:T(8,128)(2,1)S(1)}, u32[]{:S(2)}, u32[]{:S(2)}) collective-permute-start(bf16[6,2592]{1,0:T(8,128)(2,1)S(1)} %slice.123), channel_id=1, source_target_pairs={{0,192},{4,196},{8,200},{12,204},{16,208},{20,212},{24,216},{28,22... | collective-permute-start | bytes 93320 | tf_op jit(solution)/shard_map/ppermute | solution.py:311
  (2 other events, 1.7 us)

commit v4 on v3

--- a/solution.py
+++ b/solution.py
@@ -66,23 +66,24 @@
     )(y, features, gamma)
 
 
-def halo_kernel(a0, a1, a2, a3, up, dn):
+def halo_kernel(a0, a1, a2, a3, own, up, dn):
     acts = (a0, a1, a2, a3)
     for out, h in ((up, 1), (dn, 0)):
         for f in range(2):
             at = (f * 2 + h) * PART
             lines = [act[:, at : at + PART] for act in acts]
             out[f] = jnp.concatenate(lines, axis=1)
-
-
-def halo_rows(acts):
+            out[2 + f] = own[f, h]
+
+
+def halo_rows(acts, own):
     return pl.pallas_call(
         halo_kernel,
-        in_specs=[pl.BlockSpec(memory_space=pltpu.VMEM)] * 4,
+        in_specs=[pl.BlockSpec(memory_space=pltpu.VMEM)] * 5,
         out_specs=[pl.BlockSpec(memory_space=pltpu.VMEM)] * 2,
-        out_shape=[jax.ShapeDtypeStruct((2, COLS, C), BF16)] * 2,
-        compiler_params=pltpu.CompilerParams(vmem_limit_bytes=VMEM_SMALL),
-    )(*acts)
+        out_shape=[jax.ShapeDtypeStruct((4, COLS, C), BF16)] * 2,
+        compiler_params=pltpu.CompilerParams(vmem_limit_bytes=VMEM_SMALL),
+    )(*acts, own)
 
 
 def spread_kernel(a0, a1, a2, a3, up, dn, spread):
@@ -163,41 +164,56 @@
     )(y, *cots, spread, order)
 
 
-def input_kernel(y_ref, own, following, up, dn, taps_ref, features_ref, gamma_ref, out_ref, ext, side):
-    a = pl.program_id(0)
-
-    @pl.when(a == 0)
+def input_products(centre, edges, taps_ref, side, ext, lead, keep):
+    step = pl.program_id(0)
+
+    @pl.when(step == 0)
     def _():
-        keep = y_ref[0] != 3
         for f in range(2):
-            ext[f, COLS : 3 * COLS] = own[f]
-            ext[f, :COLS] = up[f]
-            ext[f, 3 * COLS :] = dn[f]
-            ext[f + 2, COLS : 3 * COLS] = jnp.where(keep, following[f], jnp.zeros_like(following[f]))
-            ext[f + 2, :COLS] = jnp.where(keep, up[f + 2], jnp.zeros_like(up[f + 2]))
-            ext[f + 2, 3 * COLS :] = jnp.where(keep, dn[f + 2], jnp.zeros_like(dn[f + 2]))
-
-    rows = []
-    for f in range(2):
-        pieces = [ext[f + 2 - a, (2 - b) * COLS : (4 - b) * COLS] for b in range(3)]
-        rows.append(jnp.concatenate(pieces, axis=1))
+            for rows, value in (
+                (slice(0, COLS), edges[0, f]),
+                (slice(COLS, 3 * COLS), centre[f]),
+                (slice(3 * COLS, 4 * COLS), edges[1, f]),
+            ):
+                ext[f, rows] = jnp.where(keep, value, jnp.zeros_like(value))
+
     weights = jnp.concatenate(
         [jnp.concatenate([taps_ref[0, b, e] for b in range(3)], axis=1) for e in range(3)], axis=0
     )
-    value = lax.dot_general(jnp.concatenate(rows, axis=0), weights, NT, preferred_element_type=F32)
-
-    @pl.when(a == 0)
+
+    def product(frames):
+        rows = []
+        for f in frames:
+            pieces = [ext[f, (2 - b) * COLS : (4 - b) * COLS] for b in range(3)]
+            rows.append(jnp.concatenate(pieces, axis=1))
+        value = rows[0] if len(rows) == 1 else jnp.concatenate(rows, axis=0)
+        return lax.dot_general(value, weights, NT, preferred_element_type=F32)
+
+    @pl.when(step == 0)
     def _():
-        side[...] = value
-
-    @pl.when(a == 1)
+        if lead is None:
+            side[...] = product((0, 1))
+        else:
+            side[...] = lead[...] + product((0, 1))
+
+    @pl.when(step == 1)
     def _():
-        side[...] += value
-
-    @pl.when(a == 2)
+        if lead is None:
+            side[: 2 * COLS] += product((1,))
+        else:
+            side[2 * COLS :] += product((0,))
+
+
+def first_input_kernel(centre, edges, taps_ref, side, ext):
+    input_products(centre, edges, taps_ref, side, ext, None, True)
+
+
+def last_input_kernel(y_ref, centre, edges, taps_ref, lead, features_ref, gamma_ref, out_ref, ext, side):
+    input_products(centre, edges, taps_ref, side, ext, lead, y_ref[0] != 3)
+
+    @pl.when(pl.program_id(0) == 1)
     def _():
         column = lax.broadcasted_iota(jnp.int32, (4 * COLS, C), 0) % COLS
-        side[...] += value
         grad_act = side[:, C : 2 * C]
         grad_act += jnp.where(column == COLS - 1, 0.0, pltpu.roll(side[:, :C], 4 * COLS - 1, 0))
         grad_act += jnp.where(column == 0, 0.0, pltpu.roll(side[:, 2 * C :], 1, 0))
@@ -212,31 +228,49 @@
         out_ref[...] = (inverse * (grad_norm - normed * inner)).astype(BF16)
 
 
-def input_gradient(y, own, following, up, dn, taps, features, gamma):
-    pixels = features.shape[0]
-    whole = lambda shape: pl.BlockSpec(shape, lambda a: (0,) * len(shape))
-    return pl.pallas_call(
-        input_kernel,
-        grid=(3,),
+def whole(*shape):
+    return pl.BlockSpec(shape, lambda step: (0,) * len(shape))
+
+
+def first_input(own, edges, taps):
+    return pl.pallas_call(
+        first_input_kernel,
+        grid=(2,),
+        in_specs=[
+            whole(2, 2 * COLS, C),
+            whole(2, 2, COLS, C),
+            pl.BlockSpec((1, 3, 3, C, C), lambda step: (2 - step, 0, 0, 0, 0)),
+        ],
+        out_specs=whole(4 * COLS, 3 * C),
+        out_shape=jax.ShapeDtypeStruct((4 * COLS, 3 * C), F32),
+        scratch_shapes=[pltpu.VMEM((2, 4 * COLS, C), BF16)],
+        compiler_params=pltpu.CompilerParams(vmem_limit_bytes=VMEM_SMALL),
+        cost_estimate=pl.CostEstimate(flops=27 * 640 * C * C, bytes_accessed=8_000_000, transcendentals=0),
+    )(own, edges, taps)
+
+
+def last_input(y, following, beyond, taps, lead, features, gamma):
+    return pl.pallas_call(
+        last_input_kernel,
+        grid=(2,),
         in_specs=[
             pl.BlockSpec(memory_space=pltpu.SMEM),
-            whole((2, 2 * COLS, C)),
-            whole((2, 2 * COLS, C)),
-            whole((4, COLS, C)),
-            whole((4, COLS, C)),
-            pl.BlockSpec((1, 3, 3, C, C), lambda a: (a, 0, 0, 0, 0)),
-            whole((pixels, C)),
-            whole((C,)),
+            whole(2, 2 * COLS, C),
+            whole(2, 2, COLS, C),
+            pl.BlockSpec((1, 3, 3, C, C), lambda step: (step, 0, 0, 0, 0)),
+            whole(4 * COLS, 3 * C),
+            whole(4 * COLS, C),
+            whole(C),
         ],
-        out_specs=whole((pixels, C)),
-        out_shape=jax.ShapeDtypeStruct((pixels, C), BF16),
+        out_specs=whole(4 * COLS, C),
+        out_shape=jax.ShapeDtypeStruct((4 * COLS, C), BF16),
         scratch_shapes=[
-            pltpu.VMEM((4, 4 * COLS, C), BF16),
-            pltpu.VMEM((pixels, 3 * C), F32),
+            pltpu.VMEM((2, 4 * COLS, C), BF16),
+            pltpu.VMEM((4 * COLS, 3 * C), F32),
         ],
-        compiler_params=pltpu.CompilerParams(vmem_limit_bytes=VMEM_LIMIT),
-        cost_estimate=pl.CostEstimate(flops=27 * 2 * 640 * C * C, bytes_accessed=12_000_000, transcendentals=0),
-    )(y, own, following, up, dn, taps, features, gamma)
+        compiler_params=pltpu.CompilerParams(vmem_limit_bytes=VMEM_SMALL),
+        cost_estimate=pl.CostEstimate(flops=27 * 640 * C * C, bytes_accessed=8_000_000, transcendentals=0),
+    )(y, following, beyond, taps, lead, features, gamma)
 
 
 def output_order(z, x, core, parts):
@@ -264,19 +298,15 @@
     local, *acts = lax.optimization_barrier((cotangent, *acts))
     following = lax.ppermute(local, "tm", y_shift(3))
     previous = lax.ppermute(local, "tm", y_shift(1))
-    rows_up, rows_dn = halo_rows(acts)
+    rows_up, rows_dn = halo_rows(acts, local)
     rows_up = lax.ppermute(rows_up, "rows", line(64, 1))
     rows_dn = lax.ppermute(rows_dn, "rows", line(64, -1))
+    edges = jnp.stack([rows_up[2:], rows_dn[2:]])
     far = [
         lax.ppermute(previous[0], "tm", y_shift(1)).reshape(pixels // 2, width),
         lax.ppermute(following[1], "tm", y_shift(3)).reshape(pixels // 2, width),
     ]
-    ext = jnp.concatenate([cotangent, following], axis=0)
-    cot_up = lax.ppermute(ext[:, 1], "rows", line(64, 1))
-    cot_dn = lax.ppermute(ext[:, 0], "rows", line(64, -1))
-    far, rows_up, rows_dn = lax.optimization_barrier((far, rows_up, rows_dn))
     spread = spread_windows(acts, rows_up, rows_dn)
-    orders[1], cot_up, cot_dn = lax.optimization_barrier((orders[1], cot_up, cot_dn))
     cots = [following.reshape(pixels, width), *far, previous.reshape(pixels, width), cotangent.reshape(pixels, width)]
 
     own, send = weight_partials(block, cots, spread, orders[0])
@@ -287,28 +317,29 @@
 
     early = [(own[48 * n : 48 * n + 48] + other[48 * n : 48 * n + 48]).astype(BF16) for n in range(2)]
     late = (own_2[:48] + other_2[:48]).astype(BF16)
-    block, *early = lax.optimization_barrier((block, *early))
+    edges, own_rows, *early = lax.optimization_barrier((edges, cotangent, *early))
     received = [lax.ppermute(value, "rows", x_shift(k)) for value, k in zip(early, groups[0])]
-    block, late = lax.optimization_barrier((block, late))
+    own_rows, late = lax.optimization_barrier((own_rows, late))
     received.append(lax.ppermute(late, "rows", x_shift(3)))
-    input_grad = input_gradient(
-        block,
-        cotangent.reshape(2, 2 * columns, width),
-        following.reshape(2, 2 * columns, width),
-        cot_up,
-        cot_dn,
-        taps,
-        flat,
-        gamma,
-    )
-    input_grad, *received = lax.optimization_barrier((input_grad, *received))
+    beyond = lax.ppermute(edges, "tm", y_shift(3))
+    lead = first_input(own_rows.reshape(2, 2 * columns, width), edges, taps)
+    lead, *received = lax.optimization_barrier((lead, *received))
     total = own_2[48:] + other_2[48:]
     for value in received:
         total = total + value.astype(F32)
     for bits in (1, 2, 6):
         half = total.shape[0] // 2
         pairs = rows_perm(lambda z, x, c: (z ^ bits, x, c))
-        total = total[:half] + lax.ppermute(total[half:].astype(BF16), "rows", pairs).astype(F32)
+        sent = total[half:].astype(BF16)
+        if bits == 1:
+            sent, block = lax.optimization_barrier((sent, block))
+        partner = lax.ppermute(sent, "rows", pairs)
+        if bits == 1:
+            input_grad = last_input(
+                block, following.reshape(2, 2 * columns, width), beyond, taps, lead, flat, gamma
+            )
+            input_grad, partner = lax.optimization_barrier((input_grad, partner))
+        total = total[:half] + partner.astype(F32)
     mine = total.reshape(6, 27, PART)
     count = pixels * lax.axis_size("tm") * lax.axis_size("rows")
     weight_grad = jnp.transpose(mine, (2, 1, 0)) * (1.0 / math.sqrt(count))

time: 91.7 us -> 90.5 us (0.987)
  the two profiles are of different devices: /device:TPU:6 before, /device:TPU:1 now
where the time goes in v4:
time: 90.5 us; the launch traced here: 90.3 us
  starting transfers between devices  34.1 us (38%)
  waiting for transfers between devices  29.1 us (32%)
  Pallas kernels  21.8 us (24%)
  local copies, waits for them, and re-layouts  3.7 us (4%)
  between operations  0.92 us (1%)
    pallas_call x2, Pallas kernels, weight_partials(): pl.pallas_call(weight_kernel, in_specs=[pl.BlockSpec(memory_space=pltpu.S...  9.79 us
    ppermute x3, waiting for transfers between devices, body(): partner = lax.ppermute(sent, 'rows', pairs)  9.59 us
    ppermute x3, starting transfers between devices, body(): partner = lax.ppermute(sent, 'rows', pairs)  7.32 us
    ppermute x3, starting transfers between devices, body(): lax.ppermute(active[k], 'tm', y_shift(k))  5.89 us
    pallas_call x1, Pallas kernels, last_input(): pl.pallas_call(last_input_kernel, grid=(2,), in_specs=[pl.BlockSpec(memor...  5.31 us
    ppermute x1, starting transfers between devices, body(): rows_up = lax.ppermute(rows_up, 'rows', line(64, 1))  5.11 us
    ppermute x3, waiting for transfers between devices, body(): lax.ppermute(active[k], 'tm', y_shift(k))  4.29 us
    ppermute x1, waiting for transfers between devices, body(): rows_dn = lax.ppermute(rows_dn, 'rows', line(64, -1))  4.16 us
  transfers between devices with their start and end apart: 18, of which 8 were waited for; matrix products, arithmetic and copies ran while one was open for 1% of the time, Pallas kernels for 18%

profile of v4, /device:TPU:1, one launch (start us, length us, event | category | flops | bytes accessed | tf_op | source)
XLA Modules:
  0.0 90.3 jit_solution(3361065315853322649)
XLA Ops:
  3.2 2.2 %collective-permute-start = (bf16[160,384]{1,0:T(8,128)(2,1)S(1)}, bf16[160,384]{1,0:T(8,128)(2,1)S(1)}, u32[]{:S(2)}, u32[]{:S(2)}) collective-permute-start(bf16[160,384]{1,0:T(8,128)(2,1)S(1)} %get-tuple-element.34), channel_id=1, source_target_pairs={{0,1},{1,2},{2,3},{3,0},{4,5},{5,6},{6,7},{7,4},{8,9},{9,10},{10,1... | collective-permute-start | bytes 368648 | tf_op jit(solution)/shard_map/ppermute | solution.py:297
  5.4 2.6 %collective-permute-start.1 = (bf16[160,384]{1,0:T(8,128)(2,1)S(1)}, bf16[160,384]{1,0:T(8,128)(2,1)S(1)}, u32[]{:S(2)}, u32[]{:S(2)}) collective-permute-start(bf16[160,384]{1,0:T(8,128)(2,1)S(1)} %get-tuple-element.35), channel_id=1, source_target_pairs={{0,2},{1,3},{2,0},{3,1},{4,6},{5,7},{6,4},{7,5},{8,10},{9,11},{10,... | collective-permute-start | bytes 368648 | tf_op jit(solution)/shard_map/ppermute | solution.py:297
  9.1 4.3 %collective-permute-done.1.a2 = bf16[160,384]{1,0:T(8,128)(2,1)S(1)} collective-permute-done((bf16[160,384]{1,0:T(8,128)(2,1)S(1)}, bf16[160,384]{1,0:T(8,128)(2,1)S(1)}, u32[]{:S(2)}, u32[]{:S(2)}) %collective-permute-start.1) | collective-permute-done | bytes 122912 | tf_op jit(solution)/shard_map/ppermute | solution.py:297
  13.4 2.7 %collective-permute-start.3 = (bf16[2,2,160,384]{3,2,1,0:T(8,128)(2,1)}, bf16[2,2,160,384]{3,2,1,0:T(8,128)(2,1)S(1)}, u32[]{:S(2)}, u32[]{:S(2)}) collective-permute-start(bf16[2,2,160,384]{3,2,1,0:T(8,128)(2,1)} %own), channel_id=1, source_target_pairs={{0,3},{1,0},{2,1},{3,2},{4,7},{5,4},{6,5},{7,6},{8,11},{9,8},{10,9... | collective-permute-start | bytes 1474568 | tf_op jit(solution)/shard_map/ppermute | solution.py:299
  17.5 5.1 %collective-permute-start.7 = (bf16[4,160,384]{2,1,0:T(8,128)(2,1)S(1)}, bf16[4,160,384]{2,1,0:T(8,128)(2,1)S(1)}, u32[]{:S(2)}, u32[]{:S(2)}) collective-permute-start(bf16[4,160,384]{2,1,0:T(8,128)(2,1)S(1)} %get-tuple-element.42), channel_id=1, source_target_pairs={{0,4},{4,8},{8,12},{12,16},{16,20},{20,24},{24,28},{28,32},{32,36}... | collective-permute-start | bytes 1474568 | tf_op jit(solution)/shard_map/ppermute | solution.py:302
  22.6 1.9 %collective-permute-start.8 = (bf16[4,160,384]{2,1,0:T(8,128)(2,1)S(1)}, bf16[4,160,384]{2,1,0:T(8,128)(2,1)S(1)}, u32[]{:S(2)}, u32[]{:S(2)}) collective-permute-start(bf16[4,160,384]{2,1,0:T(8,128)(2,1)S(1)} %get-tuple-element.43), channel_id=1, source_target_pairs={{4,0},{8,4},{12,8},{16,12},{20,16},{24,20},{28,24},{32,28},{36,32}... | collective-permute-start | bytes 1474568 | tf_op jit(solution)/shard_map/ppermute | solution.py:303
  24.6 1.2 %collective-permute-done.4 = bf16[2,2,160,384]{3,2,1,0:T(8,128)(2,1)S(1)} collective-permute-done((bf16[2,2,160,384]{3,2,1,0:T(8,128)(2,1)}, bf16[2,2,160,384]{3,2,1,0:T(8,128)(2,1)S(1)}, u32[]{:S(2)}, u32[]{:S(2)}) %collective-permute-start.4) | collective-permute-done | bytes 491552 | tf_op jit(solution)/shard_map/ppermute | solution.py:300
  25.9 2.9 %collective-permute-start.6 = (bf16[2,160,384]{2,1,0:T(8,128)(2,1)S(1)}, bf16[2,160,384]{2,1,0:T(8,128)(2,1)S(1)}, u32[]{:S(2)}, u32[]{:S(2)}) collective-permute-start(bf16[2,160,384]{2,1,0:T(8,128)(2,1)S(1)} %slice_bitcast_fusion.2), channel_id=1, source_target_pairs={{0,3},{1,0},{2,1},{3,2},{4,7},{5,4},{6,5},{7,6},{8,11},{9,8},{10,9... | collective-permute-start | bytes 737288 | tf_op jit(solution)/shard_map/ppermute | solution.py:307
  28.9 4.2 %collective-permute-done.8.dn = bf16[4,160,384]{2,1,0:T(8,128)(2,1)S(1)} collective-permute-done((bf16[4,160,384]{2,1,0:T(8,128)(2,1)S(1)}, bf16[4,160,384]{2,1,0:T(8,128)(2,1)S(1)}, u32[]{:S(2)}, u32[]{:S(2)}) %collective-permute-start.8) | collective-permute-done | bytes 491552 | tf_op jit(solution)/shard_map/ppermute | solution.py:303
  33.1 1.7 %shard_map.61.spread = bf16[3200,1152]{1,0:T(8,128)(2,1)S(1)} custom-call(bf16[160,384]{1,0:T(8,128)(2,1)S(1)} %get-tuple-element.38.a0, bf16[160,384]{1,0:T(8,128)(2,1)S(1)} %collective-permute-done.a1, bf16[160,384]{1,0:T(8,128)(2,1)S(1)} %collective-permute-done.1.a2, bf16[160,384]{1,0:T(8,128)(2,1)S(1)} %collective-permute-done.2.a3, ...), custom_call_target="tpu_custom_call" | custom-call | tf_op jit(solution)/shard_map/pallas_call | solution.py:116
  34.9 4.9 %shard_map.62 = (f32[96,2592]{1,0:T(8,128)S(1)}, f32[96,2592]{1,0:T(8,128)S(1)}) custom-call(s32[1]{0:T(128)} %bitcast.y_ref, bf16[640,384]{1,0:T(8,128)(2,1)S(1)} %bitcast.31, bf16[320,384]{1,0:T(8,128)(2,1)S(1)} %bitcast.36, bf16[320,384]{1,0:T(8,128)(2,1)S(1)} %bitcast.38, bf16[640,384]{1,0:T(8,128)(2,1)S(1)} %bitcast.34, bf16[640,384]{1,0:T(8,128)(2,1)S(1)} %bitcast.26, ...), custom_call_target="tpu_custom_call" | custom-call | flops 7046430720 | bytes 8000000 | tf_op jit(solution)/shard_map/pallas_call | solution.py:156
  39.8 1.2 %collective-permute-start.10 = (f32[96,2592]{1,0:T(8,128)S(1)}, f32[96,2592]{1,0:T(8,128)S(1)}, u32[]{:S(2)}, u32[]{:S(2)}) collective-permute-start(f32[96,2592]{1,0:T(8,128)S(1)} %get-tuple-element.49), channel_id=1, source_target_pairs={{0,4},{4,0},{8,12},{12,8},{16,20},{20,16},{24,28},{28,24},{32,36},... | collective-permute-start | bytes 2985992 | tf_op jit(solution)/shard_map/ppermute | solution.py:313
  41.0 4.9 %shard_map.63 = (f32[96,2592]{1,0:T(8,128)S(1)}, f32[96,2592]{1,0:T(8,128)S(1)}) custom-call(s32[1]{0:T(128)} %bitcast.y_ref, bf16[640,384]{1,0:T(8,128)(2,1)S(1)} %bitcast.32, bf16[320,384]{1,0:T(8,128)(2,1)S(1)} %bitcast.37, bf16[320,384]{1,0:T(8,128)(2,1)S(1)} %bitcast.39, bf16[640,384]{1,0:T(8,128)(2,1)S(1)} %bitcast.35, bf16[640,384]{1,0:T(8,128)(2,1)S(1)} %bitcast.27, ...), custom_call_target="tpu_custom_call" | custom-call | flops 7046430720 | bytes 8000000 | tf_op jit(solution)/shard_map/pallas_call | solution.py:156
  46.2 2.4 %collective-permute-done.9 = f32[96,2592]{1,0:T(8,128)S(1)} collective-permute-done((f32[96,2592]{1,0:T(8,128)S(1)}, f32[96,2592]{1,0:T(8,128)S(1)}, u32[]{:S(2)}, u32[]{:S(2)}) %collective-permute-start.9) | collective-permute-done | bytes 995360 | tf_op jit(solution)/shard_map/ppermute | solution.py:316
  48.7 3.7 %collective-permute-start.13 = (bf16[48,2592]{1,0:T(8,128)(2,1)S(1)}, bf16[48,2592]{1,0:T(8,128)(2,1)S(1)}, u32[]{:S(2)}, u32[]{:S(2)}) collective-permute-start(bf16[48,2592]{1,0:T(8,128)(2,1)S(1)} %fusion), channel_id=1, source_target_pairs={{0,24},{4,28},{8,0},{12,4},{16,8},{20,12},{24,16},{28,20},{32,56},... | collective-permute-start | bytes 746504 | tf_op jit(solution)/shard_map/ppermute | solution.py:323
  53.3 2.3 %collective-permute-start.14 = (bf16[2,2,160,384]{3,2,1,0:T(8,128)(2,1)S(1)}, bf16[2,2,160,384]{3,2,1,0:T(8,128)(2,1)S(1)}, u32[]{:S(2)}, u32[]{:S(2)}) collective-permute-start(bf16[2,2,160,384]{3,2,1,0:T(8,128)(2,1)S(1)} %pad_maximum_fusion.edges), channel_id=1, source_target_pairs={{0,3},{1,0},{2,1},{3,2},{4,7},{5,4},{6,5},{7,6},{8,11},{9,8},{10,9... | collective-permute-start | bytes 1474568 | tf_op jit(solution)/shard_map/ppermute | solution.py:324
  55.6 4.0 %shard_map.64.lead = f32[640,1152]{1,0:T(8,128)S(1)} custom-call(bf16[2,320,384]{2,1,0:T(8,128)(2,1)S(1)} %bitcast.28, bf16[2,2,160,384]{3,2,1,0:T(8,128)(2,1)S(1)} %pad_maximum_fusion.edges, bf16[3,3,3,384,384]{4,3,2,1,0:T(8,128)(2,1)S(1)} %bitcast.24), custom_call_target="tpu_custom_call" | custom-call | flops 2548039680 | bytes 8000000 | tf_op jit(solution)/shard_map/pallas_call | solution.py:236
  59.6 3.6 %collective-permute-done.13 = bf16[48,2592]{1,0:T(8,128)(2,1)S(1)} collective-permute-done((bf16[48,2592]{1,0:T(8,128)(2,1)S(1)}, bf16[48,2592]{1,0:T(8,128)(2,1)S(1)}, u32[]{:S(2)}, u32[]{:S(2)}) %collective-permute-start.13) | collective-permute-done | bytes 248864 | tf_op jit(solution)/shard_map/ppermute | solution.py:323
  63.2 3.8 %collective-permute-done.12 = bf16[48,2592]{1,0:T(8,128)(2,1)S(1)} collective-permute-done((bf16[48,2592]{1,0:T(8,128)(2,1)S(1)}, bf16[48,2592]{1,0:T(8,128)(2,1)S(1)}, u32[]{:S(2)}, u32[]{:S(2)}) %collective-permute-start.12) | collective-permute-done | bytes 248864 | tf_op jit(solution)/shard_map/ppermute | solution.py:321
  67.2 1.7 %collective-permute-start.15 = (bf16[24,2592]{1,0:T(8,128)(2,1)S(1)}, bf16[24,2592]{1,0:T(8,128)(2,1)S(1)}, u32[]{:S(2)}, u32[]{:S(2)}) collective-permute-start(bf16[24,2592]{1,0:T(8,128)(2,1)S(1)} %slice.121), channel_id=1, source_target_pairs={{0,32},{4,36},{8,40},{12,44},{16,48},{20,52},{24,56},{28,60},{32,0... | collective-permute-start | bytes 373256 | tf_op jit(solution)/shard_map/ppermute | solution.py:336
  68.9 5.3 %shard_map.65 = bf16[640,384]{1,0:T(8,128)(2,1)} custom-call(s32[1]{0:T(128)} %bitcast.y_ref, bf16[2,320,384]{2,1,0:T(8,128)(2,1)S(1)} %bitcast.33, bf16[2,2,160,384]{3,2,1,0:T(8,128)(2,1)S(1)} %collective-permute-done.14.edges, bf16[3,3,3,384,384]{4,3,2,1,0:T(8,128)(2,1)S(1)} %bitcast.25, f32[640,1152]{1,0:T(8,128)S(1)} %shard_map.64.lead, ...), custom_call_target="tpu_custom_call" | custom-call | flops 2548039680 | bytes 8000000 | tf_op jit(solution)/shard_map/pallas_call | solution.py:253
  74.3 5.5 %collective-permute-start.16 = (bf16[12,2592]{1,0:T(8,128)(2,1)S(1)}, bf16[12,2592]{1,0:T(8,128)(2,1)S(1)}, u32[]{:S(2)}, u32[]{:S(2)}) collective-permute-start(bf16[12,2592]{1,0:T(8,128)(2,1)S(1)} %slice.122), channel_id=1, source_target_pairs={{0,64},{4,68},{8,72},{12,76},{16,80},{20,84},{24,88},{28,92},{32,9... | collective-permute-start | bytes 186632 | tf_op jit(solution)/shard_map/ppermute | solution.py:336
  79.8 4.6 %collective-permute-done.16 = bf16[12,2592]{1,0:T(8,128)(2,1)S(1)} collective-permute-done((bf16[12,2592]{1,0:T(8,128)(2,1)S(1)}, bf16[12,2592]{1,0:T(8,128)(2,1)S(1)}, u32[]{:S(2)}, u32[]{:S(2)}) %collective-permute-start.16) | collective-permute-done | bytes 62240 | tf_op jit(solution)/shard_map/ppermute | solution.py:336
  84.5 5.0 %collective-permute-done.17 = bf16[6,2592]{1,0:T(8,128)(2,1)S(1)} collective-permute-done((bf16[6,2592]{1,0:T(8,128)(2,1)S(1)}, bf16[6,2592]{1,0:T(8,128)(2,1)S(1)}, u32[]{:S(2)}, u32[]{:S(2)}) %collective-permute-start.17) | collective-permute-done | bytes 31136 | tf_op jit(solution)/shard_map/ppermute | solution.py:336
  (54 shorter events, 7.7 us)
Async XLA Ops:
  0.6 34.2 %copy-start.1 = (bf16[2,2,160,384]{3,2,1,0:T(8,128)(2,1)S(1)}, bf16[2,2,160,384]{3,2,1,0:T(8,128)(2,1)}, u32[]{:S(2)}) copy-start(bf16[2,2,160,384]{3,2,1,0:T(8,128)(2,1)} %own) | copy-start | bytes 1474564
  0.6 1.1 %copy-start.2 = (bf16[2,2,160,384]{3,2,1,0:T(8,128)(2,1)S(1)}, bf16[2,2,160,384]{3,2,1,0:T(8,128)(2,1)}, u32[]{:S(2)}) copy-start(bf16[2,2,160,384]{3,2,1,0:T(8,128)(2,1)} %param.4) | copy-start | bytes 1474564
  3.2 5.9 %collective-permute-start = (bf16[160,384]{1,0:T(8,128)(2,1)S(1)}, bf16[160,384]{1,0:T(8,128)(2,1)S(1)}, u32[]{:S(2)}, u32[]{:S(2)}) collective-permute-start(bf16[160,384]{1,0:T(8,128)(2,1)S(1)} %get-tuple-element.34), channel_id=1, source_target_pairs={{0,1},{1,2},{2,3},{3,0},{4,5},{5,6},{6,7},{7,4},{8,9},{9,10},{10,1... | collective-permute-start | bytes 368648 | tf_op jit(solution)/shard_map/ppermute | solution.py:297
  5.4 8.0 %collective-permute-start.1 = (bf16[160,384]{1,0:T(8,128)(2,1)S(1)}, bf16[160,384]{1,0:T(8,128)(2,1)S(1)}, u32[]{:S(2)}, u32[]{:S(2)}) collective-permute-start(bf16[160,384]{1,0:T(8,128)(2,1)S(1)} %get-tuple-element.35), channel_id=1, source_target_pairs={{0,2},{1,3},{2,0},{3,1},{4,6},{5,7},{6,4},{7,5},{8,10},{9,11},{10,... | collective-permute-start | bytes 368648 | tf_op jit(solution)/shard_map/ppermute | solution.py:297
  8.0 5.4 %collective-permute-start.2 = (bf16[160,384]{1,0:T(8,128)(2,1)S(1)}, bf16[160,384]{1,0:T(8,128)(2,1)S(1)}, u32[]{:S(2)}, u32[]{:S(2)}) collective-permute-start(bf16[160,384]{1,0:T(8,128)(2,1)S(1)} %get-tuple-element.36), channel_id=1, source_target_pairs={{0,3},{1,0},{2,1},{3,2},{4,7},{5,4},{6,5},{7,6},{8,11},{9,8},{10,9... | collective-permute-start | bytes 368648 | tf_op jit(solution)/shard_map/ppermute | solution.py:297
  13.4 12.3 %collective-permute-start.4 = (bf16[2,2,160,384]{3,2,1,0:T(8,128)(2,1)}, bf16[2,2,160,384]{3,2,1,0:T(8,128)(2,1)S(1)}, u32[]{:S(2)}, u32[]{:S(2)}) collective-permute-start(bf16[2,2,160,384]{3,2,1,0:T(8,128)(2,1)} %own), channel_id=1, source_target_pairs={{0,1},{1,2},{2,3},{3,0},{4,5},{5,6},{6,7},{7,4},{8,9},{9,10},{10,1... | collective-permute-start | bytes 1474568 | tf_op jit(solution)/shard_map/ppermute | solution.py:300
  13.4 12.5 %collective-permute-start.3 = (bf16[2,2,160,384]{3,2,1,0:T(8,128)(2,1)}, bf16[2,2,160,384]{3,2,1,0:T(8,128)(2,1)S(1)}, u32[]{:S(2)}, u32[]{:S(2)}) collective-permute-start(bf16[2,2,160,384]{3,2,1,0:T(8,128)(2,1)} %own), channel_id=1, source_target_pairs={{0,3},{1,0},{2,1},{3,2},{4,7},{5,4},{6,5},{7,6},{8,11},{9,8},{10,9... | collective-permute-start | bytes 1474568 | tf_op jit(solution)/shard_map/ppermute | solution.py:299
  17.5 11.4 %collective-permute-start.7 = (bf16[4,160,384]{2,1,0:T(8,128)(2,1)S(1)}, bf16[4,160,384]{2,1,0:T(8,128)(2,1)S(1)}, u32[]{:S(2)}, u32[]{:S(2)}) collective-permute-start(bf16[4,160,384]{2,1,0:T(8,128)(2,1)S(1)} %get-tuple-element.42), channel_id=1, source_target_pairs={{0,4},{4,8},{8,12},{12,16},{16,20},{20,24},{24,28},{28,32},{32,36}... | collective-permute-start | bytes 1474568 | tf_op jit(solution)/shard_map/ppermute | solution.py:302
  22.6 10.4 %collective-permute-start.8 = (bf16[4,160,384]{2,1,0:T(8,128)(2,1)S(1)}, bf16[4,160,384]{2,1,0:T(8,128)(2,1)S(1)}, u32[]{:S(2)}, u32[]{:S(2)}) collective-permute-start(bf16[4,160,384]{2,1,0:T(8,128)(2,1)S(1)} %get-tuple-element.43), channel_id=1, source_target_pairs={{4,0},{8,4},{12,8},{16,12},{20,16},{24,20},{28,24},{32,28},{36,32}... | collective-permute-start | bytes 1474568 | tf_op jit(solution)/shard_map/ppermute | solution.py:303
  25.8 9.1 %collective-permute-start.5 = (bf16[2,160,384]{2,1,0:T(8,128)(2,1)S(1)}, bf16[2,160,384]{2,1,0:T(8,128)(2,1)S(1)}, u32[]{:S(2)}, u32[]{:S(2)}) collective-permute-start(bf16[2,160,384]{2,1,0:T(8,128)(2,1)S(1)} %slice_bitcast_fusion.3), channel_id=1, source_target_pairs={{0,1},{1,2},{2,3},{3,0},{4,5},{5,6},{6,7},{7,4},{8,9},{9,10},{10,1... | collective-permute-start | bytes 737288 | tf_op jit(solution)/shard_map/ppermute | solution.py:306
  25.9 8.9 %collective-permute-start.6 = (bf16[2,160,384]{2,1,0:T(8,128)(2,1)S(1)}, bf16[2,160,384]{2,1,0:T(8,128)(2,1)S(1)}, u32[]{:S(2)}, u32[]{:S(2)}) collective-permute-start(bf16[2,160,384]{2,1,0:T(8,128)(2,1)S(1)} %slice_bitcast_fusion.2), channel_id=1, source_target_pairs={{0,3},{1,0},{2,1},{3,2},{4,7},{5,4},{6,5},{7,6},{8,11},{9,8},{10,9... | collective-permute-start | bytes 737288 | tf_op jit(solution)/shard_map/ppermute | solution.py:307
  34.9 20.7 %slice-start = ((s8[7962624]{0:T(1024)(128)(4,1)}), s8[4194304]{0:T(1024)(128)(4,1)S(1)}, s32[]{:S(2)}) async-start(s8[7962624]{0:T(1024)(128)(4,1)} %bitcast.22), calls=%async_computation | async-start | bytes 8388608
  39.8 15.8 %slice-start.1 = ((s8[7962624]{0:T(1024)(128)(4,1)}), s8[3768320]{0:T(1024)(128)(4,1)S(1)}, s32[]{:S(2)}) async-start(s8[7962624]{0:T(1024)(128)(4,1)} %bitcast.22), calls=%async_computation.1 | async-start | bytes 7536640
  39.8 6.3 %collective-permute-start.10 = (f32[96,2592]{1,0:T(8,128)S(1)}, f32[96,2592]{1,0:T(8,128)S(1)}, u32[]{:S(2)}, u32[]{:S(2)}) collective-permute-start(f32[96,2592]{1,0:T(8,128)S(1)} %get-tuple-element.49), channel_id=1, source_target_pairs={{0,4},{4,0},{8,12},{12,8},{16,20},{20,16},{24,28},{28,24},{32,36},... | collective-permute-start | bytes 2985992 | tf_op jit(solution)/shard_map/ppermute | solution.py:313
  45.9 2.7 %collective-permute-start.9 = (f32[96,2592]{1,0:T(8,128)S(1)}, f32[96,2592]{1,0:T(8,128)S(1)}, u32[]{:S(2)}, u32[]{:S(2)}) collective-permute-start(f32[96,2592]{1,0:T(8,128)S(1)} %get-tuple-element.47), channel_id=1, source_target_pairs={{0,4},{4,0},{8,12},{12,8},{16,20},{20,16},{24,28},{28,24},{32,36},... | collective-permute-start | bytes 2985992 | tf_op jit(solution)/shard_map/ppermute | solution.py:316
  48.6 20.3 %copy-start.3 = (bf16[2,2,160,384]{3,2,1,0:T(8,128)(2,1)S(1)}, bf16[2,2,160,384]{3,2,1,0:T(8,128)(2,1)}, u32[]{:S(2)}) copy-start(bf16[2,2,160,384]{3,2,1,0:T(8,128)(2,1)} %param.4) | copy-start | bytes 1474564
  48.7 20.3 %copy-start.5 = (f32[384]{0:T(512)S(1)}, f32[384]{0:T(512)}, u32[]{:S(2)}) copy-start(f32[384]{0:T(512)} %gamma_ref.3) | copy-start | bytes 4612
  48.7 14.5 %collective-permute-start.13 = (bf16[48,2592]{1,0:T(8,128)(2,1)S(1)}, bf16[48,2592]{1,0:T(8,128)(2,1)S(1)}, u32[]{:S(2)}, u32[]{:S(2)}) collective-permute-start(bf16[48,2592]{1,0:T(8,128)(2,1)S(1)} %fusion), channel_id=1, source_target_pairs={{0,24},{4,28},{8,0},{12,4},{16,8},{20,12},{24,16},{28,20},{32,56},... | collective-permute-start | bytes 746504 | tf_op jit(solution)/shard_map/ppermute | solution.py:323
  52.4 10.8 %collective-permute-start.11 = (bf16[48,2592]{1,0:T(8,128)(2,1)S(1)}, bf16[48,2592]{1,0:T(8,128)(2,1)S(1)}, u32[]{:S(2)}, u32[]{:S(2)}) collective-permute-start(bf16[48,2592]{1,0:T(8,128)(2,1)S(1)} %get-tuple-element.53), channel_id=1, source_target_pairs={{0,16},{4,20},{8,24},{12,28},{16,0},{20,4},{24,8},{28,12},{32,48},... | collective-permute-start | bytes 746504 | tf_op jit(solution)/shard_map/ppermute | solution.py:321
  52.4 14.6 %collective-permute-start.12 = (bf16[48,2592]{1,0:T(8,128)(2,1)S(1)}, bf16[48,2592]{1,0:T(8,128)(2,1)S(1)}, u32[]{:S(2)}, u32[]{:S(2)}) collective-permute-start(bf16[48,2592]{1,0:T(8,128)(2,1)S(1)} %get-tuple-element.54), channel_id=1, source_target_pairs={{0,8},{4,12},{8,16},{12,20},{16,24},{20,28},{24,0},{28,4},{32,40},... | collective-permute-start | bytes 746504 | tf_op jit(solution)/shard_map/ppermute | solution.py:321
  53.3 15.6 %collective-permute-start.14 = (bf16[2,2,160,384]{3,2,1,0:T(8,128)(2,1)S(1)}, bf16[2,2,160,384]{3,2,1,0:T(8,128)(2,1)S(1)}, u32[]{:S(2)}, u32[]{:S(2)}) collective-permute-start(bf16[2,2,160,384]{3,2,1,0:T(8,128)(2,1)S(1)} %pad_maximum_fusion.edges), channel_id=1, source_target_pairs={{0,3},{1,0},{2,1},{3,2},{4,7},{5,4},{6,5},{7,6},{8,11},{9,8},{10,9... | collective-permute-start | bytes 1474568 | tf_op jit(solution)/shard_map/ppermute | solution.py:324
  67.2 7.0 %collective-permute-start.15 = (bf16[24,2592]{1,0:T(8,128)(2,1)S(1)}, bf16[24,2592]{1,0:T(8,128)(2,1)S(1)}, u32[]{:S(2)}, u32[]{:S(2)}) collective-permute-start(bf16[24,2592]{1,0:T(8,128)(2,1)S(1)} %slice.121), channel_id=1, source_target_pairs={{0,32},{4,36},{8,40},{12,44},{16,48},{20,52},{24,56},{28,60},{32,0... | collective-permute-start | bytes 373256 | tf_op jit(solution)/shard_map/ppermute | solution.py:336
  74.3 10.1 %collective-permute-start.16 = (bf16[12,2592]{1,0:T(8,128)(2,1)S(1)}, bf16[12,2592]{1,0:T(8,128)(2,1)S(1)}, u32[]{:S(2)}, u32[]{:S(2)}) collective-permute-start(bf16[12,2592]{1,0:T(8,128)(2,1)S(1)} %slice.122), channel_id=1, source_target_pairs={{0,64},{4,68},{8,72},{12,76},{16,80},{20,84},{24,88},{28,92},{32,9... | collective-permute-start | bytes 186632 | tf_op jit(solution)/shard_map/ppermute | solution.py:336
  84.4 5.1 %collective-permute-start.17 = (bf16[6,2592]{1,0:T(8,128)(2,1)S(1)}, bf16[6,2592]{1,0:T(8,128)(2,1)S(1)}, u32[]{:S(2)}, u32[]{:S(2)}) collective-permute-start(bf16[6,2592]{1,0:T(8,128)(2,1)S(1)} %slice.123), channel_id=1, source_target_pairs={{0,192},{4,196},{8,200},{12,204},{16,208},{20,212},{24,216},{28,22... | collective-permute-start | bytes 93320 | tf_op jit(solution)/shard_map/ppermute | solution.py:336
  (2 other events, 1.7 us)

commit v5 on v4

--- a/solution.py
+++ b/solution.py
@@ -171,9 +171,9 @@
     def _():
         for f in range(2):
             for rows, value in (
-                (slice(0, COLS), edges[0, f]),
+                (slice(0, COLS), edges[0, f] if lead is None else jnp.zeros_like(centre[f, :COLS])),
                 (slice(COLS, 3 * COLS), centre[f]),
-                (slice(3 * COLS, 4 * COLS), edges[1, f]),
+                (slice(3 * COLS, 4 * COLS), edges[1, f] if lead is None else jnp.zeros_like(centre[f, :COLS])),
             ):
                 ext[f, rows] = jnp.where(keep, value, jnp.zeros_like(value))
 
@@ -208,8 +208,48 @@
     input_products(centre, edges, taps_ref, side, ext, None, True)
 
 
-def last_input_kernel(y_ref, centre, edges, taps_ref, lead, features_ref, gamma_ref, out_ref, ext, side):
-    input_products(centre, edges, taps_ref, side, ext, lead, y_ref[0] != 3)
+def middle_input_kernel(y_ref, centre, taps_ref, lead, side, ext):
+    input_products(centre, None, taps_ref, side, ext, lead, y_ref[0] != 3)
+
+
+def middle_input(y, following, taps, lead):
+    return pl.pallas_call(
+        middle_input_kernel,
+        grid=(2,),
+        in_specs=[
+            pl.BlockSpec(memory_space=pltpu.SMEM),
+            whole(2, 2 * COLS, C),
+            pl.BlockSpec((1, 3, 3, C, C), lambda step: (step, 0, 0, 0, 0)),
+            whole(4 * COLS, 3 * C),
+        ],
+        out_specs=whole(4 * COLS, 3 * C),
+        out_shape=jax.ShapeDtypeStruct((4 * COLS, 3 * C), F32),
+        scratch_shapes=[pltpu.VMEM((2, 4 * COLS, C), BF16)],
+        compiler_params=pltpu.CompilerParams(vmem_limit_bytes=VMEM_SMALL),
+        cost_estimate=pl.CostEstimate(flops=27 * 640 * C * C, bytes_accessed=8_000_000, transcendentals=0),
+    )(y, following, taps, lead)
+
+
+def last_input_kernel(y_ref, edges, taps_ref, lead, features_ref, gamma_ref, out_ref, side):
+    keep = y_ref[0] != 3
+
+    def add(f, frame):
+        for h, b in ((0, 2), (1, 0)):
+            value = edges[h, frame]
+            value = jnp.where(keep, value, jnp.zeros_like(value))
+            weights = jnp.concatenate([taps_ref[0, b, e] for e in range(3)], axis=0)
+            rows = slice((f * 2 + h) * COLS, (f * 2 + h + 1) * COLS)
+            side[rows] += lax.dot_general(value, weights, NT, preferred_element_type=F32)
+
+    @pl.when(pl.program_id(0) == 0)
+    def _():
+        side[...] = lead[...]
+        add(0, 0)
+        add(1, 1)
+
+    @pl.when(pl.program_id(0) == 1)
+    def _():
+        add(1, 0)
 
     @pl.when(pl.program_id(0) == 1)
     def _():
@@ -249,13 +289,12 @@
     )(own, edges, taps)
 
 
-def last_input(y, following, beyond, taps, lead, features, gamma):
+def last_input(y, beyond, taps, lead, features, gamma):
     return pl.pallas_call(
         last_input_kernel,
         grid=(2,),
         in_specs=[
             pl.BlockSpec(memory_space=pltpu.SMEM),
-            whole(2, 2 * COLS, C),
             whole(2, 2, COLS, C),
             pl.BlockSpec((1, 3, 3, C, C), lambda step: (step, 0, 0, 0, 0)),
             whole(4 * COLS, 3 * C),
@@ -265,12 +304,11 @@
         out_specs=whole(4 * COLS, C),
         out_shape=jax.ShapeDtypeStruct((4 * COLS, C), BF16),
         scratch_shapes=[
-            pltpu.VMEM((2, 4 * COLS, C), BF16),
             pltpu.VMEM((4 * COLS, 3 * C), F32),
         ],
         compiler_params=pltpu.CompilerParams(vmem_limit_bytes=VMEM_SMALL),
         cost_estimate=pl.CostEstimate(flops=27 * 640 * C * C, bytes_accessed=8_000_000, transcendentals=0),
-    )(y, following, beyond, taps, lead, features, gamma)
+    )(y, beyond, taps, lead, features, gamma)
 
 
 def output_order(z, x, core, parts):
@@ -323,6 +361,7 @@
     received.append(lax.ppermute(late, "rows", x_shift(3)))
     beyond = lax.ppermute(edges, "tm", y_shift(3))
     lead = first_input(own_rows.reshape(2, 2 * columns, width), edges, taps)
+    lead = middle_input(block, following.reshape(2, 2 * columns, width), taps, lead)
     lead, *received = lax.optimization_barrier((lead, *received))
     total = own_2[48:] + other_2[48:]
     for value in received:
@@ -336,7 +375,7 @@
         partner = lax.ppermute(sent, "rows", pairs)
         if bits == 1:
             input_grad = last_input(
-                block, following.reshape(2, 2 * columns, width), beyond, taps, lead, flat, gamma
+                block, beyond, taps, lead, flat, gamma
             )
             input_grad, partner = lax.optimization_barrier((input_grad, partner))
         total = total[:half] + partner.astype(F32)

time: 90.5 us -> 89.2 us (0.986)
  waiting for transfers between devices: 29.1 us -> 25 us
  Pallas kernels: 21.8 us -> 24.6 us
    pallas_call x0 -> x1, Pallas kernels: none -> 4.05 us  [middle_input(): pl.pallas_call(middle_input_kernel, grid=(2,), in_specs=[pl.BlockSpec(mem...]
    ppermute x1, waiting for transfers between devices: 3.6 us -> 0.01 us  [body(): received.append(lax.ppermute(late, 'rows', x_shift(3)))]
    pallas_call x1, Pallas kernels: 5.31 us -> 3.68 us  [last_input(): pl.pallas_call(last_input_kernel, grid=(2,), in_specs=[pl.BlockSpec(memor...]
  transfers between devices with their start and end apart: 18 -> 18, of which waited for: 8 -> 7; matrix products, arithmetic and copies ran while one was open for 1% -> 1% of each run, Pallas kernels for 18% -> 21%
where the time goes in v5:
time: 89.2 us; the launch traced here: 89 us
  starting transfers between devices  34.1 us (38%)
  waiting for transfers between devices  25 us (28%)
  Pallas kernels  24.6 us (28%)
  local copies, waits for them, and re-layouts  3.7 us (4%)
  between operations  0.93 us (1%)
    pallas_call x2, Pallas kernels, weight_partials(): pl.pallas_call(weight_kernel, in_specs=[pl.BlockSpec(memory_space=pltpu.S...  10.1 us
    ppermute x3, waiting for transfers between devices, body(): partner = lax.ppermute(sent, 'rows', pairs)  9.62 us
    ppermute x3, starting transfers between devices, body(): partner = lax.ppermute(sent, 'rows', pairs)  7.31 us
    ppermute x3, starting transfers between devices, body(): lax.ppermute(active[k], 'tm', y_shift(k))  5.89 us
    ppermute x1, starting transfers between devices, body(): rows_up = lax.ppermute(rows_up, 'rows', line(64, 1))  5.11 us
    ppermute x3, waiting for transfers between devices, body(): lax.ppermute(active[k], 'tm', y_shift(k))  4.29 us
    ppermute x1, waiting for transfers between devices, body(): rows_dn = lax.ppermute(rows_dn, 'rows', line(64, -1))  4.16 us
    pallas_call x1, Pallas kernels, middle_input(): pl.pallas_call(middle_input_kernel, grid=(2,), in_specs=[pl.BlockSpec(mem...  4.05 us
  transfers between devices with their start and end apart: 18, of which 7 were waited for; matrix products, arithmetic and copies ran while one was open for 1% of the time, Pallas kernels for 21%

profile of v5, /device:TPU:1, one launch (start us, length us, event | category | flops | bytes accessed | tf_op | source)
XLA Modules:
  0.0 89.0 jit_solution(1936354502491700992)
XLA Ops:
  3.2 2.2 %collective-permute-start = (bf16[160,384]{1,0:T(8,128)(2,1)S(1)}, bf16[160,384]{1,0:T(8,128)(2,1)S(1)}, u32[]{:S(2)}, u32[]{:S(2)}) collective-permute-start(bf16[160,384]{1,0:T(8,128)(2,1)S(1)} %get-tuple-element.34), channel_id=1, source_target_pairs={{0,1},{1,2},{2,3},{3,0},{4,5},{5,6},{6,7},{7,4},{8,9},{9,10},{10,1... | collective-permute-start | bytes 368648 | tf_op jit(solution)/shard_map/ppermute | solution.py:335
  5.4 2.6 %collective-permute-start.1 = (bf16[160,384]{1,0:T(8,128)(2,1)S(1)}, bf16[160,384]{1,0:T(8,128)(2,1)S(1)}, u32[]{:S(2)}, u32[]{:S(2)}) collective-permute-start(bf16[160,384]{1,0:T(8,128)(2,1)S(1)} %get-tuple-element.35), channel_id=1, source_target_pairs={{0,2},{1,3},{2,0},{3,1},{4,6},{5,7},{6,4},{7,5},{8,10},{9,11},{10,... | collective-permute-start | bytes 368648 | tf_op jit(solution)/shard_map/ppermute | solution.py:335
  9.1 4.3 %collective-permute-done.1.a2 = bf16[160,384]{1,0:T(8,128)(2,1)S(1)} collective-permute-done((bf16[160,384]{1,0:T(8,128)(2,1)S(1)}, bf16[160,384]{1,0:T(8,128)(2,1)S(1)}, u32[]{:S(2)}, u32[]{:S(2)}) %collective-permute-start.1) | collective-permute-done | bytes 122912 | tf_op jit(solution)/shard_map/ppermute | solution.py:335
  13.4 2.7 %collective-permute-start.3 = (bf16[2,2,160,384]{3,2,1,0:T(8,128)(2,1)}, bf16[2,2,160,384]{3,2,1,0:T(8,128)(2,1)S(1)}, u32[]{:S(2)}, u32[]{:S(2)}) collective-permute-start(bf16[2,2,160,384]{3,2,1,0:T(8,128)(2,1)} %own), channel_id=1, source_target_pairs={{0,3},{1,0},{2,1},{3,2},{4,7},{5,4},{6,5},{7,6},{8,11},{9,8},{10,9... | collective-permute-start | bytes 1474568 | tf_op jit(solution)/shard_map/ppermute | solution.py:337
  17.5 5.1 %collective-permute-start.7 = (bf16[4,160,384]{2,1,0:T(8,128)(2,1)S(1)}, bf16[4,160,384]{2,1,0:T(8,128)(2,1)S(1)}, u32[]{:S(2)}, u32[]{:S(2)}) collective-permute-start(bf16[4,160,384]{2,1,0:T(8,128)(2,1)S(1)} %get-tuple-element.42), channel_id=1, source_target_pairs={{0,4},{4,8},{8,12},{12,16},{16,20},{20,24},{24,28},{28,32},{32,36}... | collective-permute-start | bytes 1474568 | tf_op jit(solution)/shard_map/ppermute | solution.py:340
  22.6 1.9 %collective-permute-start.8 = (bf16[4,160,384]{2,1,0:T(8,128)(2,1)S(1)}, bf16[4,160,384]{2,1,0:T(8,128)(2,1)S(1)}, u32[]{:S(2)}, u32[]{:S(2)}) collective-permute-start(bf16[4,160,384]{2,1,0:T(8,128)(2,1)S(1)} %get-tuple-element.43), channel_id=1, source_target_pairs={{4,0},{8,4},{12,8},{16,12},{20,16},{24,20},{28,24},{32,28},{36,32}... | collective-permute-start | bytes 1474568 | tf_op jit(solution)/shard_map/ppermute | solution.py:341
  24.6 1.2 %collective-permute-done.4 = bf16[2,2,160,384]{3,2,1,0:T(8,128)(2,1)S(1)} collective-permute-done((bf16[2,2,160,384]{3,2,1,0:T(8,128)(2,1)}, bf16[2,2,160,384]{3,2,1,0:T(8,128)(2,1)S(1)}, u32[]{:S(2)}, u32[]{:S(2)}) %collective-permute-start.4) | collective-permute-done | bytes 491552 | tf_op jit(solution)/shard_map/ppermute | solution.py:338
  25.9 2.9 %collective-permute-start.6 = (bf16[2,160,384]{2,1,0:T(8,128)(2,1)S(1)}, bf16[2,160,384]{2,1,0:T(8,128)(2,1)S(1)}, u32[]{:S(2)}, u32[]{:S(2)}) collective-permute-start(bf16[2,160,384]{2,1,0:T(8,128)(2,1)S(1)} %slice_bitcast_fusion.2), channel_id=1, source_target_pairs={{0,3},{1,0},{2,1},{3,2},{4,7},{5,4},{6,5},{7,6},{8,11},{9,8},{10,9... | collective-permute-start | bytes 737288 | tf_op jit(solution)/shard_map/ppermute | solution.py:345
  28.9 4.2 %collective-permute-done.8.dn = bf16[4,160,384]{2,1,0:T(8,128)(2,1)S(1)} collective-permute-done((bf16[4,160,384]{2,1,0:T(8,128)(2,1)S(1)}, bf16[4,160,384]{2,1,0:T(8,128)(2,1)S(1)}, u32[]{:S(2)}, u32[]{:S(2)}) %collective-permute-start.8) | collective-permute-done | bytes 491552 | tf_op jit(solution)/shard_map/ppermute | solution.py:341
  33.1 1.7 %shard_map.61.spread = bf16[3200,1152]{1,0:T(8,128)(2,1)S(1)} custom-call(bf16[160,384]{1,0:T(8,128)(2,1)S(1)} %get-tuple-element.38.a0, bf16[160,384]{1,0:T(8,128)(2,1)S(1)} %collective-permute-done.a1, bf16[160,384]{1,0:T(8,128)(2,1)S(1)} %collective-permute-done.1.a2, bf16[160,384]{1,0:T(8,128)(2,1)S(1)} %collective-permute-done.2.a3, ...), custom_call_target="tpu_custom_call" | custom-call | tf_op jit(solution)/shard_map/pallas_call | solution.py:116
  34.9 5.1 %shard_map.62 = (f32[96,2592]{1,0:T(8,128)S(1)}, f32[96,2592]{1,0:T(8,128)S(1)}) custom-call(s32[1]{0:T(128)} %bitcast.y_ref, bf16[640,384]{1,0:T(8,128)(2,1)S(1)} %bitcast.32, bf16[320,384]{1,0:T(8,128)(2,1)S(1)} %bitcast.37, bf16[320,384]{1,0:T(8,128)(2,1)S(1)} %bitcast.39, bf16[640,384]{1,0:T(8,128)(2,1)S(1)} %bitcast.35, bf16[640,384]{1,0:T(8,128)(2,1)S(1)} %bitcast.27, ...), custom_call_target="tpu_custom_call" | custom-call | flops 7046430720 | bytes 8000000 | tf_op jit(solution)/shard_map/pallas_call | solution.py:156
  40.0 1.2 %collective-permute-start.10 = (f32[96,2592]{1,0:T(8,128)S(1)}, f32[96,2592]{1,0:T(8,128)S(1)}, u32[]{:S(2)}, u32[]{:S(2)}) collective-permute-start(f32[96,2592]{1,0:T(8,128)S(1)} %get-tuple-element.49), channel_id=1, source_target_pairs={{0,4},{4,0},{8,12},{12,8},{16,20},{20,16},{24,28},{28,24},{32,36},... | collective-permute-start | bytes 2985992 | tf_op jit(solution)/shard_map/ppermute | solution.py:351
  41.1 5.1 %shard_map.63 = (f32[96,2592]{1,0:T(8,128)S(1)}, f32[96,2592]{1,0:T(8,128)S(1)}) custom-call(s32[1]{0:T(128)} %bitcast.y_ref, bf16[640,384]{1,0:T(8,128)(2,1)S(1)} %bitcast.33, bf16[320,384]{1,0:T(8,128)(2,1)S(1)} %bitcast.38, bf16[320,384]{1,0:T(8,128)(2,1)S(1)} %bitcast.40, bf16[640,384]{1,0:T(8,128)(2,1)S(1)} %bitcast.36, bf16[640,384]{1,0:T(8,128)(2,1)S(1)} %bitcast.28, ...), custom_call_target="tpu_custom_call" | custom-call | flops 7046430720 | bytes 8000000 | tf_op jit(solution)/shard_map/pallas_call | solution.py:156
  46.5 2.4 %collective-permute-done.9 = f32[96,2592]{1,0:T(8,128)S(1)} collective-permute-done((f32[96,2592]{1,0:T(8,128)S(1)}, f32[96,2592]{1,0:T(8,128)S(1)}, u32[]{:S(2)}, u32[]{:S(2)}) %collective-permute-start.9) | collective-permute-done | bytes 995360 | tf_op jit(solution)/shard_map/ppermute | solution.py:354
  49.0 3.8 %collective-permute-start.13 = (bf16[48,2592]{1,0:T(8,128)(2,1)S(1)}, bf16[48,2592]{1,0:T(8,128)(2,1)S(1)}, u32[]{:S(2)}, u32[]{:S(2)}) collective-permute-start(bf16[48,2592]{1,0:T(8,128)(2,1)S(1)} %fusion), channel_id=1, source_target_pairs={{0,24},{4,28},{8,0},{12,4},{16,8},{20,12},{24,16},{28,20},{32,56},... | collective-permute-start | bytes 746504 | tf_op jit(solution)/shard_map/ppermute | solution.py:361
  53.7 2.3 %collective-permute-start.14 = (bf16[2,2,160,384]{3,2,1,0:T(8,128)(2,1)S(1)}, bf16[2,2,160,384]{3,2,1,0:T(8,128)(2,1)S(1)}, u32[]{:S(2)}, u32[]{:S(2)}) collective-permute-start(bf16[2,2,160,384]{3,2,1,0:T(8,128)(2,1)S(1)} %pad_maximum_fusion.edges), channel_id=1, source_target_pairs={{0,3},{1,0},{2,1},{3,2},{4,7},{5,4},{6,5},{7,6},{8,11},{9,8},{10,9... | collective-permute-start | bytes 1474568 | tf_op jit(solution)/shard_map/ppermute | solution.py:362
  55.9 4.0 %shard_map.64.lead = f32[640,1152]{1,0:T(8,128)S(1)} custom-call(bf16[2,320,384]{2,1,0:T(8,128)(2,1)S(1)} %bitcast.29, bf16[2,2,160,384]{3,2,1,0:T(8,128)(2,1)S(1)} %pad_maximum_fusion.edges, bf16[3,3,3,384,384]{4,3,2,1,0:T(8,128)(2,1)S(1)} %bitcast.24), custom_call_target="tpu_custom_call" | custom-call | flops 2548039680 | bytes 8000000 | tf_op jit(solution)/shard_map/pallas_call | solution.py:276
  60.0 4.1 %shard_map.65.lead = f32[640,1152]{1,0:T(8,128)S(1)} custom-call(s32[1]{0:T(128)} %bitcast.y_ref, bf16[2,320,384]{2,1,0:T(8,128)(2,1)S(1)} %bitcast.34, bf16[3,3,3,384,384]{4,3,2,1,0:T(8,128)(2,1)S(1)} %bitcast.25, f32[640,1152]{1,0:T(8,128)S(1)} %shard_map.64.lead), custom_call_target="tpu_custom_call" | custom-call | flops 2548039680 | bytes 8000000 | tf_op jit(solution)/shard_map/pallas_call | solution.py:216
  64.1 3.3 %collective-permute-done.12 = bf16[48,2592]{1,0:T(8,128)(2,1)S(1)} collective-permute-done((bf16[48,2592]{1,0:T(8,128)(2,1)S(1)}, bf16[48,2592]{1,0:T(8,128)(2,1)S(1)}, u32[]{:S(2)}, u32[]{:S(2)}) %collective-permute-start.12) | collective-permute-done | bytes 248864 | tf_op jit(solution)/shard_map/ppermute | solution.py:359
  67.5 1.7 %collective-permute-start.15 = (bf16[24,2592]{1,0:T(8,128)(2,1)S(1)}, bf16[24,2592]{1,0:T(8,128)(2,1)S(1)}, u32[]{:S(2)}, u32[]{:S(2)}) collective-permute-start(bf16[24,2592]{1,0:T(8,128)(2,1)S(1)} %slice.121), channel_id=1, source_target_pairs={{0,32},{4,36},{8,40},{12,44},{16,48},{20,52},{24,56},{28,60},{32,0... | collective-permute-start | bytes 373256 | tf_op jit(solution)/shard_map/ppermute | solution.py:375
  69.3 3.7 %shard_map.66 = bf16[640,384]{1,0:T(8,128)(2,1)} custom-call(s32[1]{0:T(128)} %bitcast.y_ref, bf16[2,2,160,384]{3,2,1,0:T(8,128)(2,1)S(1)} %collective-permute-done.14.edges, bf16[3,3,3,384,384]{4,3,2,1,0:T(8,128)(2,1)S(1)} %bitcast.26, f32[640,1152]{1,0:T(8,128)S(1)} %shard_map.65.lead, bf16[640,384]{1,0:T(8,128)(2,1)S(1)} %bitcast.31, f32[384]{0:T(512)S(1)} %copy-done.5), custom_call_target="tpu_custom_call" | custom-call | flops 2548039680 | bytes 8000000 | tf_op jit(solution)/shard_map/pallas_call | solution.py:293
  73.0 5.5 %collective-permute-start.16 = (bf16[12,2592]{1,0:T(8,128)(2,1)S(1)}, bf16[12,2592]{1,0:T(8,128)(2,1)S(1)}, u32[]{:S(2)}, u32[]{:S(2)}) collective-permute-start(bf16[12,2592]{1,0:T(8,128)(2,1)S(1)} %slice.122), channel_id=1, source_target_pairs={{0,64},{4,68},{8,72},{12,76},{16,80},{20,84},{24,88},{28,92},{32,9... | collective-permute-start | bytes 186632 | tf_op jit(solution)/shard_map/ppermute | solution.py:375
  78.5 4.6 %collective-permute-done.16 = bf16[12,2592]{1,0:T(8,128)(2,1)S(1)} collective-permute-done((bf16[12,2592]{1,0:T(8,128)(2,1)S(1)}, bf16[12,2592]{1,0:T(8,128)(2,1)S(1)}, u32[]{:S(2)}, u32[]{:S(2)}) %collective-permute-start.16) | collective-permute-done | bytes 62240 | tf_op jit(solution)/shard_map/ppermute | solution.py:375
  83.3 5.0 %collective-permute-done.17 = bf16[6,2592]{1,0:T(8,128)(2,1)S(1)} collective-permute-done((bf16[6,2592]{1,0:T(8,128)(2,1)S(1)}, bf16[6,2592]{1,0:T(8,128)(2,1)S(1)}, u32[]{:S(2)}, u32[]{:S(2)}) %collective-permute-start.17) | collective-permute-done | bytes 31136 | tf_op jit(solution)/shard_map/ppermute | solution.py:375
  (55 shorter events, 7.7 us)
Async XLA Ops:
  0.6 34.2 %copy-start.1 = (bf16[2,2,160,384]{3,2,1,0:T(8,128)(2,1)S(1)}, bf16[2,2,160,384]{3,2,1,0:T(8,128)(2,1)}, u32[]{:S(2)}) copy-start(bf16[2,2,160,384]{3,2,1,0:T(8,128)(2,1)} %own) | copy-start | bytes 1474564
  0.6 1.1 %copy-start.2 = (bf16[2,2,160,384]{3,2,1,0:T(8,128)(2,1)S(1)}, bf16[2,2,160,384]{3,2,1,0:T(8,128)(2,1)}, u32[]{:S(2)}) copy-start(bf16[2,2,160,384]{3,2,1,0:T(8,128)(2,1)} %param.4) | copy-start | bytes 1474564
  3.2 5.9 %collective-permute-start = (bf16[160,384]{1,0:T(8,128)(2,1)S(1)}, bf16[160,384]{1,0:T(8,128)(2,1)S(1)}, u32[]{:S(2)}, u32[]{:S(2)}) collective-permute-start(bf16[160,384]{1,0:T(8,128)(2,1)S(1)} %get-tuple-element.34), channel_id=1, source_target_pairs={{0,1},{1,2},{2,3},{3,0},{4,5},{5,6},{6,7},{7,4},{8,9},{9,10},{10,1... | collective-permute-start | bytes 368648 | tf_op jit(solution)/shard_map/ppermute | solution.py:335
  5.4 8.0 %collective-permute-start.1 = (bf16[160,384]{1,0:T(8,128)(2,1)S(1)}, bf16[160,384]{1,0:T(8,128)(2,1)S(1)}, u32[]{:S(2)}, u32[]{:S(2)}) collective-permute-start(bf16[160,384]{1,0:T(8,128)(2,1)S(1)} %get-tuple-element.35), channel_id=1, source_target_pairs={{0,2},{1,3},{2,0},{3,1},{4,6},{5,7},{6,4},{7,5},{8,10},{9,11},{10,... | collective-permute-start | bytes 368648 | tf_op jit(solution)/shard_map/ppermute | solution.py:335
  8.0 5.4 %collective-permute-start.2 = (bf16[160,384]{1,0:T(8,128)(2,1)S(1)}, bf16[160,384]{1,0:T(8,128)(2,1)S(1)}, u32[]{:S(2)}, u32[]{:S(2)}) collective-permute-start(bf16[160,384]{1,0:T(8,128)(2,1)S(1)} %get-tuple-element.36), channel_id=1, source_target_pairs={{0,3},{1,0},{2,1},{3,2},{4,7},{5,4},{6,5},{7,6},{8,11},{9,8},{10,9... | collective-permute-start | bytes 368648 | tf_op jit(solution)/shard_map/ppermute | solution.py:335
  13.4 12.3 %collective-permute-start.4 = (bf16[2,2,160,384]{3,2,1,0:T(8,128)(2,1)}, bf16[2,2,160,384]{3,2,1,0:T(8,128)(2,1)S(1)}, u32[]{:S(2)}, u32[]{:S(2)}) collective-permute-start(bf16[2,2,160,384]{3,2,1,0:T(8,128)(2,1)} %own), channel_id=1, source_target_pairs={{0,1},{1,2},{2,3},{3,0},{4,5},{5,6},{6,7},{7,4},{8,9},{9,10},{10,1... | collective-permute-start | bytes 1474568 | tf_op jit(solution)/shard_map/ppermute | solution.py:338
  13.4 12.5 %collective-permute-start.3 = (bf16[2,2,160,384]{3,2,1,0:T(8,128)(2,1)}, bf16[2,2,160,384]{3,2,1,0:T(8,128)(2,1)S(1)}, u32[]{:S(2)}, u32[]{:S(2)}) collective-permute-start(bf16[2,2,160,384]{3,2,1,0:T(8,128)(2,1)} %own), channel_id=1, source_target_pairs={{0,3},{1,0},{2,1},{3,2},{4,7},{5,4},{6,5},{7,6},{8,11},{9,8},{10,9... | collective-permute-start | bytes 1474568 | tf_op jit(solution)/shard_map/ppermute | solution.py:337
  17.5 11.4 %collective-permute-start.7 = (bf16[4,160,384]{2,1,0:T(8,128)(2,1)S(1)}, bf16[4,160,384]{2,1,0:T(8,128)(2,1)S(1)}, u32[]{:S(2)}, u32[]{:S(2)}) collective-permute-start(bf16[4,160,384]{2,1,0:T(8,128)(2,1)S(1)} %get-tuple-element.42), channel_id=1, source_target_pairs={{0,4},{4,8},{8,12},{12,16},{16,20},{20,24},{24,28},{28,32},{32,36}... | collective-permute-start | bytes 1474568 | tf_op jit(solution)/shard_map/ppermute | solution.py:340
  22.6 10.4 %collective-permute-start.8 = (bf16[4,160,384]{2,1,0:T(8,128)(2,1)S(1)}, bf16[4,160,384]{2,1,0:T(8,128)(2,1)S(1)}, u32[]{:S(2)}, u32[]{:S(2)}) collective-permute-start(bf16[4,160,384]{2,1,0:T(8,128)(2,1)S(1)} %get-tuple-element.43), channel_id=1, source_target_pairs={{4,0},{8,4},{12,8},{16,12},{20,16},{24,20},{28,24},{32,28},{36,32}... | collective-permute-start | bytes 1474568 | tf_op jit(solution)/shard_map/ppermute | solution.py:341
  25.8 9.1 %collective-permute-start.5 = (bf16[2,160,384]{2,1,0:T(8,128)(2,1)S(1)}, bf16[2,160,384]{2,1,0:T(8,128)(2,1)S(1)}, u32[]{:S(2)}, u32[]{:S(2)}) collective-permute-start(bf16[2,160,384]{2,1,0:T(8,128)(2,1)S(1)} %slice_bitcast_fusion.3), channel_id=1, source_target_pairs={{0,1},{1,2},{2,3},{3,0},{4,5},{5,6},{6,7},{7,4},{8,9},{9,10},{10,1... | collective-permute-start | bytes 737288 | tf_op jit(solution)/shard_map/ppermute | solution.py:344
  25.9 8.9 %collective-permute-start.6 = (bf16[2,160,384]{2,1,0:T(8,128)(2,1)S(1)}, bf16[2,160,384]{2,1,0:T(8,128)(2,1)S(1)}, u32[]{:S(2)}, u32[]{:S(2)}) collective-permute-start(bf16[2,160,384]{2,1,0:T(8,128)(2,1)S(1)} %slice_bitcast_fusion.2), channel_id=1, source_target_pairs={{0,3},{1,0},{2,1},{3,2},{4,7},{5,4},{6,5},{7,6},{8,11},{9,8},{10,9... | collective-permute-start | bytes 737288 | tf_op jit(solution)/shard_map/ppermute | solution.py:345
  34.9 21.1 %slice-start = ((s8[7962624]{0:T(1024)(128)(4,1)}), s8[4194304]{0:T(1024)(128)(4,1)S(1)}, s32[]{:S(2)}) async-start(s8[7962624]{0:T(1024)(128)(4,1)} %bitcast.22), calls=%async_computation | async-start | bytes 8388608
  39.9 16.0 %slice-start.1 = ((s8[7962624]{0:T(1024)(128)(4,1)}), s8[3768320]{0:T(1024)(128)(4,1)S(1)}, s32[]{:S(2)}) async-start(s8[7962624]{0:T(1024)(128)(4,1)} %bitcast.22), calls=%async_computation.1 | async-start | bytes 7536640
  40.0 6.5 %collective-permute-start.10 = (f32[96,2592]{1,0:T(8,128)S(1)}, f32[96,2592]{1,0:T(8,128)S(1)}, u32[]{:S(2)}, u32[]{:S(2)}) collective-permute-start(f32[96,2592]{1,0:T(8,128)S(1)} %get-tuple-element.49), channel_id=1, source_target_pairs={{0,4},{4,0},{8,12},{12,8},{16,20},{20,16},{24,28},{28,24},{32,36},... | collective-permute-start | bytes 2985992 | tf_op jit(solution)/shard_map/ppermute | solution.py:351
  46.2 2.7 %collective-permute-start.9 = (f32[96,2592]{1,0:T(8,128)S(1)}, f32[96,2592]{1,0:T(8,128)S(1)}, u32[]{:S(2)}, u32[]{:S(2)}) collective-permute-start(f32[96,2592]{1,0:T(8,128)S(1)} %get-tuple-element.47), channel_id=1, source_target_pairs={{0,4},{4,0},{8,12},{12,8},{16,20},{20,16},{24,28},{28,24},{32,36},... | collective-permute-start | bytes 2985992 | tf_op jit(solution)/shard_map/ppermute | solution.py:354
  49.0 15.0 %collective-permute-start.13 = (bf16[48,2592]{1,0:T(8,128)(2,1)S(1)}, bf16[48,2592]{1,0:T(8,128)(2,1)S(1)}, u32[]{:S(2)}, u32[]{:S(2)}) collective-permute-start(bf16[48,2592]{1,0:T(8,128)(2,1)S(1)} %fusion), channel_id=1, source_target_pairs={{0,24},{4,28},{8,0},{12,4},{16,8},{20,12},{24,16},{28,20},{32,56},... | collective-permute-start | bytes 746504 | tf_op jit(solution)/shard_map/ppermute | solution.py:361
  52.8 11.3 %collective-permute-start.11 = (bf16[48,2592]{1,0:T(8,128)(2,1)S(1)}, bf16[48,2592]{1,0:T(8,128)(2,1)S(1)}, u32[]{:S(2)}, u32[]{:S(2)}) collective-permute-start(bf16[48,2592]{1,0:T(8,128)(2,1)S(1)} %get-tuple-element.53), channel_id=1, source_target_pairs={{0,16},{4,20},{8,24},{12,28},{16,0},{20,4},{24,8},{28,12},{32,48},... | collective-permute-start | bytes 746504 | tf_op jit(solution)/shard_map/ppermute | solution.py:359
  52.8 14.6 %collective-permute-start.12 = (bf16[48,2592]{1,0:T(8,128)(2,1)S(1)}, bf16[48,2592]{1,0:T(8,128)(2,1)S(1)}, u32[]{:S(2)}, u32[]{:S(2)}) collective-permute-start(bf16[48,2592]{1,0:T(8,128)(2,1)S(1)} %get-tuple-element.54), channel_id=1, source_target_pairs={{0,8},{4,12},{8,16},{12,20},{16,24},{20,28},{24,0},{28,4},{32,40},... | collective-permute-start | bytes 746504 | tf_op jit(solution)/shard_map/ppermute | solution.py:359
  53.7 15.6 %collective-permute-start.14 = (bf16[2,2,160,384]{3,2,1,0:T(8,128)(2,1)S(1)}, bf16[2,2,160,384]{3,2,1,0:T(8,128)(2,1)S(1)}, u32[]{:S(2)}, u32[]{:S(2)}) collective-permute-start(bf16[2,2,160,384]{3,2,1,0:T(8,128)(2,1)S(1)} %pad_maximum_fusion.edges), channel_id=1, source_target_pairs={{0,3},{1,0},{2,1},{3,2},{4,7},{5,4},{6,5},{7,6},{8,11},{9,8},{10,9... | collective-permute-start | bytes 1474568 | tf_op jit(solution)/shard_map/ppermute | solution.py:362
  59.9 9.3 %copy-start.3 = (bf16[2,2,160,384]{3,2,1,0:T(8,128)(2,1)S(1)}, bf16[2,2,160,384]{3,2,1,0:T(8,128)(2,1)}, u32[]{:S(2)}) copy-start(bf16[2,2,160,384]{3,2,1,0:T(8,128)(2,1)} %param.4) | copy-start | bytes 1474564
  60.0 9.3 %copy-start.5 = (f32[384]{0:T(512)S(1)}, f32[384]{0:T(512)}, u32[]{:S(2)}) copy-start(f32[384]{0:T(512)} %gamma_ref.3) | copy-start | bytes 4612
  67.5 5.4 %collective-permute-start.15 = (bf16[24,2592]{1,0:T(8,128)(2,1)S(1)}, bf16[24,2592]{1,0:T(8,128)(2,1)S(1)}, u32[]{:S(2)}, u32[]{:S(2)}) collective-permute-start(bf16[24,2592]{1,0:T(8,128)(2,1)S(1)} %slice.121), channel_id=1, source_target_pairs={{0,32},{4,36},{8,40},{12,44},{16,48},{20,52},{24,56},{28,60},{32,0... | collective-permute-start | bytes 373256 | tf_op jit(solution)/shard_map/ppermute | solution.py:375
  73.0 10.1 %collective-permute-start.16 = (bf16[12,2592]{1,0:T(8,128)(2,1)S(1)}, bf16[12,2592]{1,0:T(8,128)(2,1)S(1)}, u32[]{:S(2)}, u32[]{:S(2)}) collective-permute-start(bf16[12,2592]{1,0:T(8,128)(2,1)S(1)} %slice.122), channel_id=1, source_target_pairs={{0,64},{4,68},{8,72},{12,76},{16,80},{20,84},{24,88},{28,92},{32,9... | collective-permute-start | bytes 186632 | tf_op jit(solution)/shard_map/ppermute | solution.py:375
  83.2 5.1 %collective-permute-start.17 = (bf16[6,2592]{1,0:T(8,128)(2,1)S(1)}, bf16[6,2592]{1,0:T(8,128)(2,1)S(1)}, u32[]{:S(2)}, u32[]{:S(2)}) collective-permute-start(bf16[6,2592]{1,0:T(8,128)(2,1)S(1)} %slice.123), channel_id=1, source_target_pairs={{0,192},{4,196},{8,200},{12,204},{16,208},{20,212},{24,216},{28,22... | collective-permute-start | bytes 93320 | tf_op jit(solution)/shard_map/ppermute | solution.py:375
  (2 other events, 1.7 us)
